TPU v7x, 32 devices: a whole 2x2x4 slice. The times are simulated.
32 devices in a mesh: row: 8 (over y, x, core), col: 4 (over z).
Axes of the slice: x: 2, y: 2, z: 4, core: 2. Of those that a mesh axis runs over, the one named last changes fastest.
Arguments:
- cotangent: bfloat16 [2, 256, 8192], P(None, 'row', 'col')
- hidden: bfloat16 [2, 256, 26624], P(None, 'col', 'row')
- context: bfloat16 [2, 256, 8192], P(None, 'col', 'row')
- down_weight: bfloat16 [26624, 8192], P('row', 'col'), may hold values from -0.0390625 to 0.0390625
- heads_weight: bfloat16 [8192, 8192], P('row', 'col'), may hold values from -0.0625 to 0.0625
- spans: int32 [2, 2], replicated, may hold values from 0 to 256, as said below
Outputs:
- down_grad: float32 [26624, 8192], P('row', 'col')
- heads_grad: float32 [8192, 8192], P('row', 'col')
- hidden_grad: bfloat16 [2, 256, 26624], P(None, 'col', 'row')
- context_grad: bfloat16 [2, 256, 8192], P(None, 'col', 'row')
Inputs may be any that keep to these rules, and one draw needn't show every extreme that they name: spans[b, 0] is below 64 and spans[b, 1] is 128 or more; some example starts at 0 and some example ends at 256.
All inputs are finite; a program needn't handle non-finite values.
Results may differ from a plain program's by a relative error of at most 0.001.
Values may be sent and summed in bfloat16 or wider, within the bound.
No kernel may reach another device: no remote copies, remote signals or barrier semaphores. Data moves between devices by JAX's collectives and lax.ppermute only.
A program may use at most 256 MiB of HBM per device.

v0:
```python
import math

import jax
import jax.numpy as jnp
from jax import lax
from jax.sharding import PartitionSpec as P

DW = 8192
FF_W = 26624
EXAMPLE_COUNT = 2
HD = 8192


GAMMA = 0.01


def mask_rows(cotangent, spans):
    row_count = cotangent.shape[1]
    position = lax.axis_index("row") * row_count + jnp.arange(row_count, dtype=jnp.int32)
    keep_mask = (position[None, :] >= spans[:, 0:1]) & (position[None, :] < spans[:, 1:2])
    return cotangent * keep_mask[:, :, None].astype(cotangent.dtype)


def weight_terms(feature_values, cotangent_matrix_rows):
    return jnp.einsum(
        "igm,iga->ima", feature_values, cotangent_matrix_rows, preferred_element_type=jnp.float32
    )


def input_terms(cotangent_matrix_rows, down_weight, heads_weight):
    hidden_term = jnp.einsum(
        "bsd,fd->bsf", cotangent_matrix_rows, down_weight, preferred_element_type=jnp.float32
    )
    context_term = jnp.einsum(
        "bsd,hd->bsh", cotangent_matrix_rows, heads_weight, preferred_element_type=jnp.float32
    )
    return (hidden_term, context_term)


def clip_scales(down_weight_blocks, heads_blocks):
    partial_sq = jnp.sum(down_weight_blocks * down_weight_blocks, axis=(1, 2)) + jnp.sum(
        heads_blocks * heads_blocks, axis=(1, 2)
    )
    sq_norm = lax.psum(partial_sq, ("row", "col"))
    return 1.0 / (jnp.sqrt(sq_norm) + GAMMA)


def scatter_inputs(hidden_term, context_term):
    hidden_sum, context_sum = (
        lax.psum_scatter(hidden_term, "col", scatter_dimension=1, tiled=True),
        lax.psum_scatter(context_term, "col", scatter_dimension=1, tiled=True),
    )
    return (hidden_sum.astype(jnp.bfloat16), context_sum.astype(jnp.bfloat16))


def body(cotangent, hidden, context, down_weight, heads_weight, spans):
    masked_values = mask_rows(cotangent, spans)
    gathered = lax.all_gather(masked_values, "row", axis=1, tiled=True)
    hidden_all = lax.all_gather(hidden, "col", axis=1, tiled=True)
    context_all = lax.all_gather(context, "col", axis=1, tiled=True)
    hidden_all, context_all = (hidden_all, context_all)
    hidden_term, context_term = input_terms(gathered, down_weight, heads_weight)
    down_weight_blocks = weight_terms(hidden_all, gathered)
    heads_blocks = weight_terms(context_all, gathered)
    clip_factor = clip_scales(down_weight_blocks, heads_blocks)
    hidden_grad, context_grad = scatter_inputs(hidden_term, context_term)
    down_grad = jnp.sum(clip_factor[:, None, None] * down_weight_blocks, axis=0) * (
        math.sqrt(FF_W * DW) / EXAMPLE_COUNT
    )
    heads_grad = jnp.sum(clip_factor[:, None, None] * heads_blocks, axis=0) * (
        math.sqrt(HD * DW) / EXAMPLE_COUNT
    )
    return (down_grad, heads_grad, hidden_grad, context_grad)


def solution(mesh):
    in_specs = (
        P(None, "row", "col"),
        P(None, "col", "row"),
        P(None, "col", "row"),
        P("row", "col"),
        P("row", "col"),
        P(),
    )
    out_specs = (P("row", "col"), P("row", "col"), P(None, "col", "row"), P(None, "col", "row"))
    return jax.shard_map(body, mesh=mesh, in_specs=in_specs, out_specs=out_specs, check_vma=False)
```

profile of v0, /device:TPU:0, one launch (start us, length us, event | category | flops | bytes accessed | tf_op | source)
XLA Modules:
  0.0 316.2 jit_solution(1467861645478655241)
XLA Ops:
  7.2 0.0 all-gather.4.cloned.1.call-start
  7.2 1.0 slice_reduce_fusion.1
  8.2 0.1 and_convert_fusion
  8.3 1.8 broadcast_multiply_fusion
  10.0 0.0 all-gather.4.cloned.1.call-update
  10.0 0.0 all-gather.8.cloned.1.call-start
  10.1 0.7 all-gather.8.cloned.1.call-update
  10.8 0.0 all-gather.6.cloned.1.call-start
  10.8 0.7 all-gather.6.cloned.1.call-update
  11.5 0.0 reduce-scatter.5.cloned.1.call-start
  11.6 29.5 %all-gather.4.cloned.1.call-done = bf16[2,256,2048]{2,1,0:T(8,128)(2,1)} async-done(((bf16[2,32,2048]{2,1,0:T(8,128)(2,1)}), bf16[2,256,2048]{2,1,0:T(8,128)(2,1)}) %all-gather.4.cloned.1.call-update) | async-done | bytes 2097168 | tf_op jit(solution)/shard_map/all_gather | solution.py:58
  41.1 0.0 copy-start
  41.1 6.6 %fusion.2 = f32[2,256,1024]{2,1,0:T(8,128)} fusion(bf16[2,256,2048]{2,1,0:T(8,128)(2,1)} %all-gather.4.cloned.1.call-done, bf16[1024,2048]{1,0:T(8,128)(2,1)} %param.10), kind=kOutput, calls=%fused_computation.8 | convolution fusion | flops 2147483648 | bytes 8388608 | tf_op jit(solution)/shard_map/bsd,hd->bsh/dot_general | solution.py:34
  47.8 0.0 reduce-scatter.5.cloned.1.call-update
  47.8 0.2 reduce-scatter.3.cloned.1.call-start
  48.0 0.0 copy-done
  48.0 12.8 %fusion = f32[2,256,3328]{2,1,0:T(8,128)} fusion(bf16[2,256,2048]{2,1,0:T(8,128)(2,1)S(1)} %copy-done, bf16[3328,2048]{1,0:T(8,128)(2,1)} %param.9), kind=kOutput, calls=%fused_computation.5 | convolution fusion | flops 6979321856 | bytes 22544384 | tf_op jit(solution)/shard_map/bsd,fd->bsf/dot_general | solution.py:31
  60.9 0.0 reduce-scatter.3.cloned.1.call-update
  60.9 9.7 %all-gather.8.cloned.1.call-done = bf16[2,256,1024]{2,1,0:T(8,128)(2,1)} async-done(((bf16[2,64,1024]{2,1,0:T(8,128)(2,1)}), bf16[2,256,1024]{2,1,0:T(8,128)(2,1)}) %all-gather.8.cloned.1.call-update) | async-done | bytes 1048592 | tf_op jit(solution)/shard_map/all_gather | solution.py:60
  70.6 9.8 %multiply_reduce_fusion.3 = (f32[2]{0:T(128)S(1)}, f32[2,2048,1024]{2,1,0:T(8,128)}) fusion(bf16[2,256,2048]{2,1,0:T(8,128)(2,1)S(1)} %copy-done, bf16[2,256,1024]{2,1,0:T(8,128)(2,1)} %all-gather.8.cloned.1.call-done), kind=kOutput, calls=%fused_computation.4 | convolution fusion | flops 2155872256 | bytes 19922952 | tf_op jit(solution)/shard_map/igm,iga->ima/dot_general | solution.py:25
  80.5 59.1 %all-gather.6.cloned.1.call-done = bf16[2,256,3328]{2,1,0:T(8,128)(2,1)} async-done(((bf16[2,64,3328]{2,1,0:T(8,128)(2,1)}), bf16[2,256,3328]{2,1,0:T(8,128)(2,1)}) %all-gather.6.cloned.1.call-update) | async-done | bytes 3407888 | tf_op jit(solution)/shard_map/all_gather | solution.py:59
  139.5 24.9 %multiply_reduce_fusion.1 = (f32[2]{0:T(128)S(1)}, f32[2,2048,3328]{2,1,0:T(8,128)}) fusion(bf16[2,256,2048]{2,1,0:T(8,128)(2,1)S(1)} %copy-done, bf16[2,256,3328]{2,1,0:T(8,128)(2,1)} %all-gather.6.cloned.1.call-done), kind=kOutput, calls=%fused_computation.1 | convolution fusion | flops 7006584832 | bytes 60030984 | tf_op jit(solution)/shard_map/igm,iga->ima/dot_general | solution.py:25
  164.4 39.5 %psum.7 = f32[2]{0:T(128)S(1)} all-reduce(f32[2]{0:T(128)S(1)} %add.24), channel_id=1, replica_groups=mesh['row'=8,'col'=4] {'row','col'}, use_global_device_ids=true, to_apply=%region_2.0 | all-reduce | flops 2 | bytes 16 | tf_op jit(solution)/shard_map/psum | solution.py:44
  203.9 8.4 %multiply_reduce_fusion.2 = f32[2048,1024]{1,0:T(8,128)S(1)} fusion(f32[2,2048,1024]{2,1,0:T(8,128)} %get-tuple-element.13, f32[2]{0:T(128)S(1)} %add_divide_fusion), kind=kLoop, calls=%fused_computation.3 | loop fusion | flops 6291456 | bytes 25165832 | tf_op jit(solution)/shard_map/reduce_sum | solution.py:70
  212.3 4.4 %multiply_bitcast_fusion.1 = f32[1024,2048]{0,1:T(8,128)} fusion(f32[2048,1024]{1,0:T(8,128)S(1)} %multiply_reduce_fusion.2), kind=kLoop, calls=%fused_computation.7 | loop fusion | flops 2097152 | bytes 16777216 | tf_op jit(solution)/shard_map/mul | solution.py:70
  216.7 9.2 %copy.11 = f32[1024,2048]{1,0:T(8,128)} copy(f32[1024,2048]{0,1:T(8,128)} %multiply_bitcast_fusion.1) | data formatting | bytes 16777216
  225.8 31.8 %multiply_reduce_fusion = f32[2048,3328]{1,0:T(8,128)} fusion(f32[2,2048,3328]{2,1,0:T(8,128)} %get-tuple-element.11, f32[2]{0:T(128)S(1)} %add_divide_fusion), kind=kLoop, calls=%fused_computation | loop fusion | flops 20447232 | bytes 81788936 | tf_op jit(solution)/shard_map/reduce_sum | solution.py:67
  257.7 20.3 %multiply_bitcast_fusion = f32[3328,2048]{0,1:T(8,128)} fusion(f32[2048,3328]{1,0:T(8,128)} %multiply_reduce_fusion), kind=kLoop, calls=%fused_computation.2 | loop fusion | flops 6815744 | bytes 54525952 | tf_op jit(solution)/shard_map/mul | solution.py:67
  278.0 27.4 %copy.10 = f32[3328,2048]{1,0:T(8,128)} copy(f32[3328,2048]{0,1:T(8,128)} %multiply_bitcast_fusion) | data formatting | bytes 54525952
  305.4 0.0 reduce-scatter.5.cloned.1.call-done
  305.4 1.8 convert_element_type.16
  307.2 0.0 reduce-scatter.3.cloned.1.call-done
  307.2 2.4 convert_element_type.15
  (3 shorter events, 0.0 us)
Async XLA Ops:
  7.2 33.9 %all-gather.4.cloned.1.call-start = ((), (), s32[]{:S(2)}) async-start(), calls=%async_computation.2 | async-start | bytes 2359296 | tf_op jit(solution)/shard_map/all_gather | solution.py:58
  10.0 60.6 %all-gather.8.cloned.1.call-start = ((), (), s32[]{:S(2)}) async-start(), calls=%async_computation.4 | async-start | bytes 1310720 | tf_op jit(solution)/shard_map/all_gather | solution.py:60
  10.8 128.7 %all-gather.6.cloned.1.call-start = ((), (), s32[]{:S(2)}) async-start(), calls=%async_computation.3 | async-start | bytes 4259840 | tf_op jit(solution)/shard_map/all_gather | solution.py:59
  11.5 293.9 %reduce-scatter.5.cloned.1.call-start = ((), (), s32[]{:S(2)}) async-start(), calls=%async_computation.6 | async-start | bytes 2621440 | tf_op jit(solution)/shard_map/reduce_scatter | solution.py:51
  41.1 6.9 %copy-start = (bf16[2,256,2048]{2,1,0:T(8,128)(2,1)S(1)}, bf16[2,256,2048]{2,1,0:T(8,128)(2,1)}, u32[]{:S(2)}) copy-start(bf16[2,256,2048]{2,1,0:T(8,128)(2,1)} %all-gather.4.cloned.1.call-done) | copy-start | bytes 6291460
  47.8 259.4 %reduce-scatter.3.cloned.1.call-start = ((), (), s32[]{:S(2)}) async-start(), calls=%async_computation.5 | async-start | bytes 8519680 | tf_op jit(solution)/shard_map/reduce_scatter | solution.py:50
Sparse Core Ops, SparseCore 0:
  10.5 30.5 all-gather.3
  42.7 27.9 all-gather.7
  72.2 67.2 all-gather.5
  141.7 42.6 reduce-scatter.4
  186.6 118.9 reduce-scatter.2
where the time goes:
time: 317 us; the launch traced here: 316 us
  waiting for transfers between devices  99.8 us (31%)
  other arithmetic  71 us (22%)
  matrix products  54.2 us (17%)
  blocking collectives  39.5 us (12%)
  local copies, waits for them, and re-layouts  37.5 us (12%)
  between operations  13.8 us (4%)
    all_gather x1, waiting for transfers between devices, body(): hidden_all = lax.all_gather(hidden, 'col', axis=1, tiled=True)  59.1 us
    psum x1, blocking collectives, clip_scales(): sq_norm = lax.psum(partial_sq, ('row', 'col'))  39.5 us
    unnamed x4, local copies, waits for them, and re-layouts  36.5 us
    dot_general x2, matrix products, weight_terms(): jnp.einsum('igm,iga->ima', feature_values, cotangent_matrix_rows, preferr...  34.7 us
    reduce_sum x1, other arithmetic, body(): jnp.sum(clip_factor[:, None, None] * down_weight_blocks, axis=0)  31.8 us
    all_gather x1, waiting for transfers between devices, body(): gathered = lax.all_gather(masked_values, 'row', axis=1, tiled=True)  29.5 us
    mul x1, other arithmetic, body(): jnp.sum(clip_factor[:, None, None] * down_weight_blocks, axis=0)  20.3 us
    dot_general x1, matrix products, input_terms(): jnp.einsum('bsd,fd->bsf', cotangent_matrix_rows, down_weight, preferred_e...  12.8 us
  transfers between devices with their start and end apart: 5, of which 3 were waited for; matrix products, arithmetic and copies ran while one was open for 50% of the time, Pallas kernels for 0%

commit v1 on v0

v1 whole, which is shorter than its diff:
```python
import functools
import math

import jax
import jax.numpy as jnp
from jax import lax
from jax.experimental import pallas as pl
from jax.experimental.pallas import tpu as pltpu
from jax.sharding import PartitionSpec as P

GAMMA = 0.01
VMEM = pltpu.VMEM
F32 = jnp.float32
BF16 = jnp.bfloat16
I16 = jnp.int16
LANES = 128
LIMIT = 48 * 1024 * 1024


def params(grid_dims):
    return pltpu.CompilerParams(
        dimension_semantics=("arbitrary",) * grid_dims, vmem_limit_bytes=LIMIT
    )


def cost(flops, bytes_accessed):
    return pl.CostEstimate(flops=int(flops), bytes_accessed=int(bytes_accessed), transcendentals=0)


def full(shape):
    return pl.BlockSpec(shape, lambda *_: (0,) * len(shape))


def encode_tile(value):
    largest = jnp.max(jnp.abs(value), axis=1, keepdims=True)
    exponent = jnp.ceil(jnp.log2(jnp.maximum(largest, 1e-37))) - 15.0
    exponent = jnp.clip(exponent, -125.0, 120.0)
    scaled = jnp.floor(value * jnp.exp2(-exponent) + 0.5)
    codes = jnp.clip(scaled, -32767.0, 32767.0).astype(jnp.int32).astype(I16)
    return codes, exponent.astype(jnp.int32)


def decode_tile(codes, exponents, index):
    scale = jnp.exp2(exponents[:, index : index + 1].astype(jnp.int32).astype(F32))
    return codes.astype(jnp.int32).astype(F32) * scale


def lane_put(held, index, column):
    lane = lax.broadcasted_iota(jnp.int32, held.shape, 1)
    return jnp.where(lane == index, column, held)


def arrange_kernel(row_count, col_count, spans, *refs):
    pieces, out = refs[:-1], refs[-1]
    r, c = lax.axis_index("row"), lax.axis_index("col")
    examples, held, _ = pieces[0].shape
    per_block = row_count // col_count
    for j, piece in enumerate(pieces):
        source = r ^ j
        block = source // per_block
        k = lax.rem(c - block + col_count, col_count)
        start = pl.multiple_of(lax.rem(source, per_block) * held, held)
        position = source * held + lax.broadcasted_iota(jnp.int32, (held, 1), 0)
        for b in range(examples):
            keep = (position >= spans[b, 0]) & (position < spans[b, 1])
            value = piece[b].astype(F32) * keep.astype(F32)
            out[k, b, pl.ds(start, held), :] = value.astype(BF16)


def arrange(pieces, spans, row_count, col_count):
    examples, held, width = pieces[0].shape
    local = held * row_count // col_count
    shape = (col_count, examples, local, width)
    return pl.pallas_call(
        functools.partial(arrange_kernel, row_count, col_count),
        out_shape=jax.ShapeDtypeStruct(shape, BF16),
        in_specs=[pl.BlockSpec(memory_space=pltpu.SMEM)]
        + [pl.BlockSpec(memory_space=VMEM)] * len(pieces),
        out_specs=pl.BlockSpec(memory_space=VMEM),
        compiler_params=pltpu.CompilerParams(vmem_limit_bytes=LIMIT),
        cost_estimate=cost(0, 4 * math.prod(shape)),
        name="arrange",
    )(spans, *pieces)


def gather_rows(x, row_count):
    near = [x]
    for j in range(2, row_count, 2):
        near.append(lax.ppermute(x, "row", [(i, i ^ j) for i in range(row_count)]))
    pieces = []
    for piece in near:
        pieces.append(piece)
        pieces.append(lax.ppermute(piece, "row", [(i, i ^ 1) for i in range(row_count)]))
    return pieces


def tile_of(*widths):
    return 256 if all(w % 256 == 0 for w in widths) else 128


def partial_kernel(first, last, tile, coded, m_ref, wa_ref, wb_ref, *outs):
    i = pl.program_id(0)
    sums = outs[0]
    ks, rows = sums.shape[0], sums.shape[1]
    masked = m_ref[...].reshape(ks * rows, m_ref.shape[-1])

    def work(w_ref):
        value = lax.dot_general(
            masked, w_ref[...], (((1,), (1,)), ((), ())), preferred_element_type=F32
        )
        for n in range(ks):
            part = value[n * rows : (n + 1) * rows]
            sums[n] = part
            if coded:
                message = outs[1 + n]
                codes, exponent = encode_tile(part)
                message[:, pl.ds(pl.multiple_of(i * tile, tile), tile)] = codes
                side = slice(last * tile, last * tile + LANES)
                held = message[:, side].astype(jnp.int32)
                message[:, side] = lane_put(held, i, exponent).astype(I16)

    @pl.when(i < first)
    def _():
        work(wa_ref)

    @pl.when(i >= first)
    def _():
        work(wb_ref)


def partials(masked, wa, wb, coded):
    ks, examples, local, width = masked.shape
    rows = examples * local
    tile = tile_of(wa.shape[0], wb.shape[0])
    first, last = wa.shape[0] // tile, (wa.shape[0] + wb.shape[0]) // tile
    features = last * tile
    out_shape = [jax.ShapeDtypeStruct((ks, rows, features), F32)]
    out_specs = [pl.BlockSpec((ks, rows, tile), lambda i: (0, 0, i))]
    if coded:
        out_shape += [jax.ShapeDtypeStruct((rows, features + LANES), I16)] * ks
        out_specs += [full((rows, features + LANES))] * ks
    return pl.pallas_call(
        functools.partial(partial_kernel, first, last, tile, coded),
        grid=(last,),
        out_shape=out_shape,
        in_specs=[
            full(masked.shape),
            pl.BlockSpec((tile, width), lambda i: (jnp.minimum(i, first - 1), 0)),
            pl.BlockSpec((tile, width), lambda i: (jnp.maximum(i - first, 0), 0)),
        ],
        out_specs=out_specs,
        compiler_params=params(1),
        cost_estimate=cost(
            2 * ks * rows * width * features, 2 * features * width + 4 * ks * rows * features
        ),
        name="partials",
    )(masked, wa, wb)


def add_kernel(tiles, tile, sums, message, out):
    side = slice(tiles * tile, tiles * tile + LANES)
    exponents = message[:, side]
    held = jnp.zeros(exponents.shape, jnp.int32)
    for n in range(tiles):
        cut = slice(n * tile, (n + 1) * tile)
        value = sums[0, :, cut] + decode_tile(message[:, cut], exponents, n)
        codes, exponent = encode_tile(value)
        out[:, cut] = codes
        held = lane_put(held, n, exponent)
    out[:, side] = held.astype(I16)


def add_message(sums, k, message, tile):
    rows, features = sums.shape[1:]
    step = rows // 4
    return pl.pallas_call(
        functools.partial(add_kernel, features // tile, tile),
        grid=(4,),
        out_shape=jax.ShapeDtypeStruct(message.shape, I16),
        in_specs=[
            pl.BlockSpec((1, step, features), lambda i: (k, i, 0)),
            pl.BlockSpec((step, features + LANES), lambda i: (i, 0)),
        ],
        out_specs=pl.BlockSpec((step, features + LANES), lambda i: (i, 0)),
        compiler_params=params(1),
        cost_estimate=cost(8 * rows * features, 8 * rows * features),
        name="add",
    )(sums, message)


def finish_kernel(tiles, first, tile, sums, right, left, a_ref, b_ref):
    side = slice(tiles * tile, tiles * tile + LANES)
    right_exponents, left_exponents = right[:, side], left[:, side]
    for n in range(tiles):
        cut = slice(n * tile, (n + 1) * tile)
        value = sums[0, :, cut]
        value += decode_tile(right[:, cut], right_exponents, n)
        value += decode_tile(left[:, cut], left_exponents, n)
        if n < first:
            a_ref[0, :, cut] = value.astype(BF16)
        else:
            b_ref[0, :, (n - first) * tile : (n - first + 1) * tile] = value.astype(BF16)


def finish(sums, k, right, left, examples, widths, tile):
    rows, features = sums.shape[1:]
    local = rows // examples
    half = local // 2
    message = pl.BlockSpec((half, features + LANES), lambda i: (i, 0))
    return pl.pallas_call(
        functools.partial(finish_kernel, features // tile, widths[0] // tile, tile),
        grid=(2 * examples,),
        out_shape=[jax.ShapeDtypeStruct((examples, local, w), BF16) for w in widths],
        in_specs=[pl.BlockSpec((1, half, features), lambda i: (k, i, 0)), message, message],
        out_specs=[pl.BlockSpec((1, half, w), lambda i: (i // 2, i % 2, 0)) for w in widths],
        compiler_params=params(1),
        cost_estimate=cost(8 * rows * features, 10 * rows * features),
        name="finish",
    )(sums, right, left)


def norm_kernel(col_count, *refs):
    m_ref, own = refs[0], refs[1]
    rights, lefts = refs[2 : 1 + col_count], refs[1 + col_count : 2 * col_count]
    out = refs[-1]
    nt = (((1,), (1,)), ((), ()))
    lane = lax.broadcasted_iota(jnp.int32, out.shape, 1)
    total = jnp.zeros(out.shape, F32)
    for b in range(own.shape[0]):
        parts = [own[b]]
        for k in range(1, col_count):
            parts.append(rights[k - 1][b] + lefts[col_count - k - 1][b])
        feature = jnp.concatenate(parts, axis=0)
        masked = m_ref[:, b].reshape(feature.shape[0], m_ref.shape[-1])
        left_gram = lax.dot_general(feature, feature, nt, preferred_element_type=F32)
        right_gram = lax.dot_general(masked, masked, nt, preferred_element_type=F32)
        total = jnp.where(lane == b, jnp.sum(left_gram * right_gram), total)
    out[...] = total


def local_norm(masked, own, rights, lefts):
    col_count = masked.shape[0]
    arrays = [masked, own, *rights, *lefts]
    return pl.pallas_call(
        functools.partial(norm_kernel, col_count),
        out_shape=jax.ShapeDtypeStruct((8, LANES), F32),
        in_specs=[pl.BlockSpec(memory_space=VMEM)] * len(arrays),
        out_specs=pl.BlockSpec(memory_space=VMEM),
        compiler_params=pltpu.CompilerParams(vmem_limit_bytes=LIMIT),
        cost_estimate=cost(2 * 10**9, 8 * 10**6),
        name="norm",
    )(*arrays)


def sum_over(x, axis, count):
    j = 1
    while j < count:
        x = x + lax.ppermute(x, axis, [(i, i ^ j) for i in range(count)])
        j *= 2
    return x


def weight_kernel(col_count, first, scales, factor, *refs):
    m_ref, own = refs[0], refs[1]
    rights, lefts = refs[2 : 1 + col_count], refs[1 + col_count : 2 * col_count]
    a_ref, b_ref = refs[-2:]
    i = pl.program_id(0)
    total = None
    for b in range(own.shape[0]):
        parts = [own[b]]
        for k in range(1, col_count):
            parts.append(rights[k - 1][b] + lefts[col_count - k - 1][b])
        feature = jnp.concatenate(parts, axis=0)
        masked = m_ref[:, b].reshape(feature.shape[0], m_ref.shape[-1])
        each = lax.dot_general(
            feature, masked, (((0,), (0,)), ((), ())), preferred_element_type=F32
        )
        each = factor[0, b] * each
        total = each if total is None else total + each

    @pl.when(i < first)
    def _():
        a_ref[...] = total * scales[0]

    @pl.when(i >= first)
    def _():
        b_ref[...] = total * scales[1]


def weight_grads(factor, masked, own, rights, lefts, widths, scales):
    col_count, examples, local, width = masked.shape
    tile = tile_of(*widths)
    first, last = widths[0] // tile, sum(widths) // tile
    block = pl.BlockSpec((examples, local, tile), lambda i: (0, 0, i))
    count = 2 * col_count - 1
    return pl.pallas_call(
        functools.partial(weight_kernel, col_count, first, scales),
        grid=(last,),
        out_shape=[jax.ShapeDtypeStruct((w, width), F32) for w in widths],
        in_specs=[pl.BlockSpec(memory_space=pltpu.SMEM), full(masked.shape)] + [block] * count,
        out_specs=[
            pl.BlockSpec((tile, width), lambda i: (jnp.minimum(i, first - 1), 0)),
            pl.BlockSpec((tile, width), lambda i: (jnp.maximum(i - first, 0), 0)),
        ],
        compiler_params=params(1),
        cost_estimate=cost(
            2 * examples * local * col_count * width * sum(widths), 4 * width * sum(widths)
        ),
        name="weights",
    )(factor, masked, own, *rights, *lefts)


def body(row_count, col_count, scales, cotangent, hidden, context, wa, wb, spans):
    n = col_count
    widths = (hidden.shape[2], context.shape[2])
    examples = hidden.shape[0]
    tile = tile_of(*widths)
    own = jnp.concatenate([hidden, context], axis=2)

    def send_right(x, low, high):
        return lax.ppermute(x, "col", [(i, i + 1) for i in range(low, high)])

    def send_left(x, low, high):
        return lax.ppermute(x, "col", [(i, i - 1) for i in range(low, high)])

    rights, lefts = [send_right(own, 0, n - 1)], [send_left(own, 1, n)]
    masked = arrange(gather_rows(cotangent, row_count), spans, row_count, n)

    outer = jnp.stack([masked[1], masked[n - 1]])
    outer_sums, right_message, left_message = partials(outer, wa, wb, True)
    inner = [k for k in range(n) if k not in (1, n - 1)]
    inner_sums = partials(jnp.stack([masked[k] for k in inner]), wa, wb, False)[0]

    def sums_of(k):
        if k in (1, n - 1):
            return outer_sums, (0 if k == 1 else 1)
        return inner_sums, inner.index(k)

    right_came = left_came = None
    for s in range(1, n):
        if s > 1:
            sums, at = sums_of(s)
            right_message = add_message(sums, at, right_came, tile)
            sums, at = sums_of(n - s)
            left_message = add_message(sums, at, left_came, tile)
        if s < n - 1:
            rights.append(send_right(rights[-1], s, n - 1))
            lefts.append(send_left(lefts[-1], 1, n - s))
        right_came = send_right(right_message, 0, s)
        left_came = send_left(left_message, n - s, n)

    sq_norm = local_norm(masked, own, rights, lefts)
    sq_norm = sum_over(sum_over(sq_norm, "row", row_count), "col", n)
    factor = 1.0 / (jnp.sqrt(sq_norm[:1, :examples]) + GAMMA)
    down_grad, heads_grad = weight_grads(factor, masked, own, rights, lefts, widths, scales)
    sums, at = sums_of(0)
    hidden_grad, context_grad = finish(sums, at, right_came, left_came, examples, widths, tile)
    return down_grad, heads_grad, hidden_grad, context_grad


def solution(mesh):
    row_count, col_count = mesh.shape["row"], mesh.shape["col"]

    def run(cotangent, hidden, context, down_weight, heads_weight, spans):
        examples = hidden.shape[0]
        scales = tuple(math.sqrt(w.shape[0] * w.shape[1]) / examples for w in (down_weight, heads_weight))
        in_specs = (
            P(None, "row", "col"),
            P(None, "col", "row"),
            P(None, "col", "row"),
            P("row", "col"),
            P("row", "col"),
            P(),
        )
        out_specs = (P("row", "col"), P("row", "col"), P(None, "col", "row"), P(None, "col", "row"))
        return jax.shard_map(
            functools.partial(body, row_count, col_count, scales),
            mesh=mesh,
            in_specs=in_specs,
            out_specs=out_specs,
            check_vma=False,
        )(cotangent, hidden, context, down_weight, heads_weight, spans)

    return run
```

time: 317 us -> 185 us (0.58)
  Pallas kernels: 0 us -> 92.6 us
  other arithmetic: 71 us -> 0.22 us
  matrix products: 54.2 us -> 0 us
  waiting for transfers between devices: 99.8 us -> 51.6 us
  blocking collectives: 39.5 us -> 0 us
  starting transfers between devices: 0.38 us -> 35.8 us
  local copies, waits for them, and re-layouts: 37.5 us -> 2.6 us
  between operations: 13.8 us -> 1.01 us
    all_gather x3 -> x0, waiting for transfers between devices: 98.3 us -> none  [the longest x1 59.1 us: body(): hidden_all = lax.all_gather(hidden, 'col', axis=1, tiled=True)]
    pallas_call x0 -> x10, Pallas kernels: none -> 92.6 us  [the longest x2 36.1 us: partials(): pl.pallas_call(functools.partial(partial_kernel, first, last, tile, coded...]
    dot_general x4 -> x0, matrix products: 54.2 us -> none  [the longest x2 34.7 us: weight_terms(): jnp.einsum('igm,iga->ima', feature_values, cotangent_matrix_rows, preferr...]
    ppermute x0 -> x24, waiting for transfers between devices: none -> 51.6 us  [the longest x5 19.9 us: sum_over(): x = x + lax.ppermute(x, axis, [(i, i ^ j) for i in range(count)])]
    reduce_sum x2 -> x0, other arithmetic: 40.2 us -> none  [the longest x1 31.8 us: body(): jnp.sum(clip_factor[:, None, None] * down_weight_blocks, axis=0)]
    psum x1 -> x0, blocking collectives: 39.5 us -> none  [clip_scales(): sq_norm = lax.psum(partial_sq, ('row', 'col'))]
    ppermute x0 -> x24, starting transfers between devices: none -> 35.8 us  [the longest x6 18.6 us: send_right(): return lax.ppermute(x, 'col', [(i, i + 1) for i in range(low, high)])]
    unnamed x4 -> x13, local copies, waits for them, and re-layouts: 36.5 us -> 2.34 us
  transfers between devices with their start and end apart: 5 -> 24, of which waited for: 3 -> 10; matrix products, arithmetic and copies ran while one was open for 50% -> 1% of each run, Pallas kernels for 0% -> 48%
where the time goes in v1:
time: 185 us; the launch traced here: 184 us
  Pallas kernels  92.6 us (50%)
  waiting for transfers between devices  51.6 us (28%)
  starting transfers between devices  35.8 us (19%)
  local copies, waits for them, and re-layouts  2.6 us (1%)
    pallas_call x2, Pallas kernels, partials(): pl.pallas_call(functools.partial(partial_kernel, first, last, tile, coded...  36.1 us
    pallas_call x4, Pallas kernels, add_message(): pl.pallas_call(functools.partial(add_kernel, features // tile, tile), gri...  24.5 us
    pallas_call x1, Pallas kernels, weight_grads(): pl.pallas_call(functools.partial(weight_kernel, col_count, first, scales)...  22.6 us
    ppermute x5, waiting for transfers between devices, sum_over(): x = x + lax.ppermute(x, axis, [(i, i ^ j) for i in range(count)])  19.9 us
    ppermute x6, waiting for transfers between devices, send_right(): return lax.ppermute(x, 'col', [(i, i + 1) for i in range(low, high)])  19.8 us
    ppermute x6, starting transfers between devices, send_right(): return lax.ppermute(x, 'col', [(i, i + 1) for i in range(low, high)])  18.6 us
    ppermute x3, waiting for transfers between devices, gather_rows(): near.append(lax.ppermute(x, 'row', [(i, i ^ j) for i in range(row_count)]))  11.8 us
    ppermute x6, starting transfers between devices, send_left(): return lax.ppermute(x, 'col', [(i, i - 1) for i in range(low, high)])  6.64 us
  transfers between devices with their start and end apart: 24, of which 10 were waited for; matrix products, arithmetic and copies ran while one was open for 1% of the time, Pallas kernels for 48%

profile of v1, /device:TPU:0, one launch (start us, length us, event | category | flops | bytes accessed | tf_op | source)
XLA Modules:
  0.0 183.9 jit_solution(4381735460864183231)
XLA Ops:
  0.7 3.0 %collective-permute-start.3 = (bf16[2,32,2048]{2,1,0:T(8,128)(2,1)}, bf16[2,32,2048]{2,1,0:T(8,128)(2,1)S(1)}, u32[]{:S(2)}, u32[]{:S(2)}) collective-permute-start(bf16[2,32,2048]{2,1,0:T(8,128)(2,1)} %refs_0_.1), channel_id=1, source_target_pairs={{0,16},{4,20},{8,24},{12,28},{16,0},{20,4},{24,8},{28,12},{1,17},{... | collective-permute-start | bytes 786440 | tf_op jit(solution)/shard_map/ppermute | solution.py:89
  3.7 1.5 collective-permute-start.1
  5.2 0.0 collective-permute-start.5
  5.2 5.0 %collective-permute-done.3.refs_4_ = bf16[2,32,2048]{2,1,0:T(8,128)(2,1)S(1)} collective-permute-done((bf16[2,32,2048]{2,1,0:T(8,128)(2,1)}, bf16[2,32,2048]{2,1,0:T(8,128)(2,1)S(1)}, u32[]{:S(2)}, u32[]{:S(2)}) %collective-permute-start.3) | collective-permute-done | bytes 262176 | tf_op jit(solution)/shard_map/ppermute | solution.py:89
  10.2 2.9 %collective-permute-done.1.refs_2_ = bf16[2,32,2048]{2,1,0:T(8,128)(2,1)S(1)} collective-permute-done((bf16[2,32,2048]{2,1,0:T(8,128)(2,1)}, bf16[2,32,2048]{2,1,0:T(8,128)(2,1)S(1)}, u32[]{:S(2)}, u32[]{:S(2)}) %collective-permute-start.1) | collective-permute-done | bytes 262176 | tf_op jit(solution)/shard_map/ppermute | solution.py:89
  13.1 0.0 collective-permute-start.2
  13.1 3.9 %collective-permute-done.5.refs_6_ = bf16[2,32,2048]{2,1,0:T(8,128)(2,1)S(1)} collective-permute-done((bf16[2,32,2048]{2,1,0:T(8,128)(2,1)}, bf16[2,32,2048]{2,1,0:T(8,128)(2,1)S(1)}, u32[]{:S(2)}, u32[]{:S(2)}) %collective-permute-start.5) | collective-permute-done | bytes 262176 | tf_op jit(solution)/shard_map/ppermute | solution.py:89
  17.1 0.0 collective-permute-start.6
  17.1 1.2 constant_dynamic-update-slice_fusion.1
  18.3 1.3 collective-permute-start.10
  19.6 4.6 %collective-permute-start.7 = (bf16[2,64,4352]{2,1,0:T(8,128)(2,1)S(1)}, bf16[2,64,4352]{2,1,0:T(8,128)(2,1)S(1)}, u32[]{:S(2)}, u32[]{:S(2)}) collective-permute-start(bf16[2,64,4352]{2,1,0:T(8,128)(2,1)S(1)} %constant_dynamic-update-slice_fusion.refs_1_), channel_id=1, source_target_pairs={{0,1},{1,2},{2,3},{4,5},{5,6},{6,7},{8,9},{9,10},{10,11},{12,13},{... | collective-permute-start | bytes 3342344 | tf_op jit(solution)/shard_map/ppermute | solution.py:321
  24.3 1.1 arrange.1.refs_0_
  25.4 0.2 fusion
  25.7 1.1 copy-done
  26.8 0.1 pad_maximum_fusion.1.m_ref
  26.9 0.0 copy-start.1
  26.9 19.6 %partials.3 = (f32[2,128,4352]{2,1,0:T(8,128)}, s16[128,4480]{1,0:T(8,128)(2,1)S(1)}, s16[128,4480]{1,0:T(8,128)(2,1)S(1)}) custom-call(bf16[2,2,64,2048]{3,2,1,0:T(8,128)(2,1)S(1)} %pad_maximum_fusion.1.m_ref, bf16[3328,2048]{1,0:T(8,128)(2,1)} %wa_ref.3, bf16[1024,2048]{1,0:T(8,128)(2,1)} %wb_ref.3), custom_call_target="tpu_custom_call" | custom-call | flops 4563402752 | bytes 22282240 | tf_op jit(solution)/shard_map/partials/pallas_call | solution.py:142
  46.4 3.6 %collective-permute-start.18 = (s16[128,4480]{1,0:T(8,128)(2,1)S(1)}, s16[128,4480]{1,0:T(8,128)(2,1)S(1)}, u32[]{:S(2)}, u32[]{:S(2)}) collective-permute-start(s16[128,4480]{1,0:T(8,128)(2,1)S(1)} %get-tuple-element.14), channel_id=1, source_target_pairs={{0,1},{4,5},{8,9},{12,13},{16,17},{20,21},{24,25},{28,29}} | collective-permute-start | bytes 3440648 | tf_op jit(solution)/shard_map/ppermute | solution.py:321
  50.1 0.7 collective-permute-start.21
  50.8 1.3 collective-permute-start.11
  52.1 0.7 collective-permute-start.8
  52.9 0.1 pad_maximum_fusion.m_ref
  53.0 16.6 %partials.2.sums = f32[2,128,4352]{2,1,0:T(8,128)} custom-call(bf16[2,2,64,2048]{3,2,1,0:T(8,128)(2,1)S(1)} %pad_maximum_fusion.m_ref, bf16[3328,2048]{1,0:T(8,128)(2,1)} %wa_ref.3, bf16[1024,2048]{1,0:T(8,128)(2,1)S(1)} %copy-done.1), custom_call_target="tpu_custom_call" | custom-call | flops 4563402752 | bytes 22282240 | tf_op jit(solution)/shard_map/partials/pallas_call | solution.py:142
  69.6 5.0 %collective-permute-done.18.message = s16[128,4480]{1,0:T(8,128)(2,1)S(1)} collective-permute-done((s16[128,4480]{1,0:T(8,128)(2,1)S(1)}, s16[128,4480]{1,0:T(8,128)(2,1)S(1)}, u32[]{:S(2)}, u32[]{:S(2)}) %collective-permute-start.18) | collective-permute-done | bytes 1146912 | tf_op jit(solution)/shard_map/ppermute | solution.py:321
  74.6 6.1 %add.29 = s16[128,4480]{1,0:T(8,128)(2,1)S(1)} custom-call(f32[2,128,4352]{2,1,0:T(8,128)} %partials.2.sums, s16[128,4480]{1,0:T(8,128)(2,1)S(1)} %collective-permute-done.18.message), custom_call_target="tpu_custom_call" | custom-call | flops 4456448 | bytes 4456448 | tf_op jit(solution)/shard_map/add/pallas_call | solution.py:176
  80.7 4.5 %collective-permute-start.19 = (s16[128,4480]{1,0:T(8,128)(2,1)S(1)}, s16[128,4480]{1,0:T(8,128)(2,1)S(1)}, u32[]{:S(2)}, u32[]{:S(2)}) collective-permute-start(s16[128,4480]{1,0:T(8,128)(2,1)S(1)} %add.29), channel_id=1, source_target_pairs={{0,1},{1,2},{4,5},{5,6},{8,9},{9,10},{12,13},{13,14},{16,17},{17,1... | collective-permute-start | bytes 3440648 | tf_op jit(solution)/shard_map/ppermute | solution.py:321
  85.2 6.1 %add.31 = s16[128,4480]{1,0:T(8,128)(2,1)S(1)} custom-call(f32[2,128,4352]{2,1,0:T(8,128)} %partials.2.sums, s16[128,4480]{1,0:T(8,128)(2,1)S(1)} %collective-permute-done.21.message), custom_call_target="tpu_custom_call" | custom-call | flops 4456448 | bytes 4456448 | tf_op jit(solution)/shard_map/add/pallas_call | solution.py:176
  91.4 0.7 collective-permute-start.22
  92.1 1.3 collective-permute-start.12
  93.4 0.7 collective-permute-start.9
  94.2 14.7 %collective-permute-done.19.message = s16[128,4480]{1,0:T(8,128)(2,1)S(1)} collective-permute-done((s16[128,4480]{1,0:T(8,128)(2,1)S(1)}, s16[128,4480]{1,0:T(8,128)(2,1)S(1)}, u32[]{:S(2)}, u32[]{:S(2)}) %collective-permute-start.19) | collective-permute-done | bytes 1146912 | tf_op jit(solution)/shard_map/ppermute | solution.py:321
  108.9 6.1 %add.30 = s16[128,4480]{1,0:T(8,128)(2,1)S(1)} custom-call(f32[2,128,4352]{2,1,0:T(8,128)} %get-tuple-element.13.sums, s16[128,4480]{1,0:T(8,128)(2,1)S(1)} %collective-permute-done.19.message), custom_call_target="tpu_custom_call" | custom-call | flops 4456448 | bytes 4456448 | tf_op jit(solution)/shard_map/add/pallas_call | solution.py:176
  115.0 4.5 %collective-permute-start.20 = (s16[128,4480]{1,0:T(8,128)(2,1)S(1)}, s16[128,4480]{1,0:T(8,128)(2,1)S(1)}, u32[]{:S(2)}, u32[]{:S(2)}) collective-permute-start(s16[128,4480]{1,0:T(8,128)(2,1)S(1)} %add.30), channel_id=1, source_target_pairs={{0,1},{1,2},{2,3},{4,5},{5,6},{6,7},{8,9},{9,10},{10,11},{12,13},{... | collective-permute-start | bytes 3440648 | tf_op jit(solution)/shard_map/ppermute | solution.py:321
  119.5 6.1 %add.32 = s16[128,4480]{1,0:T(8,128)(2,1)S(1)} custom-call(f32[2,128,4352]{2,1,0:T(8,128)} %get-tuple-element.13.sums, s16[128,4480]{1,0:T(8,128)(2,1)S(1)} %collective-permute-done.22.message), custom_call_target="tpu_custom_call" | custom-call | flops 4456448 | bytes 4456448 | tf_op jit(solution)/shard_map/add/pallas_call | solution.py:176
  125.6 1.3 collective-permute-start.23
  127.0 4.3 %norm.1 = f32[8,128]{1,0:T(8,128)S(1)} custom-call(bf16[4,2,64,2048]{3,2,1,0:T(8,128)(2,1)} %copy-done, bf16[2,64,4352]{2,1,0:T(8,128)(2,1)S(1)} %constant_dynamic-update-slice_fusion.refs_1_, bf16[2,64,4352]{2,1,0:T(8,128)(2,1)S(1)} %collective-permute-done.7.refs_2_, bf16[2,64,4352]{2,1,0:T(8,128)(2,1)S(1)} %collective-permute-done.8.refs_3_, ...), custom_call_target="tpu_custom_call" | custom-call | flops 2000000000 | bytes 8000000 | tf_op jit(solution)/shard_map/norm/pallas_call | solution.py:244
  131.2 0.1 collective-permute-start.13
  131.3 1.2 collective-permute-done.13
  132.5 1.5 collective-permute-start.14
  134.0 2.1 %collective-permute-done.14 = f32[8,128]{1,0:T(8,128)S(1)} collective-permute-done((f32[8,128]{1,0:T(8,128)S(1)}, f32[8,128]{1,0:T(8,128)S(1)}, u32[]{:S(2)}, u32[]{:S(2)}) %collective-permute-start.14) | collective-permute-done | bytes 4128 | tf_op jit(solution)/shard_map/ppermute | solution.py:258
  136.1 1.5 collective-permute-start.15
  137.6 2.1 %collective-permute-done.15 = f32[8,128]{1,0:T(8,128)S(1)} collective-permute-done((f32[8,128]{1,0:T(8,128)S(1)}, f32[8,128]{1,0:T(8,128)S(1)}, u32[]{:S(2)}, u32[]{:S(2)}) %collective-permute-start.15) | collective-permute-done | bytes 4128 | tf_op jit(solution)/shard_map/ppermute | solution.py:258
  139.7 2.6 %collective-permute-start.16 = (f32[8,128]{1,0:T(8,128)S(1)}, f32[8,128]{1,0:T(8,128)S(1)}, u32[]{:S(2)}, u32[]{:S(2)}) collective-permute-start(f32[8,128]{1,0:T(8,128)S(1)} %add.24), channel_id=1, source_target_pairs={{0,1},{1,0},{2,3},{3,2},{4,5},{5,4},{6,7},{7,6},{8,9},{9,8},{10,11... | collective-permute-start | bytes 12296 | tf_op jit(solution)/shard_map/ppermute | solution.py:258
  142.3 10.3 %collective-permute-done.16 = f32[8,128]{1,0:T(8,128)S(1)} collective-permute-done((f32[8,128]{1,0:T(8,128)S(1)}, f32[8,128]{1,0:T(8,128)S(1)}, u32[]{:S(2)}, u32[]{:S(2)}) %collective-permute-start.16) | collective-permute-done | bytes 4128 | tf_op jit(solution)/shard_map/ppermute | solution.py:258
  152.7 0.3 collective-permute-start.17
  153.0 4.2 %collective-permute-done.17 = f32[8,128]{1,0:T(8,128)S(1)} collective-permute-done((f32[8,128]{1,0:T(8,128)S(1)}, f32[8,128]{1,0:T(8,128)S(1)}, u32[]{:S(2)}, u32[]{:S(2)}) %collective-permute-start.17) | collective-permute-done | bytes 4128 | tf_op jit(solution)/shard_map/ppermute | solution.py:258
  157.2 22.6 %weights.1 = (f32[3328,2048]{1,0:T(8,128)}, f32[1024,2048]{1,0:T(8,128)}) custom-call(f32[1,2]{1,0:T(1,128)S(1)} %add_divide_fusion.factor, bf16[4,2,64,2048]{3,2,1,0:T(8,128)(2,1)} %copy-done, bf16[2,64,4352]{2,1,0:T(8,128)(2,1)S(1)} %constant_dynamic-update-slice_fusion.refs_1_, bf16[2,64,4352]{2,1,0:T(8,128)(2,1)S(1)} %collective-permute-done.7.refs_2_, ...), custom_call_target="tpu_custom_call" | custom-call | flops 9126805504 | bytes 35651584 | tf_op jit(solution)/shard_map/weights/pallas_call | solution.py:296
  179.9 4.0 %finish.1 = (bf16[2,64,3328]{2,1,0:T(8,128)(2,1)}, bf16[2,64,1024]{2,1,0:T(8,128)(2,1)}) custom-call(f32[2,128,4352]{2,1,0:T(8,128)} %partials.2.sums, s16[128,4480]{1,0:T(8,128)(2,1)S(1)} %collective-permute-done.20.right, s16[128,4480]{1,0:T(8,128)(2,1)S(1)} %collective-permute-done.23.left), custom_call_target="tpu_custom_call" | custom-call | flops 4456448 | bytes 5570560 | tf_op jit(solution)/shard_map/finish/pallas_call | solution.py:210
  (33 shorter events, 0.1 us)
Async XLA Ops:
  0.6 23.7 %copy-start.2 = (bf16[2,32,2048]{2,1,0:T(8,128)(2,1)S(1)}, bf16[2,32,2048]{2,1,0:T(8,128)(2,1)}, u32[]{:S(2)}) copy-start(bf16[2,32,2048]{2,1,0:T(8,128)(2,1)} %refs_0_.1) | copy-start | bytes 786436
  0.6 17.7 %copy-start.5 = (bf16[2,64,1024]{2,1,0:T(8,128)(2,1)S(1)}, bf16[2,64,1024]{2,1,0:T(8,128)(2,1)}, u32[]{:S(2)}) copy-start(bf16[2,64,1024]{2,1,0:T(8,128)(2,1)} %param.8) | copy-start | bytes 786436
  0.7 23.7 %copy-start.3 = (s32[2,2]{1,0:T(2,128)S(1)}, s32[2,2]{1,0:T(2,128)}, u32[]{:S(2)}) copy-start(s32[2,2]{1,0:T(2,128)} %spans.1) | copy-start | bytes 52
  0.7 9.5 %collective-permute-start.3 = (bf16[2,32,2048]{2,1,0:T(8,128)(2,1)}, bf16[2,32,2048]{2,1,0:T(8,128)(2,1)S(1)}, u32[]{:S(2)}, u32[]{:S(2)}) collective-permute-start(bf16[2,32,2048]{2,1,0:T(8,128)(2,1)} %refs_0_.1), channel_id=1, source_target_pairs={{0,16},{4,20},{8,24},{12,28},{16,0},{20,4},{24,8},{28,12},{1,17},{... | collective-permute-start | bytes 786440 | tf_op jit(solution)/shard_map/ppermute | solution.py:89
  3.7 9.4 %collective-permute-start.1 = (bf16[2,32,2048]{2,1,0:T(8,128)(2,1)}, bf16[2,32,2048]{2,1,0:T(8,128)(2,1)S(1)}, u32[]{:S(2)}, u32[]{:S(2)}) collective-permute-start(bf16[2,32,2048]{2,1,0:T(8,128)(2,1)} %refs_0_.1), channel_id=1, source_target_pairs={{0,8},{4,12},{8,0},{12,4},{16,24},{20,28},{24,16},{28,20},{1,9},{5... | collective-permute-start | bytes 786440 | tf_op jit(solution)/shard_map/ppermute | solution.py:89
  5.2 11.9 %collective-permute-start.5 = (bf16[2,32,2048]{2,1,0:T(8,128)(2,1)}, bf16[2,32,2048]{2,1,0:T(8,128)(2,1)S(1)}, u32[]{:S(2)}, u32[]{:S(2)}) collective-permute-start(bf16[2,32,2048]{2,1,0:T(8,128)(2,1)} %refs_0_.1), channel_id=1, source_target_pairs={{0,24},{4,28},{8,16},{12,20},{16,8},{20,12},{24,0},{28,4},{1,25},{... | collective-permute-start | bytes 786440 | tf_op jit(solution)/shard_map/ppermute | solution.py:89
  5.2 14.4 %collective-permute-start = (bf16[2,32,2048]{2,1,0:T(8,128)(2,1)}, bf16[2,32,2048]{2,1,0:T(8,128)(2,1)S(1)}, u32[]{:S(2)}, u32[]{:S(2)}) collective-permute-start(bf16[2,32,2048]{2,1,0:T(8,128)(2,1)} %refs_0_.1), channel_id=1, source_target_pairs={{0,4},{4,0},{8,12},{12,8},{16,20},{20,16},{24,28},{28,24},{1,5},{5... | collective-permute-start | bytes 786440 | tf_op jit(solution)/shard_map/ppermute | solution.py:93
  10.2 14.1 %collective-permute-start.4 = (bf16[2,32,2048]{2,1,0:T(8,128)(2,1)S(1)}, bf16[2,32,2048]{2,1,0:T(8,128)(2,1)S(1)}, u32[]{:S(2)}, u32[]{:S(2)}) collective-permute-start(bf16[2,32,2048]{2,1,0:T(8,128)(2,1)S(1)} %collective-permute-done.3.refs_4_), channel_id=1, source_target_pairs={{0,4},{4,0},{8,12},{12,8},{16,20},{20,16},{24,28},{28,24},{1,5},{5... | collective-permute-start | bytes 786440 | tf_op jit(solution)/shard_map/ppermute | solution.py:93
  13.1 11.2 %collective-permute-start.2 = (bf16[2,32,2048]{2,1,0:T(8,128)(2,1)S(1)}, bf16[2,32,2048]{2,1,0:T(8,128)(2,1)S(1)}, u32[]{:S(2)}, u32[]{:S(2)}) collective-permute-start(bf16[2,32,2048]{2,1,0:T(8,128)(2,1)S(1)} %collective-permute-done.1.refs_2_), channel_id=1, source_target_pairs={{0,4},{4,0},{8,12},{12,8},{16,20},{20,16},{24,28},{28,24},{1,5},{5... | collective-permute-start | bytes 786440 | tf_op jit(solution)/shard_map/ppermute | solution.py:93
  17.1 7.2 %collective-permute-start.6 = (bf16[2,32,2048]{2,1,0:T(8,128)(2,1)S(1)}, bf16[2,32,2048]{2,1,0:T(8,128)(2,1)S(1)}, u32[]{:S(2)}, u32[]{:S(2)}) collective-permute-start(bf16[2,32,2048]{2,1,0:T(8,128)(2,1)S(1)} %collective-permute-done.5.refs_6_), channel_id=1, source_target_pairs={{0,4},{4,0},{8,12},{12,8},{16,20},{20,16},{24,28},{28,24},{1,5},{5... | collective-permute-start | bytes 786440 | tf_op jit(solution)/shard_map/ppermute | solution.py:93
  18.3 32.5 %collective-permute-start.10 = (bf16[2,64,4352]{2,1,0:T(8,128)(2,1)S(1)}, bf16[2,64,4352]{2,1,0:T(8,128)(2,1)S(1)}, u32[]{:S(2)}, u32[]{:S(2)}) collective-permute-start(bf16[2,64,4352]{2,1,0:T(8,128)(2,1)S(1)} %constant_dynamic-update-slice_fusion.refs_1_), channel_id=1, source_target_pairs={{1,0},{2,1},{3,2},{5,4},{6,5},{7,6},{9,8},{10,9},{11,10},{13,12},{... | collective-permute-start | bytes 3342344 | tf_op jit(solution)/shard_map/ppermute | solution.py:324
  19.6 32.5 %collective-permute-start.7 = (bf16[2,64,4352]{2,1,0:T(8,128)(2,1)S(1)}, bf16[2,64,4352]{2,1,0:T(8,128)(2,1)S(1)}, u32[]{:S(2)}, u32[]{:S(2)}) collective-permute-start(bf16[2,64,4352]{2,1,0:T(8,128)(2,1)S(1)} %constant_dynamic-update-slice_fusion.refs_1_), channel_id=1, source_target_pairs={{0,1},{1,2},{2,3},{4,5},{5,6},{6,7},{8,9},{9,10},{10,11},{12,13},{... | collective-permute-start | bytes 3342344 | tf_op jit(solution)/shard_map/ppermute | solution.py:321
  25.4 1.4 copy-start
  26.9 26.1 %copy-start.1 = (bf16[1024,2048]{1,0:T(8,128)(2,1)S(1)}, bf16[1024,2048]{1,0:T(8,128)(2,1)}, u32[]{:S(2)}) copy-start(bf16[1024,2048]{1,0:T(8,128)(2,1)} %wb_ref.3) | copy-start | bytes 12582916
  46.4 28.2 %collective-permute-start.18 = (s16[128,4480]{1,0:T(8,128)(2,1)S(1)}, s16[128,4480]{1,0:T(8,128)(2,1)S(1)}, u32[]{:S(2)}, u32[]{:S(2)}) collective-permute-start(s16[128,4480]{1,0:T(8,128)(2,1)S(1)} %get-tuple-element.14), channel_id=1, source_target_pairs={{0,1},{4,5},{8,9},{12,13},{16,17},{20,21},{24,25},{28,29}} | collective-permute-start | bytes 3440648 | tf_op jit(solution)/shard_map/ppermute | solution.py:321
  50.1 35.1 %collective-permute-start.21 = (s16[128,4480]{1,0:T(8,128)(2,1)S(1)}, s16[128,4480]{1,0:T(8,128)(2,1)S(1)}, u32[]{:S(2)}, u32[]{:S(2)}) collective-permute-start(s16[128,4480]{1,0:T(8,128)(2,1)S(1)} %get-tuple-element.15), channel_id=1, source_target_pairs={{3,2},{7,6},{11,10},{15,14},{19,18},{23,22},{27,26},{31,30}} | collective-permute-start | bytes 3440648 | tf_op jit(solution)/shard_map/ppermute | solution.py:324
  50.8 41.3 %collective-permute-start.11 = (bf16[2,64,4352]{2,1,0:T(8,128)(2,1)S(1)}, bf16[2,64,4352]{2,1,0:T(8,128)(2,1)S(1)}, u32[]{:S(2)}, u32[]{:S(2)}) collective-permute-start(bf16[2,64,4352]{2,1,0:T(8,128)(2,1)S(1)} %collective-permute-done.10.refs_5_), channel_id=1, source_target_pairs={{1,0},{2,1},{5,4},{6,5},{9,8},{10,9},{13,12},{14,13},{17,16},{18,1... | collective-permute-start | bytes 3342344 | tf_op jit(solution)/shard_map/ppermute | solution.py:324
  52.1 41.3 %collective-permute-start.8 = (bf16[2,64,4352]{2,1,0:T(8,128)(2,1)S(1)}, bf16[2,64,4352]{2,1,0:T(8,128)(2,1)S(1)}, u32[]{:S(2)}, u32[]{:S(2)}) collective-permute-start(bf16[2,64,4352]{2,1,0:T(8,128)(2,1)S(1)} %collective-permute-done.7.refs_2_), channel_id=1, source_target_pairs={{1,2},{2,3},{5,6},{6,7},{9,10},{10,11},{13,14},{14,15},{17,18},{18... | collective-permute-start | bytes 3342344 | tf_op jit(solution)/shard_map/ppermute | solution.py:321
  80.7 28.2 %collective-permute-start.19 = (s16[128,4480]{1,0:T(8,128)(2,1)S(1)}, s16[128,4480]{1,0:T(8,128)(2,1)S(1)}, u32[]{:S(2)}, u32[]{:S(2)}) collective-permute-start(s16[128,4480]{1,0:T(8,128)(2,1)S(1)} %add.29), channel_id=1, source_target_pairs={{0,1},{1,2},{4,5},{5,6},{8,9},{9,10},{12,13},{13,14},{16,17},{17,1... | collective-permute-start | bytes 3440648 | tf_op jit(solution)/shard_map/ppermute | solution.py:321
  91.4 28.1 %collective-permute-start.22 = (s16[128,4480]{1,0:T(8,128)(2,1)S(1)}, s16[128,4480]{1,0:T(8,128)(2,1)S(1)}, u32[]{:S(2)}, u32[]{:S(2)}) collective-permute-start(s16[128,4480]{1,0:T(8,128)(2,1)S(1)} %add.31), channel_id=1, source_target_pairs={{2,1},{3,2},{6,5},{7,6},{10,9},{11,10},{14,13},{15,14},{18,17},{19... | collective-permute-start | bytes 3440648 | tf_op jit(solution)/shard_map/ppermute | solution.py:324
  92.1 22.9 %copy-start.4 = (bf16[2,64,4352]{2,1,0:T(8,128)(2,1)}, bf16[2,64,4352]{2,1,0:T(8,128)(2,1)S(1)}, u32[]{:S(2)}) copy-start(bf16[2,64,4352]{2,1,0:T(8,128)(2,1)S(1)} %collective-permute-done.11.refs_6_) | copy-start | bytes 3342340
  92.1 34.8 %collective-permute-start.12 = (bf16[2,64,4352]{2,1,0:T(8,128)(2,1)S(1)}, bf16[2,64,4352]{2,1,0:T(8,128)(2,1)}, u32[]{:S(2)}, u32[]{:S(2)}) collective-permute-start(bf16[2,64,4352]{2,1,0:T(8,128)(2,1)S(1)} %collective-permute-done.11.refs_6_), channel_id=1, source_target_pairs={{1,0},{5,4},{9,8},{13,12},{17,16},{21,20},{25,24},{29,28}} | collective-permute-start | bytes 3342344 | tf_op jit(solution)/shard_map/ppermute | solution.py:324
  93.4 33.5 %collective-permute-start.9 = (bf16[2,64,4352]{2,1,0:T(8,128)(2,1)S(1)}, bf16[2,64,4352]{2,1,0:T(8,128)(2,1)S(1)}, u32[]{:S(2)}, u32[]{:S(2)}) collective-permute-start(bf16[2,64,4352]{2,1,0:T(8,128)(2,1)S(1)} %collective-permute-done.8.refs_3_), channel_id=1, source_target_pairs={{2,3},{6,7},{10,11},{14,15},{18,19},{22,23},{26,27},{30,31}} | collective-permute-start | bytes 3342344 | tf_op jit(solution)/shard_map/ppermute | solution.py:321
  115.0 64.8 %collective-permute-start.20 = (s16[128,4480]{1,0:T(8,128)(2,1)S(1)}, s16[128,4480]{1,0:T(8,128)(2,1)S(1)}, u32[]{:S(2)}, u32[]{:S(2)}) collective-permute-start(s16[128,4480]{1,0:T(8,128)(2,1)S(1)} %add.30), channel_id=1, source_target_pairs={{0,1},{1,2},{2,3},{4,5},{5,6},{6,7},{8,9},{9,10},{10,11},{12,13},{... | collective-permute-start | bytes 3440648 | tf_op jit(solution)/shard_map/ppermute | solution.py:321
  125.6 54.2 %collective-permute-start.23 = (s16[128,4480]{1,0:T(8,128)(2,1)S(1)}, s16[128,4480]{1,0:T(8,128)(2,1)S(1)}, u32[]{:S(2)}, u32[]{:S(2)}) collective-permute-start(s16[128,4480]{1,0:T(8,128)(2,1)S(1)} %add.32), channel_id=1, source_target_pairs={{1,0},{2,1},{3,2},{5,4},{6,5},{7,6},{9,8},{10,9},{11,10},{13,12},{... | collective-permute-start | bytes 3440648 | tf_op jit(solution)/shard_map/ppermute | solution.py:324
  131.2 1.2 collective-permute-start.13
  132.5 3.6 %collective-permute-start.14 = (f32[8,128]{1,0:T(8,128)S(1)}, f32[8,128]{1,0:T(8,128)S(1)}, u32[]{:S(2)}, u32[]{:S(2)}) collective-permute-start(f32[8,128]{1,0:T(8,128)S(1)} %add.22), channel_id=1, source_target_pairs={{0,8},{4,12},{8,0},{12,4},{16,24},{20,28},{24,16},{28,20},{1,9},{5... | collective-permute-start | bytes 12296 | tf_op jit(solution)/shard_map/ppermute | solution.py:258
  136.1 3.6 %collective-permute-start.15 = (f32[8,128]{1,0:T(8,128)S(1)}, f32[8,128]{1,0:T(8,128)S(1)}, u32[]{:S(2)}, u32[]{:S(2)}) collective-permute-start(f32[8,128]{1,0:T(8,128)S(1)} %add.23), channel_id=1, source_target_pairs={{0,16},{4,20},{8,24},{12,28},{16,0},{20,4},{24,8},{28,12},{1,17},{... | collective-permute-start | bytes 12296 | tf_op jit(solution)/shard_map/ppermute | solution.py:258
  139.7 13.0 %collective-permute-start.16 = (f32[8,128]{1,0:T(8,128)S(1)}, f32[8,128]{1,0:T(8,128)S(1)}, u32[]{:S(2)}, u32[]{:S(2)}) collective-permute-start(f32[8,128]{1,0:T(8,128)S(1)} %add.24), channel_id=1, source_target_pairs={{0,1},{1,0},{2,3},{3,2},{4,5},{5,4},{6,7},{7,6},{8,9},{9,8},{10,11... | collective-permute-start | bytes 12296 | tf_op jit(solution)/shard_map/ppermute | solution.py:258
  152.7 4.5 %collective-permute-start.17 = (f32[8,128]{1,0:T(8,128)S(1)}, f32[8,128]{1,0:T(8,128)S(1)}, u32[]{:S(2)}, u32[]{:S(2)}) collective-permute-start(f32[8,128]{1,0:T(8,128)S(1)} %add.25), channel_id=1, source_target_pairs={{0,2},{1,3},{2,0},{3,1},{4,6},{5,7},{6,4},{7,5},{8,10},{9,11},{10,... | collective-permute-start | bytes 12296 | tf_op jit(solution)/shard_map/ppermute | solution.py:258

commit v2 on v0

v2 whole, which is shorter than its diff:
```python
import functools
import math

import jax
import jax.numpy as jnp
from jax import lax
from jax.experimental import pallas as pl
from jax.experimental.pallas import tpu as pltpu
from jax.sharding import PartitionSpec as P

GAMMA = 0.01
VMEM = pltpu.VMEM
F32 = jnp.float32
BF16 = jnp.bfloat16
I16 = jnp.int16
LANES = 128
LIMIT = 32 * 1024 * 1024


def params(grid_dims):
    return pltpu.CompilerParams(
        dimension_semantics=("arbitrary",) * grid_dims, vmem_limit_bytes=LIMIT
    )


def cost(bytes_accessed):
    return pl.CostEstimate(flops=int(300 * bytes_accessed), bytes_accessed=int(bytes_accessed), transcendentals=0)


def held_back(kernel, count):
    def run(*refs, operands):
        kernel(*refs[: operands - count], *refs[operands:])

    return run


def call(kernel, arrays, specs, deps=(), **rest):
    operands = len(arrays) + len(deps)
    if deps:
        kernel = functools.partial(held_back(kernel, len(deps)), operands=operands)
    specs = list(specs) + [pl.BlockSpec(memory_space=pl.ANY)] * len(deps)
    return pl.pallas_call(kernel, in_specs=specs, **rest)(*arrays, *deps)


def full(shape):
    return pl.BlockSpec(shape, lambda *_: (0,) * len(shape))


class Chunk:
    def __init__(self, parts):
        self.parts = parts
        self.width = sum(p[2] for p in parts)
        self.groups = []
        column = 0
        for _, _, size in parts:
            count = -(-size // 1024)
            tiles = size // LANES
            for g in range(count):
                begin, end = tiles * g // count, tiles * (g + 1) // count
                self.groups.append((column + begin * LANES, (end - begin) * LANES))
            column += size
        self.message = self.width + LANES

    def places(self):
        column = 0
        for which, first, size in self.parts:
            for at in range(0, size, LANES):
                yield column + at, which, first + at
            column += size


TOP = 32760.0


def encode(chunk, value, out, start, rows):
    lane = lax.broadcasted_iota(jnp.int32, (rows, LANES), 1)
    side = jnp.zeros((rows, LANES), F32)
    at = pl.ds(start, rows)
    for g, (first, size) in enumerate(chunk.groups):
        values = [value(column) for column in range(first, first + size, LANES)]
        largest = jnp.abs(values[0])
        for v in values[1:]:
            largest = jnp.maximum(largest, jnp.abs(v))
        largest = jnp.max(largest, axis=1, keepdims=True)
        exponent = jnp.clip(jnp.ceil(jnp.log2(jnp.maximum(largest, 1e-37))), -110.0, 126.0)
        mantissa = jnp.floor(largest * jnp.exp2(-exponent) * 8192.0) + 2.0
        inverse = jnp.broadcast_to((TOP * 8192.0 / mantissa) * jnp.exp2(-exponent), (rows, LANES))
        side = jnp.where(lane == 2 * g, exponent, jnp.where(lane == 2 * g + 1, mantissa, side))
        for n, v in enumerate(values):
            codes = jnp.floor(v * inverse + 0.5).astype(jnp.int32).astype(I16)
            out[at, first + n * LANES : first + (n + 1) * LANES] = codes
    out[at, chunk.width :] = side.astype(jnp.int32).astype(I16)


def decoder(chunk, message, start, rows):
    at = pl.ds(start, rows)
    side = message[at, chunk.width :].astype(jnp.int32).astype(F32)
    scales = []
    for g in range(len(chunk.groups)):
        scale = jnp.exp2(side[:, 2 * g : 2 * g + 1]) * (side[:, 2 * g + 1 : 2 * g + 2] / (TOP * 8192.0))
        scales.append(jnp.broadcast_to(scale, (rows, LANES)))

    def value(column):
        g = [i for i, (first, size) in enumerate(chunk.groups) if first <= column < first + size][0]
        return message[at, column : column + LANES].astype(jnp.int32).astype(F32) * scales[g]

    return value


def code_kernel(chunk, step, hidden, context, out):
    arrays = (hidden, context)
    places = {column: (which, at) for column, which, at in chunk.places()}
    local = hidden.shape[1]
    for b in range(hidden.shape[0]):
        for start in range(0, local, step):

            def value(column):
                which, at = places[column]
                return arrays[which][b, start : start + step, at : at + LANES].astype(F32)

            encode(chunk, value, out, b * local + start, step)


def code_own(chunk, hidden, context, deps=()):
    examples, local, _ = hidden.shape
    rows = examples * local
    return call(
        functools.partial(code_kernel, chunk, 16),
        (hidden, context),
        [pl.BlockSpec(memory_space=VMEM)] * 2,
        deps,
        out_shape=jax.ShapeDtypeStruct((rows, chunk.message), I16),
        out_specs=pl.BlockSpec(memory_space=VMEM),
        compiler_params=pltpu.CompilerParams(vmem_limit_bytes=16 * 2**20),
        cost_estimate=cost(4e6),
        name="code",
    )


def place(n):
    c = lax.axis_index("col")
    return jnp.where(lax.axis_index("row") % 2 == 0, c, n - 1 - c)


def flow_pairs(n, row_count, flow):
    pairs = []
    for row in range(row_count):
        for c in range(n - 1):
            low, high = row * n + c, row * n + c + 1
            pairs.append((low, high) if (row % 2 == 0) == (flow == 0) else (high, low))
    return pairs


def arrange_kernel(row_count, col_count, spans, *refs):
    pieces, out = refs[:-1], refs[-1]
    r, c = lax.axis_index("row"), lax.axis_index("col")
    examples, held, _ = pieces[0].shape
    per_block = row_count // col_count
    for j, piece in enumerate(pieces):
        source = r ^ j
        block = source // per_block
        k = jnp.where(r % 2 == 0, c - block, block - c)
        k = lax.rem(k + col_count, col_count)
        start = pl.multiple_of(lax.rem(source, per_block) * held, held)
        position = source * held + lax.broadcasted_iota(jnp.int32, (held, 1), 0)
        for b in range(examples):
            keep = (position >= spans[b, 0]) & (position < spans[b, 1])
            value = piece[b].astype(F32) * keep.astype(F32)
            out[k, b, pl.ds(start, held), :] = value.astype(BF16)


def arrange(pieces, spans, row_count, col_count):
    examples, held, width = pieces[0].shape
    local = held * row_count // col_count
    shape = (col_count, examples, local, width)
    return pl.pallas_call(
        functools.partial(arrange_kernel, row_count, col_count),
        out_shape=jax.ShapeDtypeStruct(shape, BF16),
        in_specs=[pl.BlockSpec(memory_space=pltpu.SMEM)]
        + [pl.BlockSpec(memory_space=VMEM)] * len(pieces),
        out_specs=pl.BlockSpec(memory_space=VMEM),
        compiler_params=pltpu.CompilerParams(vmem_limit_bytes=LIMIT),
        cost_estimate=cost(4e6),
        name="arrange",
    )(spans, *pieces)


def after(x, *others):
    return lax.optimization_barrier((x, *others))[0]


def after(x, *others):
    return lax.optimization_barrier((x, *others))[0]


def gather_rows(x, row_count, others):
    near = [x]
    for j in range(2, row_count, 2):
        near.append(lax.ppermute(x, "row", [(i, i ^ j) for i in range(row_count)]))
    pieces = []
    for j, piece in enumerate(near):
        if j > 0:
            piece = after(piece, *others)
        pieces.append(piece)
        pieces.append(lax.ppermute(piece, "row", [(i, i ^ 1) for i in range(row_count)]))
    return pieces


def pieces_of(size):
    cut = (size // LANES + 1) // 2 * LANES if size > 1024 else size
    return [(0, cut)] + ([(cut, size - cut)] if cut < size else [])


def partial_kernel(plan, ks, m_ref, wa, wb, out, held, sems):
    weights = (wa, wb)
    copies = []
    for number, (which, source, start, size) in enumerate(plan):
        copy = pltpu.make_async_copy(
            weights[which].at[pl.ds(source, size)], held.at[pl.ds(start, size)], sems.at[number]
        )
        copy.start()
        copies.append(copy)
    rows = out.shape[1]
    p = place(m_ref.shape[0])
    masked = jnp.concatenate(
        [m_ref[pl.ds(k(p), 1)].reshape(rows, m_ref.shape[-1]) for k in ks], axis=0
    )
    for copy, (_, _, start, size) in zip(copies, plan):
        copy.wait()
        value = lax.dot_general(
            masked, held[pl.ds(start, size)], NT, preferred_element_type=F32
        )
        for n in range(len(ks)):
            out[n, :, start : start + size] = value[n * rows : (n + 1) * rows]


def partials(chunk, masked, ks, wa, wb, bytes_accessed, deps=()):
    _, examples, local, width = masked.shape
    rows = examples * local
    plan, column = [], 0
    for which, first, count in chunk.parts:
        for start, size in pieces_of(count):
            plan.append((which, first + start, column + start, size))
        column += count
    return call(
        functools.partial(partial_kernel, plan, ks),
        (masked, wa, wb),
        [pl.BlockSpec(memory_space=VMEM)] + [pl.BlockSpec(memory_space=pl.ANY)] * 2,
        deps,
        out_shape=jax.ShapeDtypeStruct((len(ks), rows, chunk.width), F32),
        out_specs=pl.BlockSpec(memory_space=VMEM),
        scratch_shapes=[
            pltpu.VMEM((chunk.width, width), BF16),
            pltpu.SemaphoreType.DMA((len(plan),)),
        ],
        compiler_params=pltpu.CompilerParams(vmem_limit_bytes=40 * 2**20),
        cost_estimate=cost(bytes_accessed),
        name="partials",
    )


STEPS = 2
FIRST = 4e6
ROWS = 16


def outer_made_first(n, k):
    early = place(n) < n // 2
    return early if k == 1 else jnp.logical_not(early)


def next_kernel(chunk, n, s, flow, keys, *refs):
    sums, (came, out) = dict(zip(keys, refs)), refs[len(keys) :]
    k = s if flow == 0 else n - s
    mine = place(n) if flow == 0 else n - 1 - place(n)
    rows = came.shape[0]

    @pl.when((mine >= s) & (mine < n - 1))
    def _():
        out[...] = came[...]

    def add(held):
        def one(i, carry):
            start = pl.multiple_of(i * ROWS, ROWS)
            old = decoder(chunk, came, start, ROWS)

            def value(column):
                return held[0, pl.ds(start, ROWS), column : column + LANES] + old(column)

            encode(chunk, value, out, start, ROWS)
            return carry

        lax.fori_loop(0, rows // ROWS, one, 0)

    if ("second", 0) not in sums:

        @pl.when(mine < s)
        def _():
            add(sums[keys[0]])

    else:

        @pl.when((mine < s) & outer_made_first(n, k))
        def _():
            add(sums["first", 0])

        @pl.when((mine < s) & jnp.logical_not(outer_made_first(n, k)))
        def _():
            add(sums["second", 0])


def next_message(chunk, n, s, flow, first, second, came, deps=()):
    rows = came.shape[0]
    step = rows // STEPS
    k = s if flow == 0 else n - s
    keys = [("first", 0 if k in (1, n - 1) else k - 1)]
    if s == n - 1 and s > 1:
        keys.append(("second", 0))
    message = pl.BlockSpec((step, chunk.message), lambda i: (i, 0))
    return call(
        functools.partial(next_kernel, chunk, n, s, flow, keys),
        [first if which == "first" else second for which, _ in keys] + [came],
        [pl.BlockSpec((1, step, chunk.width), lambda i, at=at: (at, i, 0)) for _, at in keys]
        + [message],
        deps,
        grid=(STEPS,),
        out_shape=jax.ShapeDtypeStruct(came.shape, I16),
        out_specs=message,
        compiler_params=params(1),
        cost_estimate=cost(40e6),
        name="next",
    )


def finish_kernel(chunks, at, *refs):
    count = len(chunks)
    sums, rights, lefts = refs[:count], refs[count : 2 * count], refs[2 * count : 3 * count]
    outs = refs[3 * count :]
    rows = rights[0].shape[0]
    for start in range(0, rows, ROWS):
        for chunk, total, right, left in zip(chunks, sums, rights, lefts):
            old_right = decoder(chunk, right, start, ROWS)
            old_left = decoder(chunk, left, start, ROWS)
            for column, which, place in chunk.places():
                value = total[0, start : start + ROWS, column : column + LANES]
                value = value + old_right(column) + old_left(column)
                outs[which][0, start : start + ROWS, place : place + LANES] = value.astype(BF16)


def finish(chunks, sums, at, rights, lefts, examples, widths, deps=()):
    rows = sums[0].shape[1]
    local = rows // examples
    half = local // 2
    return call(
        functools.partial(finish_kernel, chunks, at),
        [*sums, *rights, *lefts],
        [pl.BlockSpec((1, half, x.shape[2]), lambda i: (at, i, 0)) for x in sums]
        + [pl.BlockSpec((half, x.shape[1]), lambda i: (i, 0)) for x in (*rights, *lefts)],
        deps,
        grid=(2 * examples,),
        out_shape=[jax.ShapeDtypeStruct((examples, local, w), BF16) for w in widths],
        out_specs=[pl.BlockSpec((1, half, w), lambda i: (i // 2, i % 2, 0)) for w in widths],
        compiler_params=params(1),
        cost_estimate=cost(8e6),
        name="finish",
    )


NT = (((1,), (1,)), ((), ()))


def gram_kernel(m_ref, out):
    for b in range(out.shape[0]):
        masked = m_ref[:, b].reshape(out.shape[1], m_ref.shape[-1])
        out[b] = lax.dot_general(masked, masked, NT, preferred_element_type=F32)


def gram(masked, deps=()):
    col_count, examples, local, width = masked.shape
    length = col_count * local
    return call(
        gram_kernel,
        (masked,),
        [pl.BlockSpec(memory_space=VMEM)],
        deps,
        out_shape=jax.ShapeDtypeStruct((examples, length, length), F32),
        out_specs=pl.BlockSpec(memory_space=VMEM),
        compiler_params=pltpu.CompilerParams(vmem_limit_bytes=16 * 2**20),
        cost_estimate=cost(3e6),
        name="gram",
    )


def join_kernel(chunk, n, gram_ref, hidden, context, *refs):
    rights, lefts = refs[: n - 1], refs[n - 1 : 2 * n - 2]
    joined, out = refs[-2:]
    p = place(n)
    arrays = (hidden, context)
    examples, local, _ = hidden.shape
    for column, which, at in chunk.places():
        joined[:, :local, column : column + LANES] = arrays[which][:, :, at : at + LANES]

    def take(k, message):
        for b in range(examples):

            def one(i, carry):
                start = pl.multiple_of(i * ROWS, ROWS)
                value = decoder(chunk, message, b * local + start, ROWS)
                for column in range(0, chunk.width, LANES):
                    joined[b, pl.ds(k * local + start, ROWS), column : column + LANES] = value(
                        column
                    ).astype(BF16)
                return carry

            lax.fori_loop(0, local // ROWS, one, 0)

    for k in range(1, n):

        @pl.when(p >= k)
        def _():
            take(k, rights[k - 1])

        @pl.when(p < k)
        def _():
            take(k, lefts[n - k - 1])

    lane = lax.broadcasted_iota(jnp.int32, out.shape, 1)
    total = jnp.zeros(out.shape, F32)
    for b in range(examples):
        feature = joined[b]
        feature_gram = lax.dot_general(feature, feature, NT, preferred_element_type=F32)
        total = jnp.where(lane == b, jnp.sum(feature_gram * gram_ref[b]), total)
    out[...] = total


def join(chunk, masked_gram, hidden, context, rights, lefts, deps=()):
    n = len(rights) + 1
    examples, local, _ = hidden.shape
    arrays = [masked_gram, hidden, context, *rights, *lefts]
    shape = (examples, n * local, chunk.width)
    return call(
        functools.partial(join_kernel, chunk, n),
        arrays,
        [pl.BlockSpec(memory_space=VMEM)] * len(arrays),
        deps,
        out_shape=[jax.ShapeDtypeStruct(shape, BF16), jax.ShapeDtypeStruct((8, LANES), F32)],
        out_specs=[pl.BlockSpec(memory_space=VMEM)] * 2,
        compiler_params=pltpu.CompilerParams(vmem_limit_bytes=24 * 2**20),
        cost_estimate=cost(16e6),
        name="join",
    )


def sum_over(x, axis, count, groups):
    for group in groups:
        came = [lax.ppermute(x, axis, [(i, i ^ j) for i in range(count)]) for j in group]
        came = lax.optimization_barrier(came)
        for y in came:
            x = x + y
    return x


def weight_kernel(widths, factor, m_ref, *refs):
    features, outs = refs[:-2], refs[-2:]
    examples, length = features[0].shape[:2]
    masked = [m_ref[:, b].reshape(length, m_ref.shape[-1]) for b in range(examples)]
    column = 0
    for x in features:
        for start in range(0, x.shape[2], LANES):
            out, at = (0, column) if column < widths[0] else (1, column - widths[0])
            total = None
            for b in range(examples):
                each = lax.dot_general(
                    x[b, :, start : start + LANES],
                    masked[b],
                    (((0,), (0,)), ((), ())),
                    preferred_element_type=F32,
                )
                each = factor[out, b] * each
                total = each if total is None else total + each
            outs[out][at : at + LANES] = total
            column += LANES


def weight_grads(factor, masked, features, widths):
    col_count, examples, local, width = masked.shape
    tile = min(256, width)
    whole = lambda x: pl.BlockSpec(x.shape, lambda i: (0, 0, 0), pipeline_mode=pl.Buffered(1))
    return pl.pallas_call(
        functools.partial(weight_kernel, widths),
        grid=(width // tile,),
        out_shape=[jax.ShapeDtypeStruct((w, width), F32) for w in widths],
        in_specs=[
            pl.BlockSpec(memory_space=pltpu.SMEM),
            pl.BlockSpec((col_count, examples, local, tile), lambda i: (0, 0, 0, i)),
        ]
        + [whole(x) for x in features],
        out_specs=[pl.BlockSpec((w, tile), lambda i: (0, i)) for w in widths],
        compiler_params=params(1),
        cost_estimate=cost(48e6),
        name="weights",
    )(factor, masked, *features)


def body(row_count, col_count, scales, cotangent, hidden, context, wa, wb, spans):
    n = col_count
    widths = (hidden.shape[2], context.shape[2])
    examples = hidden.shape[0]
    chunk = Chunk([(0, 0, widths[0]), (1, 0, widths[1])])

    def send(x, flow):
        return lax.ppermute(x, ("row", "col"), flow_pairs(n, row_count, flow))

    own = code_own(chunk, hidden, context)
    came = [[send(own, 0)], [send(own, 1)]]
    masked = arrange(gather_rows(cotangent, row_count, (own,)), spans, row_count, n)

    first_ks = [lambda p: jnp.where(p < n // 2, 1, n - 1)]
    first_ks += [lambda p, k=k: k for k in range(2, n - 1)]
    second_ks = [lambda p: jnp.where(p < n // 2, n - 1, 1), lambda p: 0]
    first = partials(chunk, masked, first_ks, wa, wb, FIRST)
    second, latest = None, ()
    for s in range(1, n):
        if s == n - 1:
            second = partials(chunk, masked, second_ks, wa, wb, 4e6, latest)
            masked_gram = gram(masked, (second,))
            latest = (second,)
        for flow in (0, 1):
            message = next_message(chunk, n, s, flow, first, second, came[flow][-1], latest)
            latest = (message,)
            came[flow].append(send(message, flow))

    joined = [
        join(chunk, masked_gram, hidden, context, came[0][:-1], came[1][:-1], latest)
    ]
    sq_norm = sum(j[1] for j in joined)
    sq_norm = sum_over(sq_norm, "row", row_count, [[1], range(2, row_count, 2)])
    sq_norm = after(sq_norm, came[0][-1])
    sq_norm = sum_over(sq_norm, "col", n, [range(1, n)])
    factor = 1.0 / (jnp.sqrt(sq_norm[0, :examples]) + GAMMA)
    factor = jnp.stack([factor * scale for scale in scales])
    down_grad, heads_grad = weight_grads(factor, masked, [j[0] for j in joined], widths)
    hidden_grad, context_grad = finish(
        [chunk], [second], 1, [came[0][-1]], [came[1][-1]], examples, widths, (factor,)
    )
    return down_grad, heads_grad, hidden_grad, context_grad


def solution(mesh):
    row_count, col_count = mesh.shape["row"], mesh.shape["col"]

    def run(cotangent, hidden, context, down_weight, heads_weight, spans):
        examples = hidden.shape[0]
        scales = tuple(math.sqrt(w.shape[0] * w.shape[1]) / examples for w in (down_weight, heads_weight))
        in_specs = (
            P(None, "row", "col"),
            P(None, "col", "row"),
            P(None, "col", "row"),
            P("row", "col"),
            P("row", "col"),
            P(),
        )
        out_specs = (P("row", "col"), P("row", "col"), P(None, "col", "row"), P(None, "col", "row"))
        return jax.shard_map(
            functools.partial(body, row_count, col_count, scales),
            mesh=mesh,
            in_specs=in_specs,
            out_specs=out_specs,
            check_vma=False,
        )(cotangent, hidden, context, down_weight, heads_weight, spans)

    return run
```

time: 317 us -> 137 us (0.43)
  other arithmetic: 71 us -> 0.04 us
  matrix products: 54.2 us -> 0 us
  waiting for transfers between devices: 99.8 us -> 45.7 us
  Pallas kernels: 0 us -> 53.8 us
  blocking collectives: 39.5 us -> 0 us
  local copies, waits for them, and re-layouts: 37.5 us -> 2.38 us
  starting transfers between devices: 0.38 us -> 33.7 us
  between operations: 13.8 us -> 0.92 us
    all_gather x3 -> x0, waiting for transfers between devices: 98.3 us -> none  [the longest x1 59.1 us: body(): hidden_all = lax.all_gather(hidden, 'col', axis=1, tiled=True)]
    dot_general x4 -> x0, matrix products: 54.2 us -> none  [the longest x2 34.7 us: weight_terms(): jnp.einsum('igm,iga->ima', feature_values, cotangent_matrix_rows, preferr...]
    pallas_call x0 -> x14, Pallas kernels: none -> 53.8 us  [the longest x12 37.7 us: call(): return pl.pallas_call(kernel, in_specs=specs, **rest)(*arrays, *deps)]
    ppermute x0 -> x22, waiting for transfers between devices: none -> 45.7 us  [the longest x8 30.5 us: send(): return lax.ppermute(x, ('row', 'col'), flow_pairs(n, row_count, flow))]
    reduce_sum x2 -> x0, other arithmetic: 40.2 us -> none  [the longest x1 31.8 us: body(): jnp.sum(clip_factor[:, None, None] * down_weight_blocks, axis=0)]
    psum x1 -> x0, blocking collectives: 39.5 us -> none  [clip_scales(): sq_norm = lax.psum(partial_sq, ('row', 'col'))]
    unnamed x4 -> x18, local copies, waits for them, and re-layouts: 36.5 us -> 2.38 us
    ppermute x0 -> x22, starting transfers between devices: none -> 33.7 us  [the longest x8 21.7 us: send(): return lax.ppermute(x, ('row', 'col'), flow_pairs(n, row_count, flow))]
  transfers between devices with their start and end apart: 5 -> 22, of which waited for: 3 -> 13; matrix products, arithmetic and copies ran while one was open for 50% -> 0% of each run, Pallas kernels for 0% -> 37%
where the time goes in v2:
time: 137 us
  Pallas kernels  53.8 us (39%)
  waiting for transfers between devices  45.7 us (33%)
  starting transfers between devices  33.7 us (25%)
  local copies, waits for them, and re-layouts  2.38 us (2%)
    pallas_call x12, Pallas kernels, call(): return pl.pallas_call(kernel, in_specs=specs, **rest)(*arrays, *deps)  37.7 us
    ppermute x8, waiting for transfers between devices, send(): return lax.ppermute(x, ('row', 'col'), flow_pairs(n, row_count, flow))  30.5 us
    ppermute x8, starting transfers between devices, send(): return lax.ppermute(x, ('row', 'col'), flow_pairs(n, row_count, flow))  21.7 us
    pallas_call x1, Pallas kernels, weight_grads(): pl.pallas_call(functools.partial(weight_kernel, widths), grid=(width // t...  15 us
    ppermute x3, waiting for transfers between devices, gather_rows(): near.append(lax.ppermute(x, 'row', [(i, i ^ j) for i in range(row_count)]))  8.91 us
    ppermute x7, starting transfers between devices, sum_over(): lax.ppermute(x, axis, [(i, i ^ j) for i in range(count)])  8.01 us
    ppermute x7, waiting for transfers between devices, sum_over(): lax.ppermute(x, axis, [(i, i ^ j) for i in range(count)])  5.8 us
    ppermute x3, starting transfers between devices, gather_rows(): near.append(lax.ppermute(x, 'row', [(i, i ^ j) for i in range(row_count)]))  3.55 us
  transfers between devices with their start and end apart: 22, of which 13 were waited for; matrix products, arithmetic and copies ran while one was open for 0% of the time, Pallas kernels for 37%

profile of v2, /device:TPU:0, one launch (start us, length us, event | category | flops | bytes accessed | tf_op | source)
XLA Modules:
  0.0 136.6 jit_solution(8614912013644360566)
XLA Ops:
  0.6 1.1 copy-done.3
  1.8 0.9 copy-done.6
  2.7 0.8 code.1
  3.6 5.3 %collective-permute-start.8 = (s16[128,4480]{1,0:T(8,128)(2,1)S(1)}, s16[128,4480]{1,0:T(8,128)(2,1)S(1)}, u32[]{:S(2)}, u32[]{:S(2)}) collective-permute-start(s16[128,4480]{1,0:T(8,128)(2,1)S(1)} %code.1), channel_id=1, source_target_pairs={{0,1},{1,2},{2,3},{5,4},{6,5},{7,6},{8,9},{9,10},{10,11},{13,12},{... | collective-permute-start | bytes 3440648 | tf_op jit(solution)/shard_map/ppermute | solution.py:512
  8.8 2.5 %collective-permute-start.5 = (bf16[2,32,2048]{2,1,0:T(8,128)(2,1)S(1)}, bf16[2,32,2048]{2,1,0:T(8,128)(2,1)S(1)}, u32[]{:S(2)}, u32[]{:S(2)}) collective-permute-start(bf16[2,32,2048]{2,1,0:T(8,128)(2,1)S(1)} %copy-done.5), channel_id=1, source_target_pairs={{0,24},{4,28},{8,16},{12,20},{16,8},{20,12},{24,0},{28,4},{1,25},{... | collective-permute-start | bytes 786440 | tf_op jit(solution)/shard_map/ppermute | solution.py:199
  11.4 0.5 collective-permute-start.3
  11.9 0.5 collective-permute-start.1
  12.4 5.9 %collective-permute-done.5.refs_6_ = bf16[2,32,2048]{2,1,0:T(8,128)(2,1)S(1)} collective-permute-done((bf16[2,32,2048]{2,1,0:T(8,128)(2,1)S(1)}, bf16[2,32,2048]{2,1,0:T(8,128)(2,1)S(1)}, u32[]{:S(2)}, u32[]{:S(2)}) %collective-permute-start.5) | collective-permute-done | bytes 262176 | tf_op jit(solution)/shard_map/ppermute | solution.py:199
  18.3 2.7 %collective-permute-done.3.refs_4_ = bf16[2,32,2048]{2,1,0:T(8,128)(2,1)S(1)} collective-permute-done((bf16[2,32,2048]{2,1,0:T(8,128)(2,1)S(1)}, bf16[2,32,2048]{2,1,0:T(8,128)(2,1)S(1)}, u32[]{:S(2)}, u32[]{:S(2)}) %collective-permute-start.3) | collective-permute-done | bytes 262176 | tf_op jit(solution)/shard_map/ppermute | solution.py:199
  21.0 0.3 collective-permute-done.1.refs_2_
  21.3 0.5 collective-permute-start.4
  21.8 1.3 collective-permute-start.7
  23.1 0.1 collective-permute-done.4.refs_5_
  23.2 0.4 collective-permute-done.6.refs_7_
  23.6 1.1 arrange.1.m_ref.refs_0_
  24.7 9.0 %partials.2.refs_0_ = f32[2,128,4352]{2,1,0:T(8,128)S(1)} custom-call(bf16[4,2,64,2048]{3,2,1,0:T(8,128)(2,1)S(1)} %arrange.1.m_ref.refs_0_, bf16[3328,2048]{1,0:T(8,128)(2,1)} %refs_1_.2, bf16[1024,2048]{1,0:T(8,128)(2,1)S(1)} %copy-done), custom_call_target="tpu_custom_call" | custom-call | flops 1200000000 | bytes 4000000 | tf_op jit(solution)/shard_map/partials/pallas_call | solution.py:42
  33.7 2.7 %next.6.refs_2_ = s16[128,4480]{1,0:T(8,128)(2,1)S(1)} custom-call(f32[2,128,4352]{2,1,0:T(8,128)S(1)} %partials.2.refs_0_, s16[128,4480]{1,0:T(8,128)(2,1)S(1)} %collective-permute-done.8.refs_1_.refs_3_), custom_call_target="tpu_custom_call" | custom-call | flops 12000000000 | bytes 40000000 | tf_op jit(solution)/shard_map/next/pallas_call | solution.py:42
  36.3 2.0 %collective-permute-start.10 = (s16[128,4480]{1,0:T(8,128)(2,1)S(1)}, s16[128,4480]{1,0:T(8,128)(2,1)S(1)}, u32[]{:S(2)}, u32[]{:S(2)}) collective-permute-start(s16[128,4480]{1,0:T(8,128)(2,1)S(1)} %next.6.refs_2_), channel_id=1, source_target_pairs={{0,1},{1,2},{2,3},{5,4},{6,5},{7,6},{8,9},{9,10},{10,11},{13,12},{... | collective-permute-start | bytes 3440648 | tf_op jit(solution)/shard_map/ppermute | solution.py:512
  38.4 1.5 %collective-permute-done.7.refs_1_.refs_6_ = s16[128,4480]{1,0:T(8,128)(2,1)S(1)} collective-permute-done((s16[128,4480]{1,0:T(8,128)(2,1)S(1)}, s16[128,4480]{1,0:T(8,128)(2,1)S(1)}, u32[]{:S(2)}, u32[]{:S(2)}) %collective-permute-start.7) | collective-permute-done | bytes 1146912 | tf_op jit(solution)/shard_map/ppermute | solution.py:512
  39.9 1.3 collective-permute-start.9
  41.2 18.3 %collective-permute-done.10.refs_1_.refs_4_ = s16[128,4480]{1,0:T(8,128)(2,1)S(1)} collective-permute-done((s16[128,4480]{1,0:T(8,128)(2,1)S(1)}, s16[128,4480]{1,0:T(8,128)(2,1)S(1)}, u32[]{:S(2)}, u32[]{:S(2)}) %collective-permute-start.10) | collective-permute-done | bytes 1146912 | tf_op jit(solution)/shard_map/ppermute | solution.py:512
  59.5 2.6 %next.8.refs_2_ = s16[128,4480]{1,0:T(8,128)(2,1)S(1)} custom-call(f32[2,128,4352]{2,1,0:T(8,128)S(1)} %partials.2.refs_0_, s16[128,4480]{1,0:T(8,128)(2,1)S(1)} %collective-permute-done.10.refs_1_.refs_4_, s16[128,4480]{1,0:T(8,128)(2,1)S(1)} %next.7.refs_2_), custom_call_target="tpu_custom_call" | custom-call | flops 12000000000 | bytes 40000000 | tf_op jit(solution)/shard_map/next/pallas_call | solution.py:42
  62.2 4.5 %collective-permute-start.11 = (s16[128,4480]{1,0:T(8,128)(2,1)S(1)}, s16[128,4480]{1,0:T(8,128)(2,1)S(1)}, u32[]{:S(2)}, u32[]{:S(2)}) collective-permute-start(s16[128,4480]{1,0:T(8,128)(2,1)S(1)} %next.8.refs_2_), channel_id=1, source_target_pairs={{0,1},{1,2},{2,3},{5,4},{6,5},{7,6},{8,9},{9,10},{10,11},{13,12},{... | collective-permute-start | bytes 3440648 | tf_op jit(solution)/shard_map/ppermute | solution.py:512
  66.6 0.1 next.9.refs_3_
  66.7 1.5 %collective-permute-start.12 = (s16[128,4480]{1,0:T(8,128)(2,1)S(1)}, s16[128,4480]{1,0:T(8,128)(2,1)}, u32[]{:S(2)}, u32[]{:S(2)}) collective-permute-start(s16[128,4480]{1,0:T(8,128)(2,1)S(1)} %next.9.refs_3_), channel_id=1, source_target_pairs={{1,0},{2,1},{3,2},{4,5},{5,6},{6,7},{9,8},{10,9},{11,10},{12,13},{... | collective-permute-start | bytes 3440648 | tf_op jit(solution)/shard_map/ppermute | solution.py:512
  68.2 9.0 %partials.3.refs_1_.refs_3_.refs_0_ = f32[2,128,4352]{2,1,0:T(8,128)S(1)} custom-call(bf16[4,2,64,2048]{3,2,1,0:T(8,128)(2,1)S(1)} %arrange.1.m_ref.refs_0_, bf16[3328,2048]{1,0:T(8,128)(2,1)} %refs_1_.2, bf16[1024,2048]{1,0:T(8,128)(2,1)S(1)} %copy-done, s16[128,4480]{1,0:T(8,128)(2,1)S(1)} %next.9.refs_3_), custom_call_target="tpu_custom_call" | custom-call | flops 1200000000 | bytes 4000000 | tf_op jit(solution)/shard_map/partials/pallas_call | solution.py:42
  77.2 0.7 gram.1.refs_0_
  77.9 10.6 %collective-permute-done.11.refs_2_.refs_5_ = s16[128,4480]{1,0:T(8,128)(2,1)S(1)} collective-permute-done((s16[128,4480]{1,0:T(8,128)(2,1)S(1)}, s16[128,4480]{1,0:T(8,128)(2,1)S(1)}, u32[]{:S(2)}, u32[]{:S(2)}) %collective-permute-start.11) | collective-permute-done | bytes 1146912 | tf_op jit(solution)/shard_map/ppermute | solution.py:512
  88.6 2.6 %next.10.refs_3_ = s16[128,4480]{1,0:T(8,128)(2,1)S(1)} custom-call(f32[2,128,4352]{2,1,0:T(8,128)S(1)} %partials.2.refs_0_, f32[2,128,4352]{2,1,0:T(8,128)S(1)} %partials.3.refs_1_.refs_3_.refs_0_, s16[128,4480]{1,0:T(8,128)(2,1)S(1)} %collective-permute-done.11.refs_2_.refs_5_, f32[2,128,4352]{2,1,0:T(8,128)S(1)} %partials.3.refs_1_.refs_3_.refs_0_), custom_call_target="tpu_custom_call" | custom-call | flops 12000000000 | bytes 40000000 | tf_op jit(solution)/shard_map/next/pallas_call | solution.py:42
  91.2 4.6 %collective-permute-start.17 = (s16[128,4480]{1,0:T(8,128)(2,1)S(1)}, s16[128,4480]{1,0:T(8,128)(2,1)S(1)}, u32[]{:S(2)}, u32[]{:S(2)}) collective-permute-start(s16[128,4480]{1,0:T(8,128)(2,1)S(1)} %next.10.refs_3_), channel_id=1, source_target_pairs={{0,1},{1,2},{2,3},{5,4},{6,5},{7,6},{8,9},{9,10},{10,11},{13,12},{... | collective-permute-start | bytes 3440648 | tf_op jit(solution)/shard_map/ppermute | solution.py:512
  95.9 1.3 next.11.refs_9_
  97.2 0.2 copy-done.2
  97.5 6.8 %join.1 = (bf16[2,256,4352]{2,1,0:T(8,128)(2,1)S(1)}, f32[8,128]{1,0:T(8,128)S(1)}) custom-call(f32[2,256,256]{2,1,0:T(8,128)S(1)} %gram.1.refs_0_, bf16[2,64,3328]{2,1,0:T(8,128)(2,1)S(1)} %copy-done.4, bf16[2,64,1024]{2,1,0:T(8,128)(2,1)S(1)} %copy-done.7, s16[128,4480]{1,0:T(8,128)(2,1)S(1)} %collective-permute-done.8.refs_1_.refs_3_, ...), custom_call_target="tpu_custom_call" | custom-call | flops 4800000000 | bytes 16000000 | tf_op jit(solution)/shard_map/join/pallas_call | solution.py:42
  104.2 0.1 collective-permute-start.13
  104.3 1.2 collective-permute-done.13
  105.4 1.5 %collective-permute-start.16 = (f32[8,128]{1,0:T(8,128)S(1)}, f32[8,128]{1,0:T(8,128)S(1)}, u32[]{:S(2)}, u32[]{:S(2)}) collective-permute-start(f32[8,128]{1,0:T(8,128)S(1)} %add.26), channel_id=1, source_target_pairs={{0,24},{4,28},{8,16},{12,20},{16,8},{20,12},{24,0},{28,4},{1,25},{... | collective-permute-start | bytes 12296 | tf_op jit(solution)/shard_map/ppermute | solution.py:456
  107.0 1.4 %collective-permute-start.15 = (f32[8,128]{1,0:T(8,128)S(1)}, f32[8,128]{1,0:T(8,128)S(1)}, u32[]{:S(2)}, u32[]{:S(2)}) collective-permute-start(f32[8,128]{1,0:T(8,128)S(1)} %add.26), channel_id=1, source_target_pairs={{0,16},{4,20},{8,24},{12,28},{16,0},{20,4},{24,8},{28,12},{1,17},{... | collective-permute-start | bytes 12296 | tf_op jit(solution)/shard_map/ppermute | solution.py:456
  108.4 0.5 collective-permute-start.14
  108.9 1.0 collective-permute-done.16
  110.0 0.6 collective-permute-done.15
  110.6 1.4 %collective-permute-done.14 = f32[8,128]{1,0:T(8,128)S(1)} collective-permute-done((f32[8,128]{1,0:T(8,128)S(1)}, f32[8,128]{1,0:T(8,128)S(1)}, u32[]{:S(2)}, u32[]{:S(2)}) %collective-permute-start.14) | collective-permute-done | bytes 4128 | tf_op jit(solution)/shard_map/ppermute | solution.py:456
  112.0 0.9 collective-permute-start.20
  112.9 2.9 %collective-permute-start.19 = (f32[8,128]{1,0:T(8,128)S(1)}, f32[8,128]{1,0:T(8,128)S(1)}, u32[]{:S(2)}, u32[]{:S(2)}) collective-permute-start(f32[8,128]{1,0:T(8,128)S(1)} %add_add_fusion.1), channel_id=1, source_target_pairs={{0,2},{1,3},{2,0},{3,1},{4,6},{5,7},{6,4},{7,5},{8,10},{9,11},{10,... | collective-permute-start | bytes 12296 | tf_op jit(solution)/shard_map/ppermute | solution.py:456
  115.7 0.7 collective-permute-start.18
  116.5 1.3 collective-permute-start.21
  117.8 1.6 %collective-permute-done.18 = f32[8,128]{1,0:T(8,128)S(1)} collective-permute-done((f32[8,128]{1,0:T(8,128)S(1)}, f32[8,128]{1,0:T(8,128)S(1)}, u32[]{:S(2)}, u32[]{:S(2)}) %collective-permute-start.18) | collective-permute-done | bytes 4128 | tf_op jit(solution)/shard_map/ppermute | solution.py:456
  119.4 15.0 %weights.1 = (f32[3328,2048]{1,0:T(8,128)}, f32[1024,2048]{1,0:T(8,128)}) custom-call(f32[2,2]{1,0:T(2,128)S(1)} %pad_maximum_fusion.factor.refs_3_, bf16[4,2,64,2048]{3,2,1,0:T(8,128)(2,1)S(1)} %arrange.1.m_ref.refs_0_, bf16[2,256,4352]{2,1,0:T(8,128)(2,1)S(1)} %get-tuple-element.31.refs_0_), custom_call_target="tpu_custom_call" | custom-call | flops 14400000000 | bytes 48000000 | tf_op jit(solution)/shard_map/weights/pallas_call | solution.py:489
  134.4 2.2 %finish.1 = (bf16[2,64,3328]{2,1,0:T(8,128)(2,1)}, bf16[2,64,1024]{2,1,0:T(8,128)(2,1)}) custom-call(f32[2,128,4352]{2,1,0:T(8,128)S(1)} %partials.3.refs_1_.refs_3_.refs_0_, s16[128,4480]{1,0:T(8,128)(2,1)S(1)} %collective-permute-done.17.refs_1_, s16[128,4480]{1,0:T(8,128)(2,1)S(1)} %collective-permute-done.21.refs_2_, ...), custom_call_target="tpu_custom_call" | custom-call | flops 2400000000 | bytes 8000000 | tf_op jit(solution)/shard_map/finish/pallas_call | solution.py:42
  (34 shorter events, 0.1 us)
Async XLA Ops:
  0.6 1.2 copy-start.3
  1.8 0.9 copy-start.6
  2.7 6.1 %copy-start.5 = (bf16[2,32,2048]{2,1,0:T(8,128)(2,1)S(1)}, bf16[2,32,2048]{2,1,0:T(8,128)(2,1)}, u32[]{:S(2)}) copy-start(bf16[2,32,2048]{2,1,0:T(8,128)(2,1)} %refs_0_.1) | copy-start | bytes 786436
  2.7 20.9 %copy-start.8 = (s32[2,2]{1,0:T(2,128)S(1)}, s32[2,2]{1,0:T(2,128)}, u32[]{:S(2)}) copy-start(s32[2,2]{1,0:T(2,128)} %spans.1) | copy-start | bytes 52
  3.6 21.1 %copy-start = (bf16[1024,2048]{1,0:T(8,128)(2,1)S(1)}, bf16[1024,2048]{1,0:T(8,128)(2,1)}, u32[]{:S(2)}) copy-start(bf16[1024,2048]{1,0:T(8,128)(2,1)} %refs_2_.2) | copy-start | bytes 12582916
  3.6 30.1 %collective-permute-start.8 = (s16[128,4480]{1,0:T(8,128)(2,1)S(1)}, s16[128,4480]{1,0:T(8,128)(2,1)S(1)}, u32[]{:S(2)}, u32[]{:S(2)}) collective-permute-start(s16[128,4480]{1,0:T(8,128)(2,1)S(1)} %code.1), channel_id=1, source_target_pairs={{0,1},{1,2},{2,3},{5,4},{6,5},{7,6},{8,9},{9,10},{10,11},{13,12},{... | collective-permute-start | bytes 3440648 | tf_op jit(solution)/shard_map/ppermute | solution.py:512
  8.8 9.5 %collective-permute-start.5 = (bf16[2,32,2048]{2,1,0:T(8,128)(2,1)S(1)}, bf16[2,32,2048]{2,1,0:T(8,128)(2,1)S(1)}, u32[]{:S(2)}, u32[]{:S(2)}) collective-permute-start(bf16[2,32,2048]{2,1,0:T(8,128)(2,1)S(1)} %copy-done.5), channel_id=1, source_target_pairs={{0,24},{4,28},{8,16},{12,20},{16,8},{20,12},{24,0},{28,4},{1,25},{... | collective-permute-start | bytes 786440 | tf_op jit(solution)/shard_map/ppermute | solution.py:199
  11.4 9.7 %collective-permute-start.3 = (bf16[2,32,2048]{2,1,0:T(8,128)(2,1)S(1)}, bf16[2,32,2048]{2,1,0:T(8,128)(2,1)S(1)}, u32[]{:S(2)}, u32[]{:S(2)}) collective-permute-start(bf16[2,32,2048]{2,1,0:T(8,128)(2,1)S(1)} %copy-done.5), channel_id=1, source_target_pairs={{0,16},{4,20},{8,24},{12,28},{16,0},{20,4},{24,8},{28,12},{1,17},{... | collective-permute-start | bytes 786440 | tf_op jit(solution)/shard_map/ppermute | solution.py:199
  11.9 9.4 %collective-permute-start.1 = (bf16[2,32,2048]{2,1,0:T(8,128)(2,1)S(1)}, bf16[2,32,2048]{2,1,0:T(8,128)(2,1)S(1)}, u32[]{:S(2)}, u32[]{:S(2)}) collective-permute-start(bf16[2,32,2048]{2,1,0:T(8,128)(2,1)S(1)} %copy-done.5), channel_id=1, source_target_pairs={{0,8},{4,12},{8,0},{12,4},{16,24},{20,28},{24,16},{28,20},{1,9},{5... | collective-permute-start | bytes 786440 | tf_op jit(solution)/shard_map/ppermute | solution.py:199
  12.4 9.4 %collective-permute-start = (bf16[2,32,2048]{2,1,0:T(8,128)(2,1)S(1)}, bf16[2,32,2048]{2,1,0:T(8,128)(2,1)S(1)}, u32[]{:S(2)}, u32[]{:S(2)}) collective-permute-start(bf16[2,32,2048]{2,1,0:T(8,128)(2,1)S(1)} %copy-done.5), channel_id=1, source_target_pairs={{0,4},{4,0},{8,12},{12,8},{16,20},{20,16},{24,28},{28,24},{1,5},{5... | collective-permute-start | bytes 786440 | tf_op jit(solution)/shard_map/ppermute | solution.py:205
  21.3 1.8 %collective-permute-start.2 = (bf16[2,32,2048]{2,1,0:T(8,128)(2,1)S(1)}, bf16[2,32,2048]{2,1,0:T(8,128)(2,1)S(1)}, u32[]{:S(2)}, u32[]{:S(2)}) collective-permute-start(bf16[2,32,2048]{2,1,0:T(8,128)(2,1)S(1)} %collective-permute-done.1.refs_2_), channel_id=1, source_target_pairs={{0,4},{4,0},{8,12},{12,8},{16,20},{20,16},{24,28},{28,24},{1,5},{5... | collective-permute-start | bytes 786440 | tf_op jit(solution)/shard_map/ppermute | solution.py:205
  21.3 1.9 %collective-permute-start.4 = (bf16[2,32,2048]{2,1,0:T(8,128)(2,1)S(1)}, bf16[2,32,2048]{2,1,0:T(8,128)(2,1)S(1)}, u32[]{:S(2)}, u32[]{:S(2)}) collective-permute-start(bf16[2,32,2048]{2,1,0:T(8,128)(2,1)S(1)} %collective-permute-done.3.refs_4_), channel_id=1, source_target_pairs={{0,4},{4,0},{8,12},{12,8},{16,20},{20,16},{24,28},{28,24},{1,5},{5... | collective-permute-start | bytes 786440 | tf_op jit(solution)/shard_map/ppermute | solution.py:205
  21.8 1.8 %collective-permute-start.6 = (bf16[2,32,2048]{2,1,0:T(8,128)(2,1)S(1)}, bf16[2,32,2048]{2,1,0:T(8,128)(2,1)S(1)}, u32[]{:S(2)}, u32[]{:S(2)}) collective-permute-start(bf16[2,32,2048]{2,1,0:T(8,128)(2,1)S(1)} %collective-permute-done.5.refs_6_), channel_id=1, source_target_pairs={{0,4},{4,0},{8,12},{12,8},{16,20},{20,16},{24,28},{28,24},{1,5},{5... | collective-permute-start | bytes 786440 | tf_op jit(solution)/shard_map/ppermute | solution.py:205
  21.8 18.1 %collective-permute-start.7 = (s16[128,4480]{1,0:T(8,128)(2,1)S(1)}, s16[128,4480]{1,0:T(8,128)(2,1)S(1)}, u32[]{:S(2)}, u32[]{:S(2)}) collective-permute-start(s16[128,4480]{1,0:T(8,128)(2,1)S(1)} %code.1), channel_id=1, source_target_pairs={{1,0},{2,1},{3,2},{4,5},{5,6},{6,7},{9,8},{10,9},{11,10},{12,13},{... | collective-permute-start | bytes 3440648 | tf_op jit(solution)/shard_map/ppermute | solution.py:512
  36.3 23.2 %collective-permute-start.10 = (s16[128,4480]{1,0:T(8,128)(2,1)S(1)}, s16[128,4480]{1,0:T(8,128)(2,1)S(1)}, u32[]{:S(2)}, u32[]{:S(2)}) collective-permute-start(s16[128,4480]{1,0:T(8,128)(2,1)S(1)} %next.6.refs_2_), channel_id=1, source_target_pairs={{0,1},{1,2},{2,3},{5,4},{6,5},{7,6},{8,9},{9,10},{10,11},{13,12},{... | collective-permute-start | bytes 3440648 | tf_op jit(solution)/shard_map/ppermute | solution.py:512
  39.9 26.7 %collective-permute-start.9 = (s16[128,4480]{1,0:T(8,128)(2,1)S(1)}, s16[128,4480]{1,0:T(8,128)(2,1)S(1)}, u32[]{:S(2)}, u32[]{:S(2)}) collective-permute-start(s16[128,4480]{1,0:T(8,128)(2,1)S(1)} %next.7.refs_2_), channel_id=1, source_target_pairs={{1,0},{2,1},{3,2},{4,5},{5,6},{6,7},{9,8},{10,9},{11,10},{12,13},{... | collective-permute-start | bytes 3440648 | tf_op jit(solution)/shard_map/ppermute | solution.py:512
  62.2 26.4 %collective-permute-start.11 = (s16[128,4480]{1,0:T(8,128)(2,1)S(1)}, s16[128,4480]{1,0:T(8,128)(2,1)S(1)}, u32[]{:S(2)}, u32[]{:S(2)}) collective-permute-start(s16[128,4480]{1,0:T(8,128)(2,1)S(1)} %next.8.refs_2_), channel_id=1, source_target_pairs={{0,1},{1,2},{2,3},{5,4},{6,5},{7,6},{8,9},{9,10},{10,11},{13,12},{... | collective-permute-start | bytes 3440648 | tf_op jit(solution)/shard_map/ppermute | solution.py:512
  66.7 29.1 %collective-permute-start.12 = (s16[128,4480]{1,0:T(8,128)(2,1)S(1)}, s16[128,4480]{1,0:T(8,128)(2,1)}, u32[]{:S(2)}, u32[]{:S(2)}) collective-permute-start(s16[128,4480]{1,0:T(8,128)(2,1)S(1)} %next.9.refs_3_), channel_id=1, source_target_pairs={{1,0},{2,1},{3,2},{4,5},{5,6},{6,7},{9,8},{10,9},{11,10},{12,13},{... | collective-permute-start | bytes 3440648 | tf_op jit(solution)/shard_map/ppermute | solution.py:512
  88.6 2.6 %copy-start.1 = (s16[128,4480]{1,0:T(8,128)(2,1)}, s16[128,4480]{1,0:T(8,128)(2,1)S(1)}, u32[]{:S(2)}) copy-start(s16[128,4480]{1,0:T(8,128)(2,1)S(1)} %collective-permute-done.11.refs_2_.refs_5_) | copy-start | bytes 3440644
  91.2 6.0 %copy-start.4 = (bf16[2,64,3328]{2,1,0:T(8,128)(2,1)S(1)}, bf16[2,64,3328]{2,1,0:T(8,128)(2,1)}, u32[]{:S(2)}) copy-start(bf16[2,64,3328]{2,1,0:T(8,128)(2,1)} %refs_1_.3) | copy-start | bytes 2555908
  91.2 6.0 %copy-start.7 = (bf16[2,64,1024]{2,1,0:T(8,128)(2,1)S(1)}, bf16[2,64,1024]{2,1,0:T(8,128)(2,1)}, u32[]{:S(2)}) copy-start(bf16[2,64,1024]{2,1,0:T(8,128)(2,1)} %refs_2_.3) | copy-start | bytes 786436
  91.2 20.8 %collective-permute-start.17 = (s16[128,4480]{1,0:T(8,128)(2,1)S(1)}, s16[128,4480]{1,0:T(8,128)(2,1)S(1)}, u32[]{:S(2)}, u32[]{:S(2)}) collective-permute-start(s16[128,4480]{1,0:T(8,128)(2,1)S(1)} %next.10.refs_3_), channel_id=1, source_target_pairs={{0,1},{1,2},{2,3},{5,4},{6,5},{7,6},{8,9},{9,10},{10,11},{13,12},{... | collective-permute-start | bytes 3440648 | tf_op jit(solution)/shard_map/ppermute | solution.py:512
  95.8 1.6 %copy-start.2 = (s16[128,4480]{1,0:T(8,128)(2,1)S(1)}, s16[128,4480]{1,0:T(8,128)(2,1)}, u32[]{:S(2)}) copy-start(s16[128,4480]{1,0:T(8,128)(2,1)} %copy-done.1) | copy-start | bytes 3440644
  104.2 1.2 collective-permute-start.13
  105.4 4.5 %collective-permute-start.16 = (f32[8,128]{1,0:T(8,128)S(1)}, f32[8,128]{1,0:T(8,128)S(1)}, u32[]{:S(2)}, u32[]{:S(2)}) collective-permute-start(f32[8,128]{1,0:T(8,128)S(1)} %add.26), channel_id=1, source_target_pairs={{0,24},{4,28},{8,16},{12,20},{16,8},{20,12},{24,0},{28,4},{1,25},{... | collective-permute-start | bytes 12296 | tf_op jit(solution)/shard_map/ppermute | solution.py:456
  107.0 3.6 %collective-permute-start.15 = (f32[8,128]{1,0:T(8,128)S(1)}, f32[8,128]{1,0:T(8,128)S(1)}, u32[]{:S(2)}, u32[]{:S(2)}) collective-permute-start(f32[8,128]{1,0:T(8,128)S(1)} %add.26), channel_id=1, source_target_pairs={{0,16},{4,20},{8,24},{12,28},{16,0},{20,4},{24,8},{28,12},{1,17},{... | collective-permute-start | bytes 12296 | tf_op jit(solution)/shard_map/ppermute | solution.py:456
  108.4 3.6 %collective-permute-start.14 = (f32[8,128]{1,0:T(8,128)S(1)}, f32[8,128]{1,0:T(8,128)S(1)}, u32[]{:S(2)}, u32[]{:S(2)}) collective-permute-start(f32[8,128]{1,0:T(8,128)S(1)} %add.26), channel_id=1, source_target_pairs={{0,8},{4,12},{8,0},{12,4},{16,24},{20,28},{24,16},{28,20},{1,9},{5... | collective-permute-start | bytes 12296 | tf_op jit(solution)/shard_map/ppermute | solution.py:456
  112.0 5.7 %collective-permute-start.20 = (f32[8,128]{1,0:T(8,128)S(1)}, f32[8,128]{1,0:T(8,128)S(1)}, u32[]{:S(2)}, u32[]{:S(2)}) collective-permute-start(f32[8,128]{1,0:T(8,128)S(1)} %add_add_fusion.1), channel_id=1, source_target_pairs={{0,3},{1,2},{2,1},{3,0},{4,7},{5,6},{6,5},{7,4},{8,11},{9,10},{10,... | collective-permute-start | bytes 12296 | tf_op jit(solution)/shard_map/ppermute | solution.py:456
  112.9 4.9 %collective-permute-start.19 = (f32[8,128]{1,0:T(8,128)S(1)}, f32[8,128]{1,0:T(8,128)S(1)}, u32[]{:S(2)}, u32[]{:S(2)}) collective-permute-start(f32[8,128]{1,0:T(8,128)S(1)} %add_add_fusion.1), channel_id=1, source_target_pairs={{0,2},{1,3},{2,0},{3,1},{4,6},{5,7},{6,4},{7,5},{8,10},{9,11},{10,... | collective-permute-start | bytes 12296 | tf_op jit(solution)/shard_map/ppermute | solution.py:456
  115.7 3.6 %collective-permute-start.18 = (f32[8,128]{1,0:T(8,128)S(1)}, f32[8,128]{1,0:T(8,128)S(1)}, u32[]{:S(2)}, u32[]{:S(2)}) collective-permute-start(f32[8,128]{1,0:T(8,128)S(1)} %add_add_fusion.1), channel_id=1, source_target_pairs={{0,1},{1,0},{2,3},{3,2},{4,5},{5,4},{6,7},{7,6},{8,9},{9,8},{10,11... | collective-permute-start | bytes 12296 | tf_op jit(solution)/shard_map/ppermute | solution.py:456
  116.5 17.9 %collective-permute-start.21 = (s16[128,4480]{1,0:T(8,128)(2,1)S(1)}, s16[128,4480]{1,0:T(8,128)(2,1)S(1)}, u32[]{:S(2)}, u32[]{:S(2)}) collective-permute-start(s16[128,4480]{1,0:T(8,128)(2,1)S(1)} %next.11.refs_9_), channel_id=1, source_target_pairs={{1,0},{2,1},{3,2},{4,5},{5,6},{6,7},{9,8},{10,9},{11,10},{12,13},{... | collective-permute-start | bytes 3440648 | tf_op jit(solution)/shard_map/ppermute | solution.py:512

commit v3 on v2

--- a/solution.py
+++ b/solution.py
@@ -14,12 +14,11 @@
 BF16 = jnp.bfloat16
 I16 = jnp.int16
 LANES = 128
-LIMIT = 32 * 1024 * 1024
-
-
-def params(grid_dims):
+
+
+def params(grid_dims, mebibytes):
     return pltpu.CompilerParams(
-        dimension_semantics=("arbitrary",) * grid_dims, vmem_limit_bytes=LIMIT
+        dimension_semantics=("arbitrary",) * grid_dims, vmem_limit_bytes=mebibytes * 2**20
     )
 
 
@@ -132,7 +131,7 @@
         out_shape=jax.ShapeDtypeStruct((rows, chunk.message), I16),
         out_specs=pl.BlockSpec(memory_space=VMEM),
         compiler_params=pltpu.CompilerParams(vmem_limit_bytes=16 * 2**20),
-        cost_estimate=cost(4e6),
+        cost_estimate=cost(20e6),
         name="code",
     )
 
@@ -179,8 +178,8 @@
         in_specs=[pl.BlockSpec(memory_space=pltpu.SMEM)]
         + [pl.BlockSpec(memory_space=VMEM)] * len(pieces),
         out_specs=pl.BlockSpec(memory_space=VMEM),
-        compiler_params=pltpu.CompilerParams(vmem_limit_bytes=LIMIT),
-        cost_estimate=cost(4e6),
+        compiler_params=pltpu.CompilerParams(vmem_limit_bytes=12 * 2**20),
+        cost_estimate=cost(20e6),
         name="arrange",
     )(spans, *pieces)
 
@@ -206,32 +205,40 @@
     return pieces
 
 
+PIECE = 512
+RING = 4
+
+
 def pieces_of(size):
-    cut = (size // LANES + 1) // 2 * LANES if size > 1024 else size
-    return [(0, cut)] + ([(cut, size - cut)] if cut < size else [])
+    return [(start, min(PIECE, size - start)) for start in range(0, size, PIECE)]
 
 
 def partial_kernel(plan, ks, m_ref, wa, wb, out, held, sems):
     weights = (wa, wb)
-    copies = []
-    for number, (which, source, start, size) in enumerate(plan):
-        copy = pltpu.make_async_copy(
-            weights[which].at[pl.ds(source, size)], held.at[pl.ds(start, size)], sems.at[number]
+
+    def copy(number):
+        which, source, _, size = plan[number]
+        slot = number % RING
+        return pltpu.make_async_copy(
+            weights[which].at[pl.ds(source, size)], held.at[slot, pl.ds(0, size)], sems.at[slot]
         )
-        copy.start()
-        copies.append(copy)
+
+    for number in range(min(RING, len(plan))):
+        copy(number).start()
     rows = out.shape[1]
     p = place(m_ref.shape[0])
     masked = jnp.concatenate(
         [m_ref[pl.ds(k(p), 1)].reshape(rows, m_ref.shape[-1]) for k in ks], axis=0
     )
-    for copy, (_, _, start, size) in zip(copies, plan):
-        copy.wait()
+    for number, (_, _, start, size) in enumerate(plan):
+        copy(number).wait()
         value = lax.dot_general(
-            masked, held[pl.ds(start, size)], NT, preferred_element_type=F32
+            masked, held[number % RING, pl.ds(0, size)], NT, preferred_element_type=F32
         )
         for n in range(len(ks)):
             out[n, :, start : start + size] = value[n * rows : (n + 1) * rows]
+        if number + RING < len(plan):
+            copy(number + RING).start()
 
 
 def partials(chunk, masked, ks, wa, wb, bytes_accessed, deps=()):
@@ -245,22 +252,21 @@
     return call(
         functools.partial(partial_kernel, plan, ks),
         (masked, wa, wb),
-        [pl.BlockSpec(memory_space=VMEM)] + [pl.BlockSpec(memory_space=pl.ANY)] * 2,
+        [pl.BlockSpec(memory_space=VMEM)] + [pl.BlockSpec(memory_space=pltpu.HBM)] * 2,
         deps,
         out_shape=jax.ShapeDtypeStruct((len(ks), rows, chunk.width), F32),
         out_specs=pl.BlockSpec(memory_space=VMEM),
         scratch_shapes=[
-            pltpu.VMEM((chunk.width, width), BF16),
-            pltpu.SemaphoreType.DMA((len(plan),)),
+            pltpu.VMEM((RING, PIECE, width), BF16),
+            pltpu.SemaphoreType.DMA((RING,)),
         ],
-        compiler_params=pltpu.CompilerParams(vmem_limit_bytes=40 * 2**20),
+        compiler_params=pltpu.CompilerParams(vmem_limit_bytes=26 * 2**20),
         cost_estimate=cost(bytes_accessed),
         name="partials",
     )
 
 
 STEPS = 2
-FIRST = 4e6
 ROWS = 16
 
 
@@ -313,7 +319,7 @@
     rows = came.shape[0]
     step = rows // STEPS
     k = s if flow == 0 else n - s
-    keys = [("first", 0 if k in (1, n - 1) else k - 1)]
+    keys = [("first", 0) if k in (1, n - 1) else ("second", k)]
     if s == n - 1 and s > 1:
         keys.append(("second", 0))
     message = pl.BlockSpec((step, chunk.message), lambda i: (i, 0))
@@ -326,9 +332,27 @@
         grid=(STEPS,),
         out_shape=jax.ShapeDtypeStruct(came.shape, I16),
         out_specs=message,
-        compiler_params=params(1),
+        compiler_params=params(1, 12),
+        cost_estimate=cost(40e6 if s < n - 1 else 1e6 if flow == 0 else 100e6),
+        name="next",
+    )
+
+
+def wait_kernel(out):
+    out[...] = jnp.zeros(out.shape, F32)
+
+
+def wait_for(deps):
+    return call(
+        wait_kernel,
+        [],
+        [],
+        deps,
+        out_shape=jax.ShapeDtypeStruct((8, LANES), F32),
+        out_specs=pl.BlockSpec(memory_space=VMEM),
+        compiler_params=pltpu.CompilerParams(vmem_limit_bytes=2**20),
         cost_estimate=cost(40e6),
-        name="next",
+        name="wait",
     )
 
 
@@ -360,8 +384,8 @@
         grid=(2 * examples,),
         out_shape=[jax.ShapeDtypeStruct((examples, local, w), BF16) for w in widths],
         out_specs=[pl.BlockSpec((1, half, w), lambda i: (i // 2, i % 2, 0)) for w in widths],
-        compiler_params=params(1),
-        cost_estimate=cost(8e6),
+        compiler_params=params(1, 12),
+        cost_estimate=cost(1e6),
         name="finish",
     )
 
@@ -369,11 +393,16 @@
 NT = (((1,), (1,)), ((), ()))
 
 
-def gram_kernel(m_ref, out):
+def gram_kernel(m_ref, out, mine):
+    core = lax.axis_index("row") % 2
     for b in range(out.shape[0]):
         masked = m_ref[:, b].reshape(out.shape[1], m_ref.shape[-1])
         out[b] = lax.dot_general(masked, masked, NT, preferred_element_type=F32)
 
+        @pl.when(core == b % 2)
+        def _():
+            mine[b // 2] = out[b]
+
 
 def gram(masked, deps=()):
     col_count, examples, local, width = masked.shape
@@ -383,16 +412,43 @@
         (masked,),
         [pl.BlockSpec(memory_space=VMEM)],
         deps,
-        out_shape=jax.ShapeDtypeStruct((examples, length, length), F32),
-        out_specs=pl.BlockSpec(memory_space=VMEM),
+        out_shape=[
+            jax.ShapeDtypeStruct((count, length, length), F32) for count in (examples, examples // 2)
+        ],
+        out_specs=[pl.BlockSpec(memory_space=VMEM)] * 2,
         compiler_params=pltpu.CompilerParams(vmem_limit_bytes=16 * 2**20),
-        cost_estimate=cost(3e6),
+        cost_estimate=cost(20e6),
         name="gram",
     )
 
 
-def join_kernel(chunk, n, gram_ref, hidden, context, *refs):
-    rights, lefts = refs[: n - 1], refs[n - 1 : 2 * n - 2]
+def take(chunk, message, put, examples, local):
+    for b in range(examples):
+
+        def one(i, carry):
+            start = pl.multiple_of(i * ROWS, ROWS)
+            value = decoder(chunk, message, b * local + start, ROWS)
+            for column in range(0, chunk.width, LANES):
+                put(b, start, column, value(column).astype(BF16))
+            return carry
+
+        lax.fori_loop(0, local // ROWS, one, 0)
+
+
+def turned(x, shift):
+    x = jnp.concatenate([x[-shift:], x[:-shift]], axis=0)
+    return pltpu.roll(x, shift, 1)
+
+
+def mirrored(x, local, first):
+    order = [(first - j) % 4 * local for j in range(4)]
+    x = jnp.concatenate([x[at : at + local] for at in order], axis=0)
+    halves = [pltpu.roll(h, local, 1) for h in (x[:, : 2 * local], x[:, 2 * local :])]
+    return jnp.concatenate(halves if first == 1 else halves[::-1], axis=1)
+
+
+def join_kernel(chunk, n, slots, early, gram_ref, came, came_to_other, hidden, context, *refs):
+    firsts, seconds = refs[:slots], refs[slots : 2 * slots]
     joined, out = refs[-2:]
     p = place(n)
     arrays = (hidden, context)
@@ -400,53 +456,60 @@
     for column, which, at in chunk.places():
         joined[:, :local, column : column + LANES] = arrays[which][:, :, at : at + LANES]
 
-    def take(k, message):
+    for k in range(1, n):
+
+        def put(b, row, column, value):
+            joined[b, pl.ds(k * local + row, ROWS), column : column + LANES] = value
+
+        if k - 1 < slots:
+
+            @pl.when(p >= k)
+            def _():
+                take(chunk, firsts[k - 1], put, examples, local)
+
+        if n - k - 1 < slots:
+
+            @pl.when(p < k)
+            def _():
+                take(chunk, seconds[n - k - 1], put, examples, local)
+
+    lane = lax.broadcasted_iota(jnp.int32, out.shape, 1)
+    out[...] = jnp.zeros(out.shape, F32)
+
+    def norm(came_from):
+        total = jnp.zeros(out.shape, F32)
         for b in range(examples):
-
-            def one(i, carry):
-                start = pl.multiple_of(i * ROWS, ROWS)
-                value = decoder(chunk, message, b * local + start, ROWS)
-                for column in range(0, chunk.width, LANES):
-                    joined[b, pl.ds(k * local + start, ROWS), column : column + LANES] = value(
-                        column
-                    ).astype(BF16)
-                return carry
-
-            lax.fori_loop(0, local // ROWS, one, 0)
-
-    for k in range(1, n):
-
-        @pl.when(p >= k)
-        def _():
-            take(k, rights[k - 1])
-
-        @pl.when(p < k)
-        def _():
-            take(k, lefts[n - k - 1])
-
-    lane = lax.broadcasted_iota(jnp.int32, out.shape, 1)
-    total = jnp.zeros(out.shape, F32)
-    for b in range(examples):
-        feature = joined[b]
-        feature_gram = lax.dot_general(feature, feature, NT, preferred_element_type=F32)
-        total = jnp.where(lane == b, jnp.sum(feature_gram * gram_ref[b]), total)
-    out[...] = total
-
-
-def join(chunk, masked_gram, hidden, context, rights, lefts, deps=()):
-    n = len(rights) + 1
+            feature = joined[b]
+            feature_gram = lax.dot_general(feature, feature, NT, preferred_element_type=F32)
+            masked_gram = gram_ref[b]
+            if came_from:
+                shift, first = (local, 1) if came_from == 1 else ((n - 1) * local, 3)
+                mine = turned(came[b // 2], shift)
+                others = mirrored(came_to_other[b // 2], local, first)
+                masked_gram += jnp.where(lax.axis_index("row") % 2 == b % 2, mine, others)
+            total = jnp.where(lane == b, jnp.sum(feature_gram * masked_gram), total)
+        out[...] = total
+
+    if early:
+        pl.when(p == 1)(lambda: norm(1))
+        pl.when(p == 2)(lambda: norm(2))
+    else:
+        norm(0)
+
+
+def join(chunk, n, early, grams, hidden, context, firsts, seconds, deps=()):
     examples, local, _ = hidden.shape
-    arrays = [masked_gram, hidden, context, *rights, *lefts]
+    arrays = [*grams, hidden, context, *firsts, *seconds]
     shape = (examples, n * local, chunk.width)
     return call(
-        functools.partial(join_kernel, chunk, n),
+        functools.partial(join_kernel, chunk, n, len(firsts), early),
         arrays,
         [pl.BlockSpec(memory_space=VMEM)] * len(arrays),
         deps,
         out_shape=[jax.ShapeDtypeStruct(shape, BF16), jax.ShapeDtypeStruct((8, LANES), F32)],
         out_specs=[pl.BlockSpec(memory_space=VMEM)] * 2,
-        compiler_params=pltpu.CompilerParams(vmem_limit_bytes=24 * 2**20),
-        cost_estimate=cost(16e6),
+        compiler_params=pltpu.CompilerParams(vmem_limit_bytes=32 * 2**20),
+        cost_estimate=cost(1e6),
         name="join",
     )
 
@@ -460,46 +523,79 @@
     return x
 
 
-def weight_kernel(widths, factor, m_ref, *refs):
-    features, outs = refs[:-2], refs[-2:]
-    examples, length = features[0].shape[:2]
+def weight_kernel(chunk, widths, n, factor, m_ref, joined, *refs):
+    last, (token, *outs), (features, message, sems) = refs[:-6], refs[-6:-3], refs[-3:]
+    examples, length = features.shape[:2]
+    local = length // n
+    p = place(n)
+
+    @pl.when(pl.program_id(0) == 0)
+    def _():
+        copies = [
+            pltpu.make_async_copy(joined.at[b], features.at[b], sems.at[b]) for b in range(examples)
+        ]
+
+        def fill(source, k):
+            came = pltpu.make_async_copy(source, message, sems.at[examples])
+            came.start()
+            came.wait()
+
+            def put(b, row, column, value):
+                features[b, pl.ds(k * local + row, ROWS), column : column + LANES] = value
+
+            take(chunk, message, put, examples, local)
+
+        for copy in copies:
+            copy.start()
+        for copy in copies:
+            copy.wait()
+        if last:
+            pl.when(p == 0)(lambda: fill(last[1], 1))
+            pl.when(p == n - 1)(lambda: fill(last[0], n - 1))
+        token[...] = jnp.zeros(token.shape, F32)
+
     masked = [m_ref[:, b].reshape(length, m_ref.shape[-1]) for b in range(examples)]
-    column = 0
-    for x in features:
-        for start in range(0, x.shape[2], LANES):
-            out, at = (0, column) if column < widths[0] else (1, column - widths[0])
-            total = None
-            for b in range(examples):
-                each = lax.dot_general(
-                    x[b, :, start : start + LANES],
-                    masked[b],
-                    (((0,), (0,)), ((), ())),
-                    preferred_element_type=F32,
-                )
-                each = factor[out, b] * each
-                total = each if total is None else total + each
-            outs[out][at : at + LANES] = total
-            column += LANES
-
-
-def weight_grads(factor, masked, features, widths):
-    col_count, examples, local, width = masked.shape
+    for column in range(0, sum(widths), LANES):
+        out, at = (0, column) if column < widths[0] else (1, column - widths[0])
+        total = None
+        for b in range(examples):
+            each = lax.dot_general(
+                features[b, :, column : column + LANES],
+                masked[b],
+                (((0,), (0,)), ((), ())),
+                preferred_element_type=F32,
+            )
+            each = factor[out, b] * each
+            total = each if total is None else total + each
+        outs[out][at : at + LANES] = total
+
+
+def weight_grads(chunk, factor, masked, joined, last, widths, deps=()):
+    n, examples, local, width = masked.shape
     tile = min(256, width)
-    whole = lambda x: pl.BlockSpec(x.shape, lambda i: (0, 0, 0), pipeline_mode=pl.Buffered(1))
-    return pl.pallas_call(
-        functools.partial(weight_kernel, widths),
+    anywhere = pl.BlockSpec(memory_space=pl.ANY)
+    return call(
+        functools.partial(weight_kernel, chunk, widths, n),
+        [factor, masked, joined, *last],
+        [
+            pl.BlockSpec(memory_space=pltpu.SMEM),
+            pl.BlockSpec((n, examples, local, tile), lambda i: (0, 0, 0, i)),
+        ]
+        + [anywhere] * (1 + len(last)),
+        deps,
         grid=(width // tile,),
-        out_shape=[jax.ShapeDtypeStruct((w, width), F32) for w in widths],
-        in_specs=[
-            pl.BlockSpec(memory_space=pltpu.SMEM),
-            pl.BlockSpec((col_count, examples, local, tile), lambda i: (0, 0, 0, i)),
-        ]
-        + [whole(x) for x in features],
-        out_specs=[pl.BlockSpec((w, tile), lambda i: (0, i)) for w in widths],
-        compiler_params=params(1),
-        cost_estimate=cost(48e6),
+        out_shape=[jax.ShapeDtypeStruct((8, LANES), F32)]
+        + [jax.ShapeDtypeStruct((w, width), F32) for w in widths],
+        out_specs=[full((8, LANES))] + [pl.BlockSpec((w, tile), lambda i: (0, i)) for w in widths],
+        scratch_shapes=[
+            pltpu.VMEM(joined.shape, BF16),
+            pltpu.VMEM((examples * local, chunk.message), I16),
+            pltpu.SemaphoreType.DMA((examples + 1,)),
+        ],
+        compiler_params=params(1, 26),
+        cost_estimate=cost(1e6),
         name="weights",
-    )(factor, masked, *features)
+    )
 
 
 def body(row_count, col_count, scales, cotangent, hidden, context, wa, wb, spans):
@@ -515,33 +611,58 @@
     came = [[send(own, 0)], [send(own, 1)]]
     masked = arrange(gather_rows(cotangent, row_count, (own,)), spans, row_count, n)
 
+    early = n == 4
+    inward = [(row * n + a, row * n + b) for row in range(row_count) for a, b in ((0, 1), (3, 2))]
+    cores = [(i, i ^ 1) for i in range(row_count)]
+
+    def factors(sq_norm):
+        sq_norm = sum_over(sq_norm, "row", row_count, [[1], range(2, row_count, 2)])
+        sq_norm = sum_over(sq_norm, "col", n, [range(1, n)])
+        factor = 1.0 / (jnp.sqrt(sq_norm[0, :examples]) + GAMMA)
+        return jnp.stack([factor * scale for scale in scales])
+
     first_ks = [lambda p: jnp.where(p < n // 2, 1, n - 1)]
-    first_ks += [lambda p, k=k: k for k in range(2, n - 1)]
     second_ks = [lambda p: jnp.where(p < n // 2, n - 1, 1), lambda p: 0]
-    first = partials(chunk, masked, first_ks, wa, wb, FIRST)
-    second, latest = None, ()
+    second_ks += [lambda p, k=k: k for k in range(2, n - 1)]
+    first = partials(chunk, masked, first_ks, wa, wb, 4e6)
+    second, latest = first, ()
     for s in range(1, n):
-        if s == n - 1:
-            second = partials(chunk, masked, second_ks, wa, wb, 4e6, latest)
-            masked_gram = gram(masked, (second,))
-            latest = (second,)
+        if s == n - 1 and early:
+            joined, sq_norm = join(
+                chunk, n, True, grams, hidden, context, came[0][:2], came[1][:2], latest
+            )
+            factor = factors(sq_norm)
+            latest = (factor,)
         for flow in (0, 1):
             message = next_message(chunk, n, s, flow, first, second, came[flow][-1], latest)
             latest = (message,)
             came[flow].append(send(message, flow))
-
-    joined = [
-        join(chunk, masked_gram, hidden, context, came[0][:-1], came[1][:-1], latest)
-    ]
-    sq_norm = sum(j[1] for j in joined)
-    sq_norm = sum_over(sq_norm, "row", row_count, [[1], range(2, row_count, 2)])
-    sq_norm = after(sq_norm, came[0][-1])
-    sq_norm = sum_over(sq_norm, "col", n, [range(1, n)])
-    factor = 1.0 / (jnp.sqrt(sq_norm[0, :examples]) + GAMMA)
-    factor = jnp.stack([factor * scale for scale in scales])
-    down_grad, heads_grad = weight_grads(factor, masked, [j[0] for j in joined], widths)
+            if s == 1 and flow == 0:
+                masked_gram, mine = gram(masked, latest)
+                grams = [masked_gram, mine, mine]
+                if early:
+                    grams[1] = lax.ppermute(mine, ("row", "col"), inward)
+                latest = (masked_gram,)
+            if s == 2 and flow == 0 and early:
+                grams[2] = lax.ppermute(after(grams[1], message), "row", cores)
+        if s == 1:
+            second = partials(chunk, masked, second_ks, wa, wb, 4e6, latest)
+            latest = (second,)
+
+    if early:
+        last = [came[0][2], came[1][2]]
+    else:
+        last = []
+        joined, sq_norm = join(
+            chunk, n, False, grams, hidden, context, came[0][:-1], came[1][:-1], latest
+        )
+        factor = factors(sq_norm)
+    token, down_grad, heads_grad = weight_grads(
+        chunk, factor, masked, joined, last, widths, latest
+    )
+    token = wait_for((came[0][-1], token))
     hidden_grad, context_grad = finish(
-        [chunk], [second], 1, [came[0][-1]], [came[1][-1]], examples, widths, (factor,)
+        [chunk], [second], 1, [came[0][-1]], [came[1][-1]], examples, widths, (token,)
     )
     return down_grad, heads_grad, hidden_grad, context_grad
 

time: 137 us -> 132 us (0.964)
  waiting for transfers between devices: 45.7 us -> 20.9 us
  starting transfers between devices: 33.7 us -> 51.7 us
  local copies, waits for them, and re-layouts: 2.38 us -> 5.52 us
    ppermute x8, waiting for transfers between devices: 30.5 us -> 9.27 us  [send(): return lax.ppermute(x, ('row', 'col'), flow_pairs(n, row_count, flow))]
    pallas_call x1 -> x0, Pallas kernels: 15 us -> none  [weight_grads(): pl.pallas_call(functools.partial(weight_kernel, widths), grid=(width // t...]
    ppermute x0 -> x2, starting transfers between devices: none -> 14.1 us  [the longest x1 9.55 us: body(): grams[2] = lax.ppermute(after(grams[1], message), 'row', cores)]
    pallas_call x12 -> x14, Pallas kernels: 37.7 us -> 51.8 us  [call(): return pl.pallas_call(kernel, in_specs=specs, **rest)(*arrays, *deps)]
    ppermute x7, starting transfers between devices: 8.01 us -> 13.6 us  [sum_over(): lax.ppermute(x, axis, [(i, i ^ j) for i in range(count)])]
    ppermute x3, waiting for transfers between devices: 8.91 us -> 4.23 us  [gather_rows(): near.append(lax.ppermute(x, 'row', [(i, i ^ j) for i in range(row_count)]))]
    ppermute x8, starting transfers between devices: 21.7 us -> 18.4 us  [send(): return lax.ppermute(x, ('row', 'col'), flow_pairs(n, row_count, flow))]
    unnamed x18 -> x30, local copies, waits for them, and re-layouts: 2.38 us -> 5.52 us
  transfers between devices with their start and end apart: 22 -> 24, of which waited for: 13 -> 11; matrix products, arithmetic and copies ran while one was open for 0% -> 0% of each run, Pallas kernels for 37% -> 38%
where the time goes in v3:
time: 132 us
  Pallas kernels  52.9 us (40%)
  starting transfers between devices  51.7 us (39%)
  waiting for transfers between devices  20.9 us (16%)
  local copies, waits for them, and re-layouts  5.52 us (4%)
    pallas_call x14, Pallas kernels, call(): return pl.pallas_call(kernel, in_specs=specs, **rest)(*arrays, *deps)  51.8 us
    ppermute x8, starting transfers between devices, send(): return lax.ppermute(x, ('row', 'col'), flow_pairs(n, row_count, flow))  18.4 us
    ppermute x7, starting transfers between devices, sum_over(): lax.ppermute(x, axis, [(i, i ^ j) for i in range(count)])  13.6 us
    ppermute x1, starting transfers between devices, body(): grams[2] = lax.ppermute(after(grams[1], message), 'row', cores)  9.55 us
    ppermute x8, waiting for transfers between devices, send(): return lax.ppermute(x, ('row', 'col'), flow_pairs(n, row_count, flow))  9.27 us
    ppermute x7, waiting for transfers between devices, sum_over(): lax.ppermute(x, axis, [(i, i ^ j) for i in range(count)])  7.29 us
    unnamed x30, local copies, waits for them, and re-layouts  5.52 us
    ppermute x1, starting transfers between devices, body(): grams[1] = lax.ppermute(mine, ('row', 'col'), inward)  4.57 us
  transfers between devices with their start and end apart: 24, of which 11 were waited for; matrix products, arithmetic and copies ran while one was open for 0% of the time, Pallas kernels for 38%

profile of v3, /device:TPU:0, one launch (start us, length us, event | category | flops | bytes accessed | tf_op | source)
XLA Modules:
  0.0 132.0 jit_solution(6818409692421151630)
XLA Ops:
  0.6 3.0 %collective-permute-start.1 = (bf16[2,32,2048]{2,1,0:T(8,128)(2,1)}, bf16[2,32,2048]{2,1,0:T(8,128)(2,1)S(1)}, u32[]{:S(2)}, u32[]{:S(2)}) collective-permute-start(bf16[2,32,2048]{2,1,0:T(8,128)(2,1)} %refs_0_.1), channel_id=1, source_target_pairs={{0,8},{4,12},{8,0},{12,4},{16,24},{20,28},{24,16},{28,20},{1,9},{5... | collective-permute-start | bytes 786440 | tf_op jit(solution)/shard_map/ppermute | solution.py:198
  3.6 1.5 %collective-permute-start.3 = (bf16[2,32,2048]{2,1,0:T(8,128)(2,1)}, bf16[2,32,2048]{2,1,0:T(8,128)(2,1)S(1)}, u32[]{:S(2)}, u32[]{:S(2)}) collective-permute-start(bf16[2,32,2048]{2,1,0:T(8,128)(2,1)} %refs_0_.1), channel_id=1, source_target_pairs={{0,16},{4,20},{8,24},{12,28},{16,0},{20,4},{24,8},{28,12},{1,17},{... | collective-permute-start | bytes 786440 | tf_op jit(solution)/shard_map/ppermute | solution.py:198
  5.2 1.2 copy-done.3
  6.3 0.9 copy-done.7
  7.3 0.8 code.1
  8.1 4.3 %collective-permute-start.7 = (s16[128,4480]{1,0:T(8,128)(2,1)S(1)}, s16[128,4480]{1,0:T(8,128)(2,1)S(1)}, u32[]{:S(2)}, u32[]{:S(2)}) collective-permute-start(s16[128,4480]{1,0:T(8,128)(2,1)S(1)} %code.1), channel_id=1, source_target_pairs={{0,1},{1,2},{2,3},{5,4},{6,5},{7,6},{8,9},{9,10},{10,11},{13,12},{... | collective-permute-start | bytes 3440648 | tf_op jit(solution)/shard_map/ppermute | solution.py:608
  12.5 0.5 collective-permute-start.2
  13.0 4.2 %collective-permute-done.3.refs_4_ = bf16[2,32,2048]{2,1,0:T(8,128)(2,1)S(1)} collective-permute-done((bf16[2,32,2048]{2,1,0:T(8,128)(2,1)}, bf16[2,32,2048]{2,1,0:T(8,128)(2,1)S(1)}, u32[]{:S(2)}, u32[]{:S(2)}) %collective-permute-start.3) | collective-permute-done | bytes 262176 | tf_op jit(solution)/shard_map/ppermute | solution.py:198
  17.2 0.5 collective-permute-start.6
  17.7 1.3 collective-permute-start.9
  19.1 1.1 arrange.1.m_ref.refs_0_.refs_1_
  20.3 1.1 copy-done
  21.3 8.7 %partials.2.refs_0_ = f32[1,128,4352]{2,1,0:T(8,128)S(1)} custom-call(bf16[4,2,64,2048]{3,2,1,0:T(8,128)(2,1)S(1)} %arrange.1.m_ref.refs_0_.refs_1_, bf16[3328,2048]{1,0:T(8,128)(2,1)S(1)} %bitcast.1, bf16[1024,2048]{1,0:T(8,128)(2,1)S(1)} %copy-done), custom_call_target="tpu_custom_call" | custom-call | flops 1200000000 | bytes 4000000 | tf_op jit(solution)/shard_map/partials/pallas_call | solution.py:41
  30.1 2.7 %next.6.refs_1_ = s16[128,4480]{1,0:T(8,128)(2,1)S(1)} custom-call(f32[1,128,4352]{2,1,0:T(8,128)S(1)} %partials.2.refs_0_, s16[128,4480]{1,0:T(8,128)(2,1)S(1)} %collective-permute-done.7.refs_1_.refs_5_), custom_call_target="tpu_custom_call" | custom-call | flops 12000000000 | bytes 40000000 | tf_op jit(solution)/shard_map/next/pallas_call | solution.py:41
  32.8 2.1 %collective-permute-start.10 = (s16[128,4480]{1,0:T(8,128)(2,1)S(1)}, s16[128,4480]{1,0:T(8,128)(2,1)S(1)}, u32[]{:S(2)}, u32[]{:S(2)}) collective-permute-start(s16[128,4480]{1,0:T(8,128)(2,1)S(1)} %next.6.refs_1_), channel_id=1, source_target_pairs={{0,1},{1,2},{2,3},{5,4},{6,5},{7,6},{8,9},{9,10},{10,11},{13,12},{... | collective-permute-start | bytes 3440648 | tf_op jit(solution)/shard_map/ppermute | solution.py:608
  34.8 1.5 %gram.1 = (f32[2,256,256]{2,1,0:T(8,128)S(1)}, f32[1,256,256]{2,1,0:T(8,128)S(1)}) custom-call(bf16[4,2,64,2048]{3,2,1,0:T(8,128)(2,1)S(1)} %arrange.1.m_ref.refs_0_.refs_1_, s16[128,4480]{1,0:T(8,128)(2,1)S(1)} %next.6.refs_1_), custom_call_target="tpu_custom_call" | custom-call | flops 6000000000 | bytes 20000000 | tf_op jit(solution)/shard_map/gram/pallas_call | solution.py:41
  36.3 0.8 collective-permute-done.9.refs_1_.refs_7_
  37.1 1.5 %collective-permute-start.12 = (s16[128,4480]{1,0:T(8,128)(2,1)S(1)}, s16[128,4480]{1,0:T(8,128)(2,1)S(1)}, u32[]{:S(2)}, u32[]{:S(2)}) collective-permute-start(s16[128,4480]{1,0:T(8,128)(2,1)S(1)} %next.7.refs_3_), channel_id=1, source_target_pairs={{1,0},{2,1},{3,2},{4,5},{5,6},{6,7},{9,8},{10,9},{11,10},{12,13},{... | collective-permute-start | bytes 3440648 | tf_op jit(solution)/shard_map/ppermute | solution.py:608
  38.6 10.8 %partials.3.refs_0_.refs_2_.refs_1_ = f32[3,128,4352]{2,1,0:T(8,128)S(1)} custom-call(bf16[4,2,64,2048]{3,2,1,0:T(8,128)(2,1)S(1)} %arrange.1.m_ref.refs_0_.refs_1_, bf16[3328,2048]{1,0:T(8,128)(2,1)S(1)} %bitcast.1, bf16[1024,2048]{1,0:T(8,128)(2,1)S(1)} %copy-done, s16[128,4480]{1,0:T(8,128)(2,1)S(1)} %next.7.refs_3_), custom_call_target="tpu_custom_call" | custom-call | flops 1200000000 | bytes 4000000 | tf_op jit(solution)/shard_map/partials/pallas_call | solution.py:41
  49.4 4.6 %collective-permute-start.8 = (f32[1,256,256]{2,1,0:T(8,128)S(1)}, f32[1,256,256]{2,1,0:T(8,128)S(1)}, u32[]{:S(2)}, u32[]{:S(2)}) collective-permute-start(f32[1,256,256]{2,1,0:T(8,128)S(1)} %get-tuple-element.27), channel_id=1, source_target_pairs={{0,1},{3,2},{4,5},{7,6},{8,9},{11,10},{12,13},{15,14},{16,17},{19,... | collective-permute-start | bytes 786440 | tf_op jit(solution)/shard_map/ppermute | solution.py:644
  54.0 1.7 %collective-permute-done.10.refs_1_.refs_6_ = s16[128,4480]{1,0:T(8,128)(2,1)S(1)} collective-permute-done((s16[128,4480]{1,0:T(8,128)(2,1)S(1)}, s16[128,4480]{1,0:T(8,128)(2,1)S(1)}, u32[]{:S(2)}, u32[]{:S(2)}) %collective-permute-start.10) | collective-permute-done | bytes 1146912 | tf_op jit(solution)/shard_map/ppermute | solution.py:608
  55.7 2.6 %next.8.refs_2_ = s16[128,4480]{1,0:T(8,128)(2,1)S(1)} custom-call(f32[3,128,4352]{2,1,0:T(8,128)S(1)} %partials.3.refs_0_.refs_2_.refs_1_, s16[128,4480]{1,0:T(8,128)(2,1)S(1)} %collective-permute-done.10.refs_1_.refs_6_, f32[3,128,4352]{2,1,0:T(8,128)S(1)} %partials.3.refs_0_.refs_2_.refs_1_), custom_call_target="tpu_custom_call" | custom-call | flops 12000000000 | bytes 40000000 | tf_op jit(solution)/shard_map/next/pallas_call | solution.py:41
  58.3 4.6 %collective-permute-start.20 = (s16[128,4480]{1,0:T(8,128)(2,1)S(1)}, s16[128,4480]{1,0:T(8,128)(2,1)S(1)}, u32[]{:S(2)}, u32[]{:S(2)}) collective-permute-start(s16[128,4480]{1,0:T(8,128)(2,1)S(1)} %next.8.refs_2_), channel_id=1, source_target_pairs={{0,1},{1,2},{2,3},{5,4},{6,5},{7,6},{8,9},{9,10},{10,11},{13,12},{... | collective-permute-start | bytes 3440648 | tf_op jit(solution)/shard_map/ppermute | solution.py:608
  62.9 9.6 %collective-permute-start.11 = (f32[1,256,256]{2,1,0:T(8,128)S(1)}, f32[1,256,256]{2,1,0:T(8,128)S(1)}, u32[]{:S(2)}, u32[]{:S(2)}) collective-permute-start(f32[1,256,256]{2,1,0:T(8,128)S(1)} %collective-permute-done.8.refs_1_), channel_id=1, source_target_pairs={{0,4},{4,0},{8,12},{12,8},{16,20},{20,16},{24,28},{28,24},{1,5},{5... | collective-permute-start | bytes 786440 | tf_op jit(solution)/shard_map/ppermute | solution.py:647
  72.5 1.0 copy-done.1
  73.5 1.3 collective-permute-start.21
  74.8 1.2 copy-done.2
  76.1 2.7 %join.1 = (bf16[2,256,4352]{2,1,0:T(8,128)(2,1)S(1)}, f32[8,128]{1,0:T(8,128)S(1)}) custom-call(f32[2,256,256]{2,1,0:T(8,128)S(1)} %copy-done.6, f32[1,256,256]{2,1,0:T(8,128)S(1)} %collective-permute-done.8.refs_1_, f32[1,256,256]{2,1,0:T(8,128)S(1)} %collective-permute-done.11.refs_2_, bf16[2,64,3328]{2,1,0:T(8,128)(2,1)S(1)} %copy-done.4, ...), custom_call_target="tpu_custom_call" | custom-call | flops 300000000 | bytes 1000000 | tf_op jit(solution)/shard_map/join/pallas_call | solution.py:41
  78.8 4.6 %collective-permute-start.13 = (f32[8,128]{1,0:T(8,128)S(1)}, f32[8,128]{1,0:T(8,128)S(1)}, u32[]{:S(2)}, u32[]{:S(2)}) collective-permute-start(f32[8,128]{1,0:T(8,128)S(1)} %get-tuple-element.29), channel_id=1, source_target_pairs={{0,4},{4,0},{8,12},{12,8},{16,20},{20,16},{24,28},{28,24},{1,5},{5... | collective-permute-start | bytes 12296 | tf_op jit(solution)/shard_map/ppermute | solution.py:519
  83.4 0.8 collective-permute-done.13
  84.3 1.5 %collective-permute-start.14 = (f32[8,128]{1,0:T(8,128)S(1)}, f32[8,128]{1,0:T(8,128)S(1)}, u32[]{:S(2)}, u32[]{:S(2)}) collective-permute-start(f32[8,128]{1,0:T(8,128)S(1)} %add.26), channel_id=1, source_target_pairs={{0,8},{4,12},{8,0},{12,4},{16,24},{20,28},{24,16},{28,20},{1,9},{5... | collective-permute-start | bytes 12296 | tf_op jit(solution)/shard_map/ppermute | solution.py:519
  85.8 0.8 collective-permute-start.15
  86.6 1.2 collective-permute-start.16
  87.8 0.1 collective-permute-done.14
  87.9 1.5 %collective-permute-done.15 = f32[8,128]{1,0:T(8,128)S(1)} collective-permute-done((f32[8,128]{1,0:T(8,128)S(1)}, f32[8,128]{1,0:T(8,128)S(1)}, u32[]{:S(2)}, u32[]{:S(2)}) %collective-permute-start.15) | collective-permute-done | bytes 4128 | tf_op jit(solution)/shard_map/ppermute | solution.py:519
  89.4 1.7 %collective-permute-done.16 = f32[8,128]{1,0:T(8,128)S(1)} collective-permute-done((f32[8,128]{1,0:T(8,128)S(1)}, f32[8,128]{1,0:T(8,128)S(1)}, u32[]{:S(2)}, u32[]{:S(2)}) %collective-permute-start.16) | collective-permute-done | bytes 4128 | tf_op jit(solution)/shard_map/ppermute | solution.py:519
  91.1 3.0 %collective-permute-start.17 = (f32[8,128]{1,0:T(8,128)S(1)}, f32[8,128]{1,0:T(8,128)S(1)}, u32[]{:S(2)}, u32[]{:S(2)}) collective-permute-start(f32[8,128]{1,0:T(8,128)S(1)} %add_add_fusion.1), channel_id=1, source_target_pairs={{0,1},{1,0},{2,3},{3,2},{4,5},{5,4},{6,7},{7,6},{8,9},{9,8},{10,11... | collective-permute-start | bytes 12296 | tf_op jit(solution)/shard_map/ppermute | solution.py:519
  94.1 0.2 collective-permute-start.18
  94.3 2.3 %collective-permute-start.19 = (f32[8,128]{1,0:T(8,128)S(1)}, f32[8,128]{1,0:T(8,128)S(1)}, u32[]{:S(2)}, u32[]{:S(2)}) collective-permute-start(f32[8,128]{1,0:T(8,128)S(1)} %add_add_fusion.1), channel_id=1, source_target_pairs={{0,3},{1,2},{2,1},{3,0},{4,7},{5,6},{6,5},{7,4},{8,11},{9,10},{10,... | collective-permute-start | bytes 12296 | tf_op jit(solution)/shard_map/ppermute | solution.py:519
  96.5 2.1 %collective-permute-done.18 = f32[8,128]{1,0:T(8,128)S(1)} collective-permute-done((f32[8,128]{1,0:T(8,128)S(1)}, f32[8,128]{1,0:T(8,128)S(1)}, u32[]{:S(2)}, u32[]{:S(2)}) %collective-permute-start.18) | collective-permute-done | bytes 4128 | tf_op jit(solution)/shard_map/ppermute | solution.py:519
  98.6 1.1 collective-permute-done.19
  99.7 2.7 %next.10.refs_3_ = s16[128,4480]{1,0:T(8,128)(2,1)S(1)} custom-call(f32[1,128,4352]{2,1,0:T(8,128)S(1)} %partials.2.refs_0_, f32[3,128,4352]{2,1,0:T(8,128)S(1)} %partials.3.refs_0_.refs_2_.refs_1_, s16[128,4480]{1,0:T(8,128)(2,1)S(1)} %collective-permute-done.20.refs_2_.refs_3_, f32[2,2]{1,0:T(2,128)S(1)} %pad_maximum_fusion.refs_3_.refs_0_), custom_call_target="tpu_custom_call" | custom-call | flops 300000000 | bytes 1000000 | tf_op jit(solution)/shard_map/next/pallas_call | solution.py:41
  102.4 2.1 %collective-permute-start.22 = (s16[128,4480]{1,0:T(8,128)(2,1)S(1)}, s16[128,4480]{1,0:T(8,128)(2,1)S(1)}, u32[]{:S(2)}, u32[]{:S(2)}) collective-permute-start(s16[128,4480]{1,0:T(8,128)(2,1)S(1)} %next.10.refs_3_), channel_id=1, source_target_pairs={{0,1},{1,2},{2,3},{5,4},{6,5},{7,6},{8,9},{9,10},{10,11},{13,12},{... | collective-permute-start | bytes 3440648 | tf_op jit(solution)/shard_map/ppermute | solution.py:608
  104.6 0.1 next.11.refs_5_
  104.7 1.3 collective-permute-start.23
  106.0 17.0 %weights.1 = (f32[8,128]{1,0:T(8,128)S(1)}, f32[3328,2048]{1,0:T(8,128)}, f32[1024,2048]{1,0:T(8,128)}) custom-call(f32[2,2]{1,0:T(2,128)S(1)} %pad_maximum_fusion.refs_3_.refs_0_, bf16[4,2,64,2048]{3,2,1,0:T(8,128)(2,1)S(1)} %arrange.1.m_ref.refs_0_.refs_1_, bf16[2,256,4352]{2,1,0:T(8,128)(2,1)S(1)} %get-tuple-element.36.refs_2_, ...), custom_call_target="tpu_custom_call" | custom-call | flops 300000000 | bytes 1000000 | tf_op jit(solution)/shard_map/weights/pallas_call | solution.py:41
  123.0 6.8 %collective-permute-done.22.refs_0_.refs_1_ = s16[128,4480]{1,0:T(8,128)(2,1)S(1)} collective-permute-done((s16[128,4480]{1,0:T(8,128)(2,1)S(1)}, s16[128,4480]{1,0:T(8,128)(2,1)S(1)}, u32[]{:S(2)}, u32[]{:S(2)}) %collective-permute-start.22) | collective-permute-done | bytes 1146912 | tf_op jit(solution)/shard_map/ppermute | solution.py:608
  129.8 2.2 %finish.1 = (bf16[2,64,3328]{2,1,0:T(8,128)(2,1)}, bf16[2,64,1024]{2,1,0:T(8,128)(2,1)}) custom-call(f32[3,128,4352]{2,1,0:T(8,128)S(1)} %partials.3.refs_0_.refs_2_.refs_1_, s16[128,4480]{1,0:T(8,128)(2,1)S(1)} %collective-permute-done.22.refs_0_.refs_1_, s16[128,4480]{1,0:T(8,128)(2,1)S(1)} %collective-permute-done.23.refs_2_, f32[8,128]{1,0:T(8,128)S(1)} %wait.1.refs_3_), custom_call_target="tpu_custom_call" | custom-call | flops 300000000 | bytes 1000000 | tf_op jit(solution)/shard_map/finish/pallas_call | solution.py:41
  (52 shorter events, 0.3 us)
Async XLA Ops:
  0.6 11.9 %collective-permute-start.1 = (bf16[2,32,2048]{2,1,0:T(8,128)(2,1)}, bf16[2,32,2048]{2,1,0:T(8,128)(2,1)S(1)}, u32[]{:S(2)}, u32[]{:S(2)}) collective-permute-start(bf16[2,32,2048]{2,1,0:T(8,128)(2,1)} %refs_0_.1), channel_id=1, source_target_pairs={{0,8},{4,12},{8,0},{12,4},{16,24},{20,28},{24,16},{28,20},{1,9},{5... | collective-permute-start | bytes 786440 | tf_op jit(solution)/shard_map/ppermute | solution.py:198
  3.6 13.6 %collective-permute-start.3 = (bf16[2,32,2048]{2,1,0:T(8,128)(2,1)}, bf16[2,32,2048]{2,1,0:T(8,128)(2,1)S(1)}, u32[]{:S(2)}, u32[]{:S(2)}) collective-permute-start(bf16[2,32,2048]{2,1,0:T(8,128)(2,1)} %refs_0_.1), channel_id=1, source_target_pairs={{0,16},{4,20},{8,24},{12,28},{16,0},{20,4},{24,8},{28,12},{1,17},{... | collective-permute-start | bytes 786440 | tf_op jit(solution)/shard_map/ppermute | solution.py:198
  5.2 12.1 %collective-permute-start.5 = (bf16[2,32,2048]{2,1,0:T(8,128)(2,1)}, bf16[2,32,2048]{2,1,0:T(8,128)(2,1)S(1)}, u32[]{:S(2)}, u32[]{:S(2)}) collective-permute-start(bf16[2,32,2048]{2,1,0:T(8,128)(2,1)} %refs_0_.1), channel_id=1, source_target_pairs={{0,24},{4,28},{8,16},{12,20},{16,8},{20,12},{24,0},{28,4},{1,25},{... | collective-permute-start | bytes 786440 | tf_op jit(solution)/shard_map/ppermute | solution.py:198
  5.2 1.2 copy-start.3
  6.3 0.9 copy-start.7
  7.3 5.1 %copy-start.9 = (bf16[2,32,2048]{2,1,0:T(8,128)(2,1)S(1)}, bf16[2,32,2048]{2,1,0:T(8,128)(2,1)}, u32[]{:S(2)}) copy-start(bf16[2,32,2048]{2,1,0:T(8,128)(2,1)} %refs_0_.1) | copy-start | bytes 786436
  7.3 11.9 %copy-start.10 = (s32[2,2]{1,0:T(2,128)S(1)}, s32[2,2]{1,0:T(2,128)}, u32[]{:S(2)}) copy-start(s32[2,2]{1,0:T(2,128)} %spans.1) | copy-start | bytes 52
  7.3 12.9 %slice-start = ((s8[13631488]{0:T(1024)(128)(4,1)}), s8[4194304]{0:T(1024)(128)(4,1)S(1)}, s32[]{:S(2)}) async-start(s8[13631488]{0:T(1024)(128)(4,1)} %bitcast), calls=%async_computation | async-start | bytes 8388608
  7.3 12.9 %slice-start.1 = ((s8[13631488]{0:T(1024)(128)(4,1)}), s8[4194304]{0:T(1024)(128)(4,1)S(1)}, s32[]{:S(2)}) async-start(s8[13631488]{0:T(1024)(128)(4,1)} %bitcast), calls=%async_computation.1 | async-start | bytes 8388608
  8.1 12.1 %slice-start.2 = ((s8[13631488]{0:T(1024)(128)(4,1)}), s8[4194304]{0:T(1024)(128)(4,1)S(1)}, s32[]{:S(2)}) async-start(s8[13631488]{0:T(1024)(128)(4,1)} %bitcast), calls=%async_computation.2 | async-start | bytes 8388608
  8.1 12.1 %slice-start.3 = ((s8[13631488]{0:T(1024)(128)(4,1)}), s8[1048576]{0:T(1024)(128)(4,1)S(1)}, s32[]{:S(2)}) async-start(s8[13631488]{0:T(1024)(128)(4,1)} %bitcast), calls=%async_computation.3 | async-start | bytes 2097152
  8.1 22.0 %collective-permute-start.7 = (s16[128,4480]{1,0:T(8,128)(2,1)S(1)}, s16[128,4480]{1,0:T(8,128)(2,1)S(1)}, u32[]{:S(2)}, u32[]{:S(2)}) collective-permute-start(s16[128,4480]{1,0:T(8,128)(2,1)S(1)} %code.1), channel_id=1, source_target_pairs={{0,1},{1,2},{2,3},{5,4},{6,5},{7,6},{8,9},{9,10},{10,11},{13,12},{... | collective-permute-start | bytes 3440648 | tf_op jit(solution)/shard_map/ppermute | solution.py:608
  12.4 5.3 %collective-permute-start = (bf16[2,32,2048]{2,1,0:T(8,128)(2,1)S(1)}, bf16[2,32,2048]{2,1,0:T(8,128)(2,1)S(1)}, u32[]{:S(2)}, u32[]{:S(2)}) collective-permute-start(bf16[2,32,2048]{2,1,0:T(8,128)(2,1)S(1)} %copy-done.9), channel_id=1, source_target_pairs={{0,4},{4,0},{8,12},{12,8},{16,20},{20,16},{24,28},{28,24},{1,5},{5... | collective-permute-start | bytes 786440 | tf_op jit(solution)/shard_map/ppermute | solution.py:204
  12.5 6.5 %collective-permute-start.2 = (bf16[2,32,2048]{2,1,0:T(8,128)(2,1)S(1)}, bf16[2,32,2048]{2,1,0:T(8,128)(2,1)S(1)}, u32[]{:S(2)}, u32[]{:S(2)}) collective-permute-start(bf16[2,32,2048]{2,1,0:T(8,128)(2,1)S(1)} %collective-permute-done.1.refs_2_), channel_id=1, source_target_pairs={{0,4},{4,0},{8,12},{12,8},{16,20},{20,16},{24,28},{28,24},{1,5},{5... | collective-permute-start | bytes 786440 | tf_op jit(solution)/shard_map/ppermute | solution.py:204
  17.2 1.8 %collective-permute-start.4 = (bf16[2,32,2048]{2,1,0:T(8,128)(2,1)S(1)}, bf16[2,32,2048]{2,1,0:T(8,128)(2,1)S(1)}, u32[]{:S(2)}, u32[]{:S(2)}) collective-permute-start(bf16[2,32,2048]{2,1,0:T(8,128)(2,1)S(1)} %collective-permute-done.3.refs_4_), channel_id=1, source_target_pairs={{0,4},{4,0},{8,12},{12,8},{16,20},{20,16},{24,28},{28,24},{1,5},{5... | collective-permute-start | bytes 786440 | tf_op jit(solution)/shard_map/ppermute | solution.py:204
  17.2 1.9 %collective-permute-start.6 = (bf16[2,32,2048]{2,1,0:T(8,128)(2,1)S(1)}, bf16[2,32,2048]{2,1,0:T(8,128)(2,1)S(1)}, u32[]{:S(2)}, u32[]{:S(2)}) collective-permute-start(bf16[2,32,2048]{2,1,0:T(8,128)(2,1)S(1)} %collective-permute-done.5.refs_6_), channel_id=1, source_target_pairs={{0,4},{4,0},{8,12},{12,8},{16,20},{20,16},{24,28},{28,24},{1,5},{5... | collective-permute-start | bytes 786440 | tf_op jit(solution)/shard_map/ppermute | solution.py:204
  17.7 19.3 %collective-permute-start.9 = (s16[128,4480]{1,0:T(8,128)(2,1)S(1)}, s16[128,4480]{1,0:T(8,128)(2,1)S(1)}, u32[]{:S(2)}, u32[]{:S(2)}) collective-permute-start(s16[128,4480]{1,0:T(8,128)(2,1)S(1)} %code.1), channel_id=1, source_target_pairs={{1,0},{2,1},{3,2},{4,5},{5,6},{6,7},{9,8},{10,9},{11,10},{12,13},{... | collective-permute-start | bytes 3440648 | tf_op jit(solution)/shard_map/ppermute | solution.py:608
  19.1 2.2 %copy-start = (bf16[1024,2048]{1,0:T(8,128)(2,1)S(1)}, bf16[1024,2048]{1,0:T(8,128)(2,1)}, u32[]{:S(2)}) copy-start(bf16[1024,2048]{1,0:T(8,128)(2,1)} %refs_2_.1) | copy-start | bytes 12582916
  32.8 22.9 %collective-permute-start.10 = (s16[128,4480]{1,0:T(8,128)(2,1)S(1)}, s16[128,4480]{1,0:T(8,128)(2,1)S(1)}, u32[]{:S(2)}, u32[]{:S(2)}) collective-permute-start(s16[128,4480]{1,0:T(8,128)(2,1)S(1)} %next.6.refs_1_), channel_id=1, source_target_pairs={{0,1},{1,2},{2,3},{5,4},{6,5},{7,6},{8,9},{9,10},{10,11},{13,12},{... | collective-permute-start | bytes 3440648 | tf_op jit(solution)/shard_map/ppermute | solution.py:608
  36.3 0.8 copy-start.5
  37.1 35.4 %collective-permute-start.12 = (s16[128,4480]{1,0:T(8,128)(2,1)S(1)}, s16[128,4480]{1,0:T(8,128)(2,1)S(1)}, u32[]{:S(2)}, u32[]{:S(2)}) collective-permute-start(s16[128,4480]{1,0:T(8,128)(2,1)S(1)} %next.7.refs_3_), channel_id=1, source_target_pairs={{1,0},{2,1},{3,2},{4,5},{5,6},{6,7},{9,8},{10,9},{11,10},{12,13},{... | collective-permute-start | bytes 3440648 | tf_op jit(solution)/shard_map/ppermute | solution.py:608
  49.4 13.5 %collective-permute-start.8 = (f32[1,256,256]{2,1,0:T(8,128)S(1)}, f32[1,256,256]{2,1,0:T(8,128)S(1)}, u32[]{:S(2)}, u32[]{:S(2)}) collective-permute-start(f32[1,256,256]{2,1,0:T(8,128)S(1)} %get-tuple-element.27), channel_id=1, source_target_pairs={{0,1},{3,2},{4,5},{7,6},{8,9},{11,10},{12,13},{15,14},{16,17},{19,... | collective-permute-start | bytes 786440 | tf_op jit(solution)/shard_map/ppermute | solution.py:644
  58.3 16.5 %copy-start.4 = (bf16[2,64,3328]{2,1,0:T(8,128)(2,1)S(1)}, bf16[2,64,3328]{2,1,0:T(8,128)(2,1)}, u32[]{:S(2)}) copy-start(bf16[2,64,3328]{2,1,0:T(8,128)(2,1)} %refs_3_.1) | copy-start | bytes 2555908
  58.3 16.5 %copy-start.6 = (f32[2,256,256]{2,1,0:T(8,128)S(1)}, f32[2,256,256]{2,1,0:T(8,128)}, u32[]{:S(2)}) copy-start(f32[2,256,256]{2,1,0:T(8,128)} %copy-done.5) | copy-start | bytes 1572868
  58.3 16.5 %copy-start.8 = (bf16[2,64,1024]{2,1,0:T(8,128)(2,1)S(1)}, bf16[2,64,1024]{2,1,0:T(8,128)(2,1)}, u32[]{:S(2)}) copy-start(bf16[2,64,1024]{2,1,0:T(8,128)(2,1)} %refs_4_.1) | copy-start | bytes 786436
  58.3 41.4 %collective-permute-start.20 = (s16[128,4480]{1,0:T(8,128)(2,1)S(1)}, s16[128,4480]{1,0:T(8,128)(2,1)S(1)}, u32[]{:S(2)}, u32[]{:S(2)}) collective-permute-start(s16[128,4480]{1,0:T(8,128)(2,1)S(1)} %next.8.refs_2_), channel_id=1, source_target_pairs={{0,1},{1,2},{2,3},{5,4},{6,5},{7,6},{8,9},{9,10},{10,11},{13,12},{... | collective-permute-start | bytes 3440648 | tf_op jit(solution)/shard_map/ppermute | solution.py:608
  62.9 11.8 %collective-permute-start.11 = (f32[1,256,256]{2,1,0:T(8,128)S(1)}, f32[1,256,256]{2,1,0:T(8,128)S(1)}, u32[]{:S(2)}, u32[]{:S(2)}) collective-permute-start(f32[1,256,256]{2,1,0:T(8,128)S(1)} %collective-permute-done.8.refs_1_), channel_id=1, source_target_pairs={{0,4},{4,0},{8,12},{12,8},{16,20},{20,16},{24,28},{28,24},{1,5},{5... | collective-permute-start | bytes 786440 | tf_op jit(solution)/shard_map/ppermute | solution.py:647
  72.5 1.0 copy-start.1
  73.5 31.1 %collective-permute-start.21 = (s16[128,4480]{1,0:T(8,128)(2,1)S(1)}, s16[128,4480]{1,0:T(8,128)(2,1)S(1)}, u32[]{:S(2)}, u32[]{:S(2)}) collective-permute-start(s16[128,4480]{1,0:T(8,128)(2,1)S(1)} %next.9.refs_9_), channel_id=1, source_target_pairs={{1,0},{2,1},{3,2},{4,5},{5,6},{6,7},{9,8},{10,9},{11,10},{12,13},{... | collective-permute-start | bytes 3440648 | tf_op jit(solution)/shard_map/ppermute | solution.py:608
  74.8 1.3 copy-start.2
  78.8 5.5 %collective-permute-start.13 = (f32[8,128]{1,0:T(8,128)S(1)}, f32[8,128]{1,0:T(8,128)S(1)}, u32[]{:S(2)}, u32[]{:S(2)}) collective-permute-start(f32[8,128]{1,0:T(8,128)S(1)} %get-tuple-element.29), channel_id=1, source_target_pairs={{0,4},{4,0},{8,12},{12,8},{16,20},{20,16},{24,28},{28,24},{1,5},{5... | collective-permute-start | bytes 12296 | tf_op jit(solution)/shard_map/ppermute | solution.py:519
  84.3 3.6 %collective-permute-start.14 = (f32[8,128]{1,0:T(8,128)S(1)}, f32[8,128]{1,0:T(8,128)S(1)}, u32[]{:S(2)}, u32[]{:S(2)}) collective-permute-start(f32[8,128]{1,0:T(8,128)S(1)} %add.26), channel_id=1, source_target_pairs={{0,8},{4,12},{8,0},{12,4},{16,24},{20,28},{24,16},{28,20},{1,9},{5... | collective-permute-start | bytes 12296 | tf_op jit(solution)/shard_map/ppermute | solution.py:519
  85.8 3.6 %collective-permute-start.15 = (f32[8,128]{1,0:T(8,128)S(1)}, f32[8,128]{1,0:T(8,128)S(1)}, u32[]{:S(2)}, u32[]{:S(2)}) collective-permute-start(f32[8,128]{1,0:T(8,128)S(1)} %add.26), channel_id=1, source_target_pairs={{0,16},{4,20},{8,24},{12,28},{16,0},{20,4},{24,8},{28,12},{1,17},{... | collective-permute-start | bytes 12296 | tf_op jit(solution)/shard_map/ppermute | solution.py:519
  86.6 4.5 %collective-permute-start.16 = (f32[8,128]{1,0:T(8,128)S(1)}, f32[8,128]{1,0:T(8,128)S(1)}, u32[]{:S(2)}, u32[]{:S(2)}) collective-permute-start(f32[8,128]{1,0:T(8,128)S(1)} %add.26), channel_id=1, source_target_pairs={{0,24},{4,28},{8,16},{12,20},{16,8},{20,12},{24,0},{28,4},{1,25},{... | collective-permute-start | bytes 12296 | tf_op jit(solution)/shard_map/ppermute | solution.py:519
  91.1 5.4 %collective-permute-start.17 = (f32[8,128]{1,0:T(8,128)S(1)}, f32[8,128]{1,0:T(8,128)S(1)}, u32[]{:S(2)}, u32[]{:S(2)}) collective-permute-start(f32[8,128]{1,0:T(8,128)S(1)} %add_add_fusion.1), channel_id=1, source_target_pairs={{0,1},{1,0},{2,3},{3,2},{4,5},{5,4},{6,7},{7,6},{8,9},{9,8},{10,11... | collective-permute-start | bytes 12296 | tf_op jit(solution)/shard_map/ppermute | solution.py:519
  94.1 4.5 %collective-permute-start.18 = (f32[8,128]{1,0:T(8,128)S(1)}, f32[8,128]{1,0:T(8,128)S(1)}, u32[]{:S(2)}, u32[]{:S(2)}) collective-permute-start(f32[8,128]{1,0:T(8,128)S(1)} %add_add_fusion.1), channel_id=1, source_target_pairs={{0,2},{1,3},{2,0},{3,1},{4,6},{5,7},{6,4},{7,5},{8,10},{9,11},{10,... | collective-permute-start | bytes 12296 | tf_op jit(solution)/shard_map/ppermute | solution.py:519
  94.3 5.4 %collective-permute-start.19 = (f32[8,128]{1,0:T(8,128)S(1)}, f32[8,128]{1,0:T(8,128)S(1)}, u32[]{:S(2)}, u32[]{:S(2)}) collective-permute-start(f32[8,128]{1,0:T(8,128)S(1)} %add_add_fusion.1), channel_id=1, source_target_pairs={{0,3},{1,2},{2,1},{3,0},{4,7},{5,6},{6,5},{7,4},{8,11},{9,10},{10,... | collective-permute-start | bytes 12296 | tf_op jit(solution)/shard_map/ppermute | solution.py:519
  102.4 27.4 %collective-permute-start.22 = (s16[128,4480]{1,0:T(8,128)(2,1)S(1)}, s16[128,4480]{1,0:T(8,128)(2,1)S(1)}, u32[]{:S(2)}, u32[]{:S(2)}) collective-permute-start(s16[128,4480]{1,0:T(8,128)(2,1)S(1)} %next.10.refs_3_), channel_id=1, source_target_pairs={{0,1},{1,2},{2,3},{5,4},{6,5},{7,6},{8,9},{9,10},{10,11},{13,12},{... | collective-permute-start | bytes 3440648 | tf_op jit(solution)/shard_map/ppermute | solution.py:608
  104.7 25.1 %collective-permute-start.23 = (s16[128,4480]{1,0:T(8,128)(2,1)S(1)}, s16[128,4480]{1,0:T(8,128)(2,1)S(1)}, u32[]{:S(2)}, u32[]{:S(2)}) collective-permute-start(s16[128,4480]{1,0:T(8,128)(2,1)S(1)} %next.11.refs_5_), channel_id=1, source_target_pairs={{1,0},{2,1},{3,2},{4,5},{5,6},{6,7},{9,8},{10,9},{11,10},{12,13},{... | collective-permute-start | bytes 3440648 | tf_op jit(solution)/shard_map/ppermute | solution.py:608

commit v4 on v3

--- a/solution.py
+++ b/solution.py
@@ -615,8 +615,10 @@
     inward = [(row * n + a, row * n + b) for row in range(row_count) for a, b in ((0, 1), (3, 2))]
     cores = [(i, i ^ 1) for i in range(row_count)]
 
+    def over_rows(sq_norm):
+        return sum_over(sq_norm, "row", row_count, [[1], range(2, row_count, 2)])
+
     def factors(sq_norm):
-        sq_norm = sum_over(sq_norm, "row", row_count, [[1], range(2, row_count, 2)])
         sq_norm = sum_over(sq_norm, "col", n, [range(1, n)])
         factor = 1.0 / (jnp.sqrt(sq_norm[0, :examples]) + GAMMA)
         return jnp.stack([factor * scale for scale in scales])
@@ -631,8 +633,8 @@
             joined, sq_norm = join(
                 chunk, n, True, grams, hidden, context, came[0][:2], came[1][:2], latest
             )
-            factor = factors(sq_norm)
-            latest = (factor,)
+            sq_norm = over_rows(sq_norm)
+            latest = (sq_norm,)
         for flow in (0, 1):
             message = next_message(chunk, n, s, flow, first, second, came[flow][-1], latest)
             latest = (message,)
@@ -643,6 +645,9 @@
                 if early:
                     grams[1] = lax.ppermute(mine, ("row", "col"), inward)
                 latest = (masked_gram,)
+            if s == n - 1 and flow == 0 and early:
+                factor = factors(after(sq_norm, message))
+                latest = (factor,)
             if s == 2 and flow == 0 and early:
                 grams[2] = lax.ppermute(after(grams[1], message), "row", cores)
         if s == 1:
@@ -656,7 +661,7 @@
         joined, sq_norm = join(
             chunk, n, False, grams, hidden, context, came[0][:-1], came[1][:-1], latest
         )
-        factor = factors(sq_norm)
+        factor = factors(over_rows(sq_norm))
     token, down_grad, heads_grad = weight_grads(
         chunk, factor, masked, joined, last, widths, latest
     )

time: 132 us -> 130 us (0.985); the launches traced: 132 us -> 129 us
  waiting for transfers between devices: 20.9 us -> 16.6 us
    ppermute x7, waiting for transfers between devices: 7.29 us -> 4.36 us  [sum_over(): lax.ppermute(x, axis, [(i, i ^ j) for i in range(count)])]
    ppermute x8, waiting for transfers between devices: 9.27 us -> 7.9 us  [send(): return lax.ppermute(x, ('row', 'col'), flow_pairs(n, row_count, flow))]
  transfers between devices with their start and end apart: 24 -> 24, of which waited for: 11 -> 11; matrix products, arithmetic and copies ran while one was open for 0% -> 0% of each run, Pallas kernels for 38% -> 39%
where the time goes in v4:
time: 130 us; the launch traced here: 129 us
  Pallas kernels  52.9 us (41%)
  starting transfers between devices  52.6 us (40%)
  waiting for transfers between devices  16.6 us (13%)
  local copies, waits for them, and re-layouts  5.52 us (4%)
    pallas_call x14, Pallas kernels, call(): return pl.pallas_call(kernel, in_specs=specs, **rest)(*arrays, *deps)  51.8 us
    ppermute x8, starting transfers between devices, send(): return lax.ppermute(x, ('row', 'col'), flow_pairs(n, row_count, flow))  19.2 us
    ppermute x7, starting transfers between devices, sum_over(): lax.ppermute(x, axis, [(i, i ^ j) for i in range(count)])  13.6 us
    ppermute x1, starting transfers between devices, body(): grams[2] = lax.ppermute(after(grams[1], message), 'row', cores)  9.55 us
    ppermute x8, waiting for transfers between devices, send(): return lax.ppermute(x, ('row', 'col'), flow_pairs(n, row_count, flow))  7.9 us
    unnamed x30, local copies, waits for them, and re-layouts  5.52 us
    ppermute x1, starting transfers between devices, body(): grams[1] = lax.ppermute(mine, ('row', 'col'), inward)  4.57 us
    ppermute x3, starting transfers between devices, gather_rows(): near.append(lax.ppermute(x, 'row', [(i, i ^ j) for i in range(row_count)]))  4.54 us
  transfers between devices with their start and end apart: 24, of which 11 were waited for; matrix products, arithmetic and copies ran while one was open for 0% of the time, Pallas kernels for 39%

profile of v4, /device:TPU:0, one launch (start us, length us, event | category | flops | bytes accessed | tf_op | source)
XLA Modules:
  0.0 128.7 jit_solution(5521344639150179323)
XLA Ops:
  0.6 3.0 %collective-permute-start.1 = (bf16[2,32,2048]{2,1,0:T(8,128)(2,1)}, bf16[2,32,2048]{2,1,0:T(8,128)(2,1)S(1)}, u32[]{:S(2)}, u32[]{:S(2)}) collective-permute-start(bf16[2,32,2048]{2,1,0:T(8,128)(2,1)} %refs_0_.1), channel_id=1, source_target_pairs={{0,8},{4,12},{8,0},{12,4},{16,24},{20,28},{24,16},{28,20},{1,9},{5... | collective-permute-start | bytes 786440 | tf_op jit(solution)/shard_map/ppermute | solution.py:198
  3.6 1.5 %collective-permute-start.3 = (bf16[2,32,2048]{2,1,0:T(8,128)(2,1)}, bf16[2,32,2048]{2,1,0:T(8,128)(2,1)S(1)}, u32[]{:S(2)}, u32[]{:S(2)}) collective-permute-start(bf16[2,32,2048]{2,1,0:T(8,128)(2,1)} %refs_0_.1), channel_id=1, source_target_pairs={{0,16},{4,20},{8,24},{12,28},{16,0},{20,4},{24,8},{28,12},{1,17},{... | collective-permute-start | bytes 786440 | tf_op jit(solution)/shard_map/ppermute | solution.py:198
  5.2 1.2 copy-done.3
  6.3 0.9 copy-done.7
  7.3 0.8 code.1
  8.1 4.3 %collective-permute-start.7 = (s16[128,4480]{1,0:T(8,128)(2,1)S(1)}, s16[128,4480]{1,0:T(8,128)(2,1)S(1)}, u32[]{:S(2)}, u32[]{:S(2)}) collective-permute-start(s16[128,4480]{1,0:T(8,128)(2,1)S(1)} %code.1), channel_id=1, source_target_pairs={{0,1},{1,2},{2,3},{5,4},{6,5},{7,6},{8,9},{9,10},{10,11},{13,12},{... | collective-permute-start | bytes 3440648 | tf_op jit(solution)/shard_map/ppermute | solution.py:608
  12.5 0.5 collective-permute-start.2
  13.0 4.2 %collective-permute-done.3.refs_4_ = bf16[2,32,2048]{2,1,0:T(8,128)(2,1)S(1)} collective-permute-done((bf16[2,32,2048]{2,1,0:T(8,128)(2,1)}, bf16[2,32,2048]{2,1,0:T(8,128)(2,1)S(1)}, u32[]{:S(2)}, u32[]{:S(2)}) %collective-permute-start.3) | collective-permute-done | bytes 262176 | tf_op jit(solution)/shard_map/ppermute | solution.py:198
  17.2 0.5 collective-permute-start.6
  17.7 1.3 collective-permute-start.9
  19.1 1.1 arrange.1.m_ref.refs_0_.refs_1_
  20.3 1.1 copy-done
  21.3 8.7 %partials.2.refs_0_ = f32[1,128,4352]{2,1,0:T(8,128)S(1)} custom-call(bf16[4,2,64,2048]{3,2,1,0:T(8,128)(2,1)S(1)} %arrange.1.m_ref.refs_0_.refs_1_, bf16[3328,2048]{1,0:T(8,128)(2,1)S(1)} %bitcast.1, bf16[1024,2048]{1,0:T(8,128)(2,1)S(1)} %copy-done), custom_call_target="tpu_custom_call" | custom-call | flops 1200000000 | bytes 4000000 | tf_op jit(solution)/shard_map/partials/pallas_call | solution.py:41
  30.1 2.7 %next.6.refs_1_ = s16[128,4480]{1,0:T(8,128)(2,1)S(1)} custom-call(f32[1,128,4352]{2,1,0:T(8,128)S(1)} %partials.2.refs_0_, s16[128,4480]{1,0:T(8,128)(2,1)S(1)} %collective-permute-done.7.refs_1_.refs_5_), custom_call_target="tpu_custom_call" | custom-call | flops 12000000000 | bytes 40000000 | tf_op jit(solution)/shard_map/next/pallas_call | solution.py:41
  32.8 2.1 %collective-permute-start.10 = (s16[128,4480]{1,0:T(8,128)(2,1)S(1)}, s16[128,4480]{1,0:T(8,128)(2,1)S(1)}, u32[]{:S(2)}, u32[]{:S(2)}) collective-permute-start(s16[128,4480]{1,0:T(8,128)(2,1)S(1)} %next.6.refs_1_), channel_id=1, source_target_pairs={{0,1},{1,2},{2,3},{5,4},{6,5},{7,6},{8,9},{9,10},{10,11},{13,12},{... | collective-permute-start | bytes 3440648 | tf_op jit(solution)/shard_map/ppermute | solution.py:608
  34.8 1.5 %gram.1 = (f32[2,256,256]{2,1,0:T(8,128)S(1)}, f32[1,256,256]{2,1,0:T(8,128)S(1)}) custom-call(bf16[4,2,64,2048]{3,2,1,0:T(8,128)(2,1)S(1)} %arrange.1.m_ref.refs_0_.refs_1_, s16[128,4480]{1,0:T(8,128)(2,1)S(1)} %next.6.refs_1_), custom_call_target="tpu_custom_call" | custom-call | flops 6000000000 | bytes 20000000 | tf_op jit(solution)/shard_map/gram/pallas_call | solution.py:41
  36.3 0.8 collective-permute-done.9.refs_1_.refs_7_
  37.1 1.5 %collective-permute-start.12 = (s16[128,4480]{1,0:T(8,128)(2,1)S(1)}, s16[128,4480]{1,0:T(8,128)(2,1)S(1)}, u32[]{:S(2)}, u32[]{:S(2)}) collective-permute-start(s16[128,4480]{1,0:T(8,128)(2,1)S(1)} %next.7.refs_3_), channel_id=1, source_target_pairs={{1,0},{2,1},{3,2},{4,5},{5,6},{6,7},{9,8},{10,9},{11,10},{12,13},{... | collective-permute-start | bytes 3440648 | tf_op jit(solution)/shard_map/ppermute | solution.py:608
  38.6 10.8 %partials.3.refs_0_.refs_2_.refs_1_ = f32[3,128,4352]{2,1,0:T(8,128)S(1)} custom-call(bf16[4,2,64,2048]{3,2,1,0:T(8,128)(2,1)S(1)} %arrange.1.m_ref.refs_0_.refs_1_, bf16[3328,2048]{1,0:T(8,128)(2,1)S(1)} %bitcast.1, bf16[1024,2048]{1,0:T(8,128)(2,1)S(1)} %copy-done, s16[128,4480]{1,0:T(8,128)(2,1)S(1)} %next.7.refs_3_), custom_call_target="tpu_custom_call" | custom-call | flops 1200000000 | bytes 4000000 | tf_op jit(solution)/shard_map/partials/pallas_call | solution.py:41
  49.4 4.6 %collective-permute-start.8 = (f32[1,256,256]{2,1,0:T(8,128)S(1)}, f32[1,256,256]{2,1,0:T(8,128)S(1)}, u32[]{:S(2)}, u32[]{:S(2)}) collective-permute-start(f32[1,256,256]{2,1,0:T(8,128)S(1)} %get-tuple-element.28), channel_id=1, source_target_pairs={{0,1},{3,2},{4,5},{7,6},{8,9},{11,10},{12,13},{15,14},{16,17},{19,... | collective-permute-start | bytes 786440 | tf_op jit(solution)/shard_map/ppermute | solution.py:646
  54.0 1.7 %collective-permute-done.10.refs_1_.refs_6_ = s16[128,4480]{1,0:T(8,128)(2,1)S(1)} collective-permute-done((s16[128,4480]{1,0:T(8,128)(2,1)S(1)}, s16[128,4480]{1,0:T(8,128)(2,1)S(1)}, u32[]{:S(2)}, u32[]{:S(2)}) %collective-permute-start.10) | collective-permute-done | bytes 1146912 | tf_op jit(solution)/shard_map/ppermute | solution.py:608
  55.7 2.6 %next.8.refs_2_ = s16[128,4480]{1,0:T(8,128)(2,1)S(1)} custom-call(f32[3,128,4352]{2,1,0:T(8,128)S(1)} %partials.3.refs_0_.refs_2_.refs_1_, s16[128,4480]{1,0:T(8,128)(2,1)S(1)} %collective-permute-done.10.refs_1_.refs_6_, f32[3,128,4352]{2,1,0:T(8,128)S(1)} %partials.3.refs_0_.refs_2_.refs_1_), custom_call_target="tpu_custom_call" | custom-call | flops 12000000000 | bytes 40000000 | tf_op jit(solution)/shard_map/next/pallas_call | solution.py:41
  58.3 4.6 %collective-permute-start.17 = (s16[128,4480]{1,0:T(8,128)(2,1)S(1)}, s16[128,4480]{1,0:T(8,128)(2,1)S(1)}, u32[]{:S(2)}, u32[]{:S(2)}) collective-permute-start(s16[128,4480]{1,0:T(8,128)(2,1)S(1)} %next.8.refs_2_), channel_id=1, source_target_pairs={{0,1},{1,2},{2,3},{5,4},{6,5},{7,6},{8,9},{9,10},{10,11},{13,12},{... | collective-permute-start | bytes 3440648 | tf_op jit(solution)/shard_map/ppermute | solution.py:608
  62.9 9.6 %collective-permute-start.11 = (f32[1,256,256]{2,1,0:T(8,128)S(1)}, f32[1,256,256]{2,1,0:T(8,128)S(1)}, u32[]{:S(2)}, u32[]{:S(2)}) collective-permute-start(f32[1,256,256]{2,1,0:T(8,128)S(1)} %collective-permute-done.8.refs_1_), channel_id=1, source_target_pairs={{0,4},{4,0},{8,12},{12,8},{16,20},{20,16},{24,28},{28,24},{1,5},{5... | collective-permute-start | bytes 786440 | tf_op jit(solution)/shard_map/ppermute | solution.py:652
  72.5 1.0 copy-done.1
  73.5 1.3 collective-permute-start.21
  74.8 1.2 copy-done.2
  76.1 2.7 %join.1 = (bf16[2,256,4352]{2,1,0:T(8,128)(2,1)S(1)}, f32[8,128]{1,0:T(8,128)S(1)}) custom-call(f32[2,256,256]{2,1,0:T(8,128)S(1)} %copy-done.6, f32[1,256,256]{2,1,0:T(8,128)S(1)} %collective-permute-done.8.refs_1_, f32[1,256,256]{2,1,0:T(8,128)S(1)} %collective-permute-done.11.refs_2_, bf16[2,64,3328]{2,1,0:T(8,128)(2,1)S(1)} %copy-done.4, ...), custom_call_target="tpu_custom_call" | custom-call | flops 300000000 | bytes 1000000 | tf_op jit(solution)/shard_map/join/pallas_call | solution.py:41
  78.8 4.6 %collective-permute-start.13 = (f32[8,128]{1,0:T(8,128)S(1)}, f32[8,128]{1,0:T(8,128)S(1)}, u32[]{:S(2)}, u32[]{:S(2)}) collective-permute-start(f32[8,128]{1,0:T(8,128)S(1)} %get-tuple-element.30), channel_id=1, source_target_pairs={{0,4},{4,0},{8,12},{12,8},{16,20},{20,16},{24,28},{28,24},{1,5},{5... | collective-permute-start | bytes 12296 | tf_op jit(solution)/shard_map/ppermute | solution.py:519
  83.4 0.8 collective-permute-done.13
  84.3 1.5 %collective-permute-start.14 = (f32[8,128]{1,0:T(8,128)S(1)}, f32[8,128]{1,0:T(8,128)S(1)}, u32[]{:S(2)}, u32[]{:S(2)}) collective-permute-start(f32[8,128]{1,0:T(8,128)S(1)} %add.26), channel_id=1, source_target_pairs={{0,8},{4,12},{8,0},{12,4},{16,24},{20,28},{24,16},{28,20},{1,9},{5... | collective-permute-start | bytes 12296 | tf_op jit(solution)/shard_map/ppermute | solution.py:519
  85.8 0.8 collective-permute-start.15
  86.6 1.2 collective-permute-start.16
  87.8 0.1 collective-permute-done.14
  87.9 1.5 %collective-permute-done.15 = f32[8,128]{1,0:T(8,128)S(1)} collective-permute-done((f32[8,128]{1,0:T(8,128)S(1)}, f32[8,128]{1,0:T(8,128)S(1)}, u32[]{:S(2)}, u32[]{:S(2)}) %collective-permute-start.15) | collective-permute-done | bytes 4128 | tf_op jit(solution)/shard_map/ppermute | solution.py:519
  89.4 1.7 %collective-permute-done.16 = f32[8,128]{1,0:T(8,128)S(1)} collective-permute-done((f32[8,128]{1,0:T(8,128)S(1)}, f32[8,128]{1,0:T(8,128)S(1)}, u32[]{:S(2)}, u32[]{:S(2)}) %collective-permute-start.16) | collective-permute-done | bytes 4128 | tf_op jit(solution)/shard_map/ppermute | solution.py:519
  91.1 2.7 %next.10 = s16[128,4480]{1,0:T(8,128)(2,1)S(1)} custom-call(f32[1,128,4352]{2,1,0:T(8,128)S(1)} %partials.2.refs_0_, f32[3,128,4352]{2,1,0:T(8,128)S(1)} %partials.3.refs_0_.refs_2_.refs_1_, s16[128,4480]{1,0:T(8,128)(2,1)S(1)} %collective-permute-done.17.refs_2_.refs_3_, f32[8,128]{1,0:T(8,128)S(1)} %add_add_fusion.1.refs_3_), custom_call_target="tpu_custom_call" | custom-call | flops 300000000 | bytes 1000000 | tf_op jit(solution)/shard_map/next/pallas_call | solution.py:41
  93.8 3.1 %collective-permute-start.18 = (f32[8,128]{1,0:T(8,128)S(1)}, f32[8,128]{1,0:T(8,128)S(1)}, u32[]{:S(2)}, u32[]{:S(2)}) collective-permute-start(f32[8,128]{1,0:T(8,128)S(1)} %add_add_fusion.1.refs_3_), channel_id=1, source_target_pairs={{0,1},{1,0},{2,3},{3,2},{4,5},{5,4},{6,7},{7,6},{8,9},{9,8},{10,11... | collective-permute-start | bytes 12296 | tf_op jit(solution)/shard_map/ppermute | solution.py:519
  96.9 0.2 collective-permute-start.19
  97.0 2.3 %collective-permute-start.20 = (f32[8,128]{1,0:T(8,128)S(1)}, f32[8,128]{1,0:T(8,128)S(1)}, u32[]{:S(2)}, u32[]{:S(2)}) collective-permute-start(f32[8,128]{1,0:T(8,128)S(1)} %add_add_fusion.1.refs_3_), channel_id=1, source_target_pairs={{0,3},{1,2},{2,1},{3,0},{4,7},{5,6},{6,5},{7,4},{8,11},{9,10},{10,... | collective-permute-start | bytes 12296 | tf_op jit(solution)/shard_map/ppermute | solution.py:519
  99.3 3.0 %collective-permute-start.22 = (s16[128,4480]{1,0:T(8,128)(2,1)S(1)}, s16[128,4480]{1,0:T(8,128)(2,1)S(1)}, u32[]{:S(2)}, u32[]{:S(2)}) collective-permute-start(s16[128,4480]{1,0:T(8,128)(2,1)S(1)} %next.10), channel_id=1, source_target_pairs={{0,1},{1,2},{2,3},{5,4},{6,5},{7,6},{8,9},{9,10},{10,11},{13,12},{... | collective-permute-start | bytes 3440648 | tf_op jit(solution)/shard_map/ppermute | solution.py:608
  102.3 0.2 collective-permute-done.20
  102.6 0.1 next.11.refs_5_
  102.7 1.3 %collective-permute-start.23 = (s16[128,4480]{1,0:T(8,128)(2,1)S(1)}, s16[128,4480]{1,0:T(8,128)(2,1)S(1)}, u32[]{:S(2)}, u32[]{:S(2)}) collective-permute-start(s16[128,4480]{1,0:T(8,128)(2,1)S(1)} %next.11.refs_5_), channel_id=1, source_target_pairs={{1,0},{2,1},{3,2},{4,5},{5,6},{6,7},{9,8},{10,9},{11,10},{12,13},{... | collective-permute-start | bytes 3440648 | tf_op jit(solution)/shard_map/ppermute | solution.py:608
  104.0 17.0 %weights.1 = (f32[8,128]{1,0:T(8,128)S(1)}, f32[3328,2048]{1,0:T(8,128)}, f32[1024,2048]{1,0:T(8,128)}) custom-call(f32[2,2]{1,0:T(2,128)S(1)} %pad_maximum_fusion.refs_3_.refs_0_, bf16[4,2,64,2048]{3,2,1,0:T(8,128)(2,1)S(1)} %arrange.1.m_ref.refs_0_.refs_1_, bf16[2,256,4352]{2,1,0:T(8,128)(2,1)S(1)} %get-tuple-element.38.refs_2_, ...), custom_call_target="tpu_custom_call" | custom-call | flops 300000000 | bytes 1000000 | tf_op jit(solution)/shard_map/weights/pallas_call | solution.py:41
  121.0 4.3 %collective-permute-done.22.refs_0_.refs_1_ = s16[128,4480]{1,0:T(8,128)(2,1)S(1)} collective-permute-done((s16[128,4480]{1,0:T(8,128)(2,1)S(1)}, s16[128,4480]{1,0:T(8,128)(2,1)S(1)}, u32[]{:S(2)}, u32[]{:S(2)}) %collective-permute-start.22) | collective-permute-done | bytes 1146912 | tf_op jit(solution)/shard_map/ppermute | solution.py:608
  125.3 1.1 collective-permute-done.23.refs_2_
  126.5 2.2 %finish.1 = (bf16[2,64,3328]{2,1,0:T(8,128)(2,1)}, bf16[2,64,1024]{2,1,0:T(8,128)(2,1)}) custom-call(f32[3,128,4352]{2,1,0:T(8,128)S(1)} %partials.3.refs_0_.refs_2_.refs_1_, s16[128,4480]{1,0:T(8,128)(2,1)S(1)} %collective-permute-done.22.refs_0_.refs_1_, s16[128,4480]{1,0:T(8,128)(2,1)S(1)} %collective-permute-done.23.refs_2_, f32[8,128]{1,0:T(8,128)S(1)} %wait.1.refs_3_), custom_call_target="tpu_custom_call" | custom-call | flops 300000000 | bytes 1000000 | tf_op jit(solution)/shard_map/finish/pallas_call | solution.py:41
  (52 shorter events, 0.3 us)
Async XLA Ops:
  0.6 11.9 %collective-permute-start.1 = (bf16[2,32,2048]{2,1,0:T(8,128)(2,1)}, bf16[2,32,2048]{2,1,0:T(8,128)(2,1)S(1)}, u32[]{:S(2)}, u32[]{:S(2)}) collective-permute-start(bf16[2,32,2048]{2,1,0:T(8,128)(2,1)} %refs_0_.1), channel_id=1, source_target_pairs={{0,8},{4,12},{8,0},{12,4},{16,24},{20,28},{24,16},{28,20},{1,9},{5... | collective-permute-start | bytes 786440 | tf_op jit(solution)/shard_map/ppermute | solution.py:198
  3.6 13.6 %collective-permute-start.3 = (bf16[2,32,2048]{2,1,0:T(8,128)(2,1)}, bf16[2,32,2048]{2,1,0:T(8,128)(2,1)S(1)}, u32[]{:S(2)}, u32[]{:S(2)}) collective-permute-start(bf16[2,32,2048]{2,1,0:T(8,128)(2,1)} %refs_0_.1), channel_id=1, source_target_pairs={{0,16},{4,20},{8,24},{12,28},{16,0},{20,4},{24,8},{28,12},{1,17},{... | collective-permute-start | bytes 786440 | tf_op jit(solution)/shard_map/ppermute | solution.py:198
  5.2 12.1 %collective-permute-start.5 = (bf16[2,32,2048]{2,1,0:T(8,128)(2,1)}, bf16[2,32,2048]{2,1,0:T(8,128)(2,1)S(1)}, u32[]{:S(2)}, u32[]{:S(2)}) collective-permute-start(bf16[2,32,2048]{2,1,0:T(8,128)(2,1)} %refs_0_.1), channel_id=1, source_target_pairs={{0,24},{4,28},{8,16},{12,20},{16,8},{20,12},{24,0},{28,4},{1,25},{... | collective-permute-start | bytes 786440 | tf_op jit(solution)/shard_map/ppermute | solution.py:198
  5.2 1.2 copy-start.3
  6.3 0.9 copy-start.7
  7.3 5.1 %copy-start.9 = (bf16[2,32,2048]{2,1,0:T(8,128)(2,1)S(1)}, bf16[2,32,2048]{2,1,0:T(8,128)(2,1)}, u32[]{:S(2)}) copy-start(bf16[2,32,2048]{2,1,0:T(8,128)(2,1)} %refs_0_.1) | copy-start | bytes 786436
  7.3 11.9 %copy-start.10 = (s32[2,2]{1,0:T(2,128)S(1)}, s32[2,2]{1,0:T(2,128)}, u32[]{:S(2)}) copy-start(s32[2,2]{1,0:T(2,128)} %spans.1) | copy-start | bytes 52
  7.3 12.9 %slice-start = ((s8[13631488]{0:T(1024)(128)(4,1)}), s8[4194304]{0:T(1024)(128)(4,1)S(1)}, s32[]{:S(2)}) async-start(s8[13631488]{0:T(1024)(128)(4,1)} %bitcast), calls=%async_computation | async-start | bytes 8388608
  7.3 12.9 %slice-start.1 = ((s8[13631488]{0:T(1024)(128)(4,1)}), s8[4194304]{0:T(1024)(128)(4,1)S(1)}, s32[]{:S(2)}) async-start(s8[13631488]{0:T(1024)(128)(4,1)} %bitcast), calls=%async_computation.1 | async-start | bytes 8388608
  8.1 12.1 %slice-start.2 = ((s8[13631488]{0:T(1024)(128)(4,1)}), s8[4194304]{0:T(1024)(128)(4,1)S(1)}, s32[]{:S(2)}) async-start(s8[13631488]{0:T(1024)(128)(4,1)} %bitcast), calls=%async_computation.2 | async-start | bytes 8388608
  8.1 12.1 %slice-start.3 = ((s8[13631488]{0:T(1024)(128)(4,1)}), s8[1048576]{0:T(1024)(128)(4,1)S(1)}, s32[]{:S(2)}) async-start(s8[13631488]{0:T(1024)(128)(4,1)} %bitcast), calls=%async_computation.3 | async-start | bytes 2097152
  8.1 22.0 %collective-permute-start.7 = (s16[128,4480]{1,0:T(8,128)(2,1)S(1)}, s16[128,4480]{1,0:T(8,128)(2,1)S(1)}, u32[]{:S(2)}, u32[]{:S(2)}) collective-permute-start(s16[128,4480]{1,0:T(8,128)(2,1)S(1)} %code.1), channel_id=1, source_target_pairs={{0,1},{1,2},{2,3},{5,4},{6,5},{7,6},{8,9},{9,10},{10,11},{13,12},{... | collective-permute-start | bytes 3440648 | tf_op jit(solution)/shard_map/ppermute | solution.py:608
  12.4 5.3 %collective-permute-start = (bf16[2,32,2048]{2,1,0:T(8,128)(2,1)S(1)}, bf16[2,32,2048]{2,1,0:T(8,128)(2,1)S(1)}, u32[]{:S(2)}, u32[]{:S(2)}) collective-permute-start(bf16[2,32,2048]{2,1,0:T(8,128)(2,1)S(1)} %copy-done.9), channel_id=1, source_target_pairs={{0,4},{4,0},{8,12},{12,8},{16,20},{20,16},{24,28},{28,24},{1,5},{5... | collective-permute-start | bytes 786440 | tf_op jit(solution)/shard_map/ppermute | solution.py:204
  12.5 6.5 %collective-permute-start.2 = (bf16[2,32,2048]{2,1,0:T(8,128)(2,1)S(1)}, bf16[2,32,2048]{2,1,0:T(8,128)(2,1)S(1)}, u32[]{:S(2)}, u32[]{:S(2)}) collective-permute-start(bf16[2,32,2048]{2,1,0:T(8,128)(2,1)S(1)} %collective-permute-done.1.refs_2_), channel_id=1, source_target_pairs={{0,4},{4,0},{8,12},{12,8},{16,20},{20,16},{24,28},{28,24},{1,5},{5... | collective-permute-start | bytes 786440 | tf_op jit(solution)/shard_map/ppermute | solution.py:204
  17.2 1.8 %collective-permute-start.4 = (bf16[2,32,2048]{2,1,0:T(8,128)(2,1)S(1)}, bf16[2,32,2048]{2,1,0:T(8,128)(2,1)S(1)}, u32[]{:S(2)}, u32[]{:S(2)}) collective-permute-start(bf16[2,32,2048]{2,1,0:T(8,128)(2,1)S(1)} %collective-permute-done.3.refs_4_), channel_id=1, source_target_pairs={{0,4},{4,0},{8,12},{12,8},{16,20},{20,16},{24,28},{28,24},{1,5},{5... | collective-permute-start | bytes 786440 | tf_op jit(solution)/shard_map/ppermute | solution.py:204
  17.2 1.9 %collective-permute-start.6 = (bf16[2,32,2048]{2,1,0:T(8,128)(2,1)S(1)}, bf16[2,32,2048]{2,1,0:T(8,128)(2,1)S(1)}, u32[]{:S(2)}, u32[]{:S(2)}) collective-permute-start(bf16[2,32,2048]{2,1,0:T(8,128)(2,1)S(1)} %collective-permute-done.5.refs_6_), channel_id=1, source_target_pairs={{0,4},{4,0},{8,12},{12,8},{16,20},{20,16},{24,28},{28,24},{1,5},{5... | collective-permute-start | bytes 786440 | tf_op jit(solution)/shard_map/ppermute | solution.py:204
  17.7 19.3 %collective-permute-start.9 = (s16[128,4480]{1,0:T(8,128)(2,1)S(1)}, s16[128,4480]{1,0:T(8,128)(2,1)S(1)}, u32[]{:S(2)}, u32[]{:S(2)}) collective-permute-start(s16[128,4480]{1,0:T(8,128)(2,1)S(1)} %code.1), channel_id=1, source_target_pairs={{1,0},{2,1},{3,2},{4,5},{5,6},{6,7},{9,8},{10,9},{11,10},{12,13},{... | collective-permute-start | bytes 3440648 | tf_op jit(solution)/shard_map/ppermute | solution.py:608
  19.1 2.2 %copy-start = (bf16[1024,2048]{1,0:T(8,128)(2,1)S(1)}, bf16[1024,2048]{1,0:T(8,128)(2,1)}, u32[]{:S(2)}) copy-start(bf16[1024,2048]{1,0:T(8,128)(2,1)} %refs_2_.1) | copy-start | bytes 12582916
  32.8 22.9 %collective-permute-start.10 = (s16[128,4480]{1,0:T(8,128)(2,1)S(1)}, s16[128,4480]{1,0:T(8,128)(2,1)S(1)}, u32[]{:S(2)}, u32[]{:S(2)}) collective-permute-start(s16[128,4480]{1,0:T(8,128)(2,1)S(1)} %next.6.refs_1_), channel_id=1, source_target_pairs={{0,1},{1,2},{2,3},{5,4},{6,5},{7,6},{8,9},{9,10},{10,11},{13,12},{... | collective-permute-start | bytes 3440648 | tf_op jit(solution)/shard_map/ppermute | solution.py:608
  36.3 0.8 copy-start.5
  37.1 35.4 %collective-permute-start.12 = (s16[128,4480]{1,0:T(8,128)(2,1)S(1)}, s16[128,4480]{1,0:T(8,128)(2,1)S(1)}, u32[]{:S(2)}, u32[]{:S(2)}) collective-permute-start(s16[128,4480]{1,0:T(8,128)(2,1)S(1)} %next.7.refs_3_), channel_id=1, source_target_pairs={{1,0},{2,1},{3,2},{4,5},{5,6},{6,7},{9,8},{10,9},{11,10},{12,13},{... | collective-permute-start | bytes 3440648 | tf_op jit(solution)/shard_map/ppermute | solution.py:608
  49.4 13.5 %collective-permute-start.8 = (f32[1,256,256]{2,1,0:T(8,128)S(1)}, f32[1,256,256]{2,1,0:T(8,128)S(1)}, u32[]{:S(2)}, u32[]{:S(2)}) collective-permute-start(f32[1,256,256]{2,1,0:T(8,128)S(1)} %get-tuple-element.28), channel_id=1, source_target_pairs={{0,1},{3,2},{4,5},{7,6},{8,9},{11,10},{12,13},{15,14},{16,17},{19,... | collective-permute-start | bytes 786440 | tf_op jit(solution)/shard_map/ppermute | solution.py:646
  58.3 16.5 %copy-start.4 = (bf16[2,64,3328]{2,1,0:T(8,128)(2,1)S(1)}, bf16[2,64,3328]{2,1,0:T(8,128)(2,1)}, u32[]{:S(2)}) copy-start(bf16[2,64,3328]{2,1,0:T(8,128)(2,1)} %refs_3_.1) | copy-start | bytes 2555908
  58.3 16.5 %copy-start.6 = (f32[2,256,256]{2,1,0:T(8,128)S(1)}, f32[2,256,256]{2,1,0:T(8,128)}, u32[]{:S(2)}) copy-start(f32[2,256,256]{2,1,0:T(8,128)} %copy-done.5) | copy-start | bytes 1572868
  58.3 16.5 %copy-start.8 = (bf16[2,64,1024]{2,1,0:T(8,128)(2,1)S(1)}, bf16[2,64,1024]{2,1,0:T(8,128)(2,1)}, u32[]{:S(2)}) copy-start(bf16[2,64,1024]{2,1,0:T(8,128)(2,1)} %refs_4_.1) | copy-start | bytes 786436
  58.3 32.8 %collective-permute-start.17 = (s16[128,4480]{1,0:T(8,128)(2,1)S(1)}, s16[128,4480]{1,0:T(8,128)(2,1)S(1)}, u32[]{:S(2)}, u32[]{:S(2)}) collective-permute-start(s16[128,4480]{1,0:T(8,128)(2,1)S(1)} %next.8.refs_2_), channel_id=1, source_target_pairs={{0,1},{1,2},{2,3},{5,4},{6,5},{7,6},{8,9},{9,10},{10,11},{13,12},{... | collective-permute-start | bytes 3440648 | tf_op jit(solution)/shard_map/ppermute | solution.py:608
  62.9 11.8 %collective-permute-start.11 = (f32[1,256,256]{2,1,0:T(8,128)S(1)}, f32[1,256,256]{2,1,0:T(8,128)S(1)}, u32[]{:S(2)}, u32[]{:S(2)}) collective-permute-start(f32[1,256,256]{2,1,0:T(8,128)S(1)} %collective-permute-done.8.refs_1_), channel_id=1, source_target_pairs={{0,4},{4,0},{8,12},{12,8},{16,20},{20,16},{24,28},{28,24},{1,5},{5... | collective-permute-start | bytes 786440 | tf_op jit(solution)/shard_map/ppermute | solution.py:652
  72.5 1.0 copy-start.1
  73.5 29.1 %collective-permute-start.21 = (s16[128,4480]{1,0:T(8,128)(2,1)S(1)}, s16[128,4480]{1,0:T(8,128)(2,1)S(1)}, u32[]{:S(2)}, u32[]{:S(2)}) collective-permute-start(s16[128,4480]{1,0:T(8,128)(2,1)S(1)} %next.9.refs_9_), channel_id=1, source_target_pairs={{1,0},{2,1},{3,2},{4,5},{5,6},{6,7},{9,8},{10,9},{11,10},{12,13},{... | collective-permute-start | bytes 3440648 | tf_op jit(solution)/shard_map/ppermute | solution.py:608
  74.8 1.3 copy-start.2
  78.8 5.5 %collective-permute-start.13 = (f32[8,128]{1,0:T(8,128)S(1)}, f32[8,128]{1,0:T(8,128)S(1)}, u32[]{:S(2)}, u32[]{:S(2)}) collective-permute-start(f32[8,128]{1,0:T(8,128)S(1)} %get-tuple-element.30), channel_id=1, source_target_pairs={{0,4},{4,0},{8,12},{12,8},{16,20},{20,16},{24,28},{28,24},{1,5},{5... | collective-permute-start | bytes 12296 | tf_op jit(solution)/shard_map/ppermute | solution.py:519
  84.3 3.6 %collective-permute-start.14 = (f32[8,128]{1,0:T(8,128)S(1)}, f32[8,128]{1,0:T(8,128)S(1)}, u32[]{:S(2)}, u32[]{:S(2)}) collective-permute-start(f32[8,128]{1,0:T(8,128)S(1)} %add.26), channel_id=1, source_target_pairs={{0,8},{4,12},{8,0},{12,4},{16,24},{20,28},{24,16},{28,20},{1,9},{5... | collective-permute-start | bytes 12296 | tf_op jit(solution)/shard_map/ppermute | solution.py:519
  85.8 3.6 %collective-permute-start.15 = (f32[8,128]{1,0:T(8,128)S(1)}, f32[8,128]{1,0:T(8,128)S(1)}, u32[]{:S(2)}, u32[]{:S(2)}) collective-permute-start(f32[8,128]{1,0:T(8,128)S(1)} %add.26), channel_id=1, source_target_pairs={{0,16},{4,20},{8,24},{12,28},{16,0},{20,4},{24,8},{28,12},{1,17},{... | collective-permute-start | bytes 12296 | tf_op jit(solution)/shard_map/ppermute | solution.py:519
  86.6 4.5 %collective-permute-start.16 = (f32[8,128]{1,0:T(8,128)S(1)}, f32[8,128]{1,0:T(8,128)S(1)}, u32[]{:S(2)}, u32[]{:S(2)}) collective-permute-start(f32[8,128]{1,0:T(8,128)S(1)} %add.26), channel_id=1, source_target_pairs={{0,24},{4,28},{8,16},{12,20},{16,8},{20,12},{24,0},{28,4},{1,25},{... | collective-permute-start | bytes 12296 | tf_op jit(solution)/shard_map/ppermute | solution.py:519
  93.8 8.5 %collective-permute-start.18 = (f32[8,128]{1,0:T(8,128)S(1)}, f32[8,128]{1,0:T(8,128)S(1)}, u32[]{:S(2)}, u32[]{:S(2)}) collective-permute-start(f32[8,128]{1,0:T(8,128)S(1)} %add_add_fusion.1.refs_3_), channel_id=1, source_target_pairs={{0,1},{1,0},{2,3},{3,2},{4,5},{5,4},{6,7},{7,6},{8,9},{9,8},{10,11... | collective-permute-start | bytes 12296 | tf_op jit(solution)/shard_map/ppermute | solution.py:519
  96.9 5.5 %collective-permute-start.19 = (f32[8,128]{1,0:T(8,128)S(1)}, f32[8,128]{1,0:T(8,128)S(1)}, u32[]{:S(2)}, u32[]{:S(2)}) collective-permute-start(f32[8,128]{1,0:T(8,128)S(1)} %add_add_fusion.1.refs_3_), channel_id=1, source_target_pairs={{0,2},{1,3},{2,0},{3,1},{4,6},{5,7},{6,4},{7,5},{8,10},{9,11},{10,... | collective-permute-start | bytes 12296 | tf_op jit(solution)/shard_map/ppermute | solution.py:519
  97.0 5.5 %collective-permute-start.20 = (f32[8,128]{1,0:T(8,128)S(1)}, f32[8,128]{1,0:T(8,128)S(1)}, u32[]{:S(2)}, u32[]{:S(2)}) collective-permute-start(f32[8,128]{1,0:T(8,128)S(1)} %add_add_fusion.1.refs_3_), channel_id=1, source_target_pairs={{0,3},{1,2},{2,1},{3,0},{4,7},{5,6},{6,5},{7,4},{8,11},{9,10},{10,... | collective-permute-start | bytes 12296 | tf_op jit(solution)/shard_map/ppermute | solution.py:519
  99.3 26.0 %collective-permute-start.22 = (s16[128,4480]{1,0:T(8,128)(2,1)S(1)}, s16[128,4480]{1,0:T(8,128)(2,1)S(1)}, u32[]{:S(2)}, u32[]{:S(2)}) collective-permute-start(s16[128,4480]{1,0:T(8,128)(2,1)S(1)} %next.10), channel_id=1, source_target_pairs={{0,1},{1,2},{2,3},{5,4},{6,5},{7,6},{8,9},{9,10},{10,11},{13,12},{... | collective-permute-start | bytes 3440648 | tf_op jit(solution)/shard_map/ppermute | solution.py:608
  102.7 23.8 %collective-permute-start.23 = (s16[128,4480]{1,0:T(8,128)(2,1)S(1)}, s16[128,4480]{1,0:T(8,128)(2,1)S(1)}, u32[]{:S(2)}, u32[]{:S(2)}) collective-permute-start(s16[128,4480]{1,0:T(8,128)(2,1)S(1)} %next.11.refs_5_), channel_id=1, source_target_pairs={{1,0},{2,1},{3,2},{4,5},{5,6},{6,7},{9,8},{10,9},{11,10},{12,13},{... | collective-permute-start | bytes 3440648 | tf_op jit(solution)/shard_map/ppermute | solution.py:608
